TPU v7x, 128 devices: a whole 4x4x4 slice. The times are simulated.
128 devices in a mesh: cluster: 8 (over z, core), slab: 16 (over x, y).
Axes of the slice: x: 4, y: 4, z: 4, core: 2. Of those that a mesh axis runs over, the one named last changes fastest.
Arguments:
- queries: bfloat16 [4096, 8, 1024], P(('cluster', 'slab')), may hold values from -30 to 30
- corpus: bfloat16 [128, 1024, 1024], P(('cluster', 'slab')), may hold values from -8 to 8
- block_pairs: int32 [4096, 2], P(('cluster', 'slab')), may hold values from 0 to 127, as said below
- owner_table: int32 [128], replicated, may hold values from 0 to 127, as said below
Outputs:
- shifted: bfloat16 [4096, 8, 1024], P(('cluster', 'slab'))
- log_density: float32 [2, 32768], P(None, ('cluster', 'slab'))
Inputs may be any that keep to these rules, and one draw needn't show every extreme that they name: `owner_table`: a permutation: each cluster has its own corpus entry; entry e is held by device e of cluster+slab, so its slab index is e % 16 and its cluster index e // 16. `block_pairs`: the two clusters of a block differ; the 32 blocks of one device name no cluster more than 1 times, and some cluster exactly 1 times; of the 64 clusters named by one device's blocks, exactly 4 are held at each slab index; the blocks of all devices of one cluster index name the cluster of each device exactly 8 times.
All inputs are finite; a program needn't handle non-finite values.
Results may differ from a plain program's by a relative error of at most 0.0046.
Values may be sent and summed in bfloat16 or wider, within the bound.
No kernel may reach another device: no remote copies, remote signals or barrier semaphores. Data moves between devices by JAX's collectives and lax.ppermute only.
A program may use at most 64 MiB of HBM per device.

v0:
```python
import math

import jax
import jax.numpy as jnp
from jax import lax
from jax.sharding import PartitionSpec as P

REF_ROWS = 1024
STEPS = 2


INV_WIDTH = 1.0 / 16.0


def partials(query_rows, cluster_rows, half_norms):
    products = lax.dot_general(
        query_rows, cluster_rows, (((1,), (1,)), ((), ())), preferred_element_type=jnp.float32
    )
    scores = (products - half_norms[None, :]) * INV_WIDTH
    row_top = jnp.max(scores, axis=1)
    weights = jnp.exp(scores - row_top[:, None])
    totals = jnp.sum(weights, axis=1)
    summed = jnp.dot(weights.astype(jnp.bfloat16), cluster_rows, preferred_element_type=jnp.float32)
    shifted_part = (summed / totals[:, None]).astype(jnp.bfloat16)
    return (shifted_part, row_top + jnp.log(totals))


def combine_pairs(query_rows, first_part, second_part, first_log, second_log):
    both_top = jnp.maximum(first_log, second_log)
    first_share = jnp.exp(first_log - both_top)
    second_share = jnp.exp(second_log - both_top)
    pair_total = first_share + second_share
    mixed = (
        first_share[:, None] * first_part.astype(jnp.float32)
        + second_share[:, None] * second_part.astype(jnp.float32)
    ) / pair_total[:, None]
    squares = jnp.sum(jnp.square(query_rows.astype(jnp.float32)), axis=1)
    density = both_top + jnp.log(pair_total) - 0.5 * INV_WIDTH * squares - jnp.log(2.0 * REF_ROWS)
    return (mixed.astype(jnp.bfloat16), density)


def score_items(arrived, cluster_rows, half_norms):
    features = arrived.shape[3]
    flat_rows = arrived.reshape(-1, features)
    row_total = flat_rows.shape[0]
    group_rows = math.gcd(row_total, 512)
    grouped = flat_rows.reshape(row_total // group_rows, group_rows, features)
    shifted_parts, log_weights = lax.map(
        lambda chosen: partials(chosen, cluster_rows, half_norms), grouped
    )
    return (shifted_parts.reshape(arrived.shape), log_weights.reshape(arrived.shape[:3]))


def rank_within(labels):
    message_order = jnp.arange(labels.shape[0], dtype=jnp.int32)
    earlier = (labels[:, None] == labels[None, :]) & (
        message_order[None, :] < message_order[:, None]
    )
    return jnp.sum(earlier.astype(jnp.int32), axis=1)


def local(queries, corpus, block_pairs, owner_table):
    devices = lax.axis_size(("cluster", "slab"))
    block_count, block_rows, features = queries.shape
    message_total = 2 * block_count
    capacity = (message_total + devices - 1) // devices
    cluster_rows = corpus[0]
    half_norms = 0.5 * jnp.sum(jnp.square(cluster_rows.astype(jnp.float32)), axis=1)
    matches = (
        block_pairs[:, :, None] == jnp.arange(owner_table.shape[0], dtype=jnp.int32)[None, None, :]
    )
    owners = jnp.sum(jnp.where(matches, owner_table[None, None, :], 0), axis=2).reshape(-1)
    slot_index = owners * capacity + rank_within(owners)
    current = queries
    densities = []
    for iteration in range(STEPS):
        messages = jnp.repeat(current, 2, axis=0)
        outgoing = jnp.zeros((devices * capacity, block_rows, features), jnp.bfloat16)
        outgoing = outgoing.at[slot_index].set(messages)
        outgoing = outgoing.reshape(devices, capacity, block_rows, features)
        shifted_parts, log_weights = score_items(
            lax.all_to_all(outgoing, ("cluster", "slab"), split_axis=0, concat_axis=0, tiled=True),
            cluster_rows,
            half_norms,
        )
        returned = lax.all_to_all(
            shifted_parts, ("cluster", "slab"), split_axis=0, concat_axis=0, tiled=True
        )
        returned_logs = lax.all_to_all(
            log_weights, ("cluster", "slab"), split_axis=0, concat_axis=0, tiled=True
        )
        picked = returned.reshape(devices * capacity, block_rows, features)[slot_index].reshape(
            block_count, 2, block_rows, features
        )
        picked_logs = returned_logs.reshape(devices * capacity, block_rows)[slot_index].reshape(
            block_count, 2, block_rows
        )
        query_rows = current.reshape(-1, features)
        first_part = picked[:, 0].reshape(-1, features)
        second_part = picked[:, 1].reshape(-1, features)
        mixed, density = combine_pairs(
            query_rows,
            first_part,
            second_part,
            picked_logs[:, 0].reshape(-1),
            picked_logs[:, 1].reshape(-1),
        )
        current = mixed.reshape(block_count, block_rows, features)
        densities.append(density)
    return (current, jnp.stack(densities))


def solution(mesh):
    return jax.shard_map(
        local,
        mesh=mesh,
        in_specs=(
            P(("cluster", "slab"), None, None),
            P(("cluster", "slab"), None, None),
            P(("cluster", "slab"), None),
            P(),
        ),
        out_specs=(P(("cluster", "slab"), None, None), P(None, ("cluster", "slab"))),
        check_vma=False,
    )
```

profile of v0, /device:TPU:0, one launch (start us, length us, event | category | flops | bytes accessed | tf_op | source)
XLA Modules:
  0.0 223.3 jit_solution(1689235409236680988)
XLA Ops:
  0.6 0.9 select_reduce_fusion
  1.5 0.1 copy.24
  1.6 0.1 eq.31
  1.7 0.1 reshape.400
  1.8 0.2 convert_reduce_fusion
  2.0 1.2 broadcast_in_dim.31
  3.2 1.6 broadcast.105.clone
  4.7 8.1 %scatter_fusion = bf16[128,8,1024]{2,1,0:T(8,128)(2,1)} fusion(bf16[128,8,1024]{2,1,0:T(8,128)(2,1)} %broadcast.105.clone, s32[64]{0:T(128)S(1)} %fusion.46, bf16[64,8,1024]{2,1,0:T(8,128)(2,1)S(1)} %bitcast.128), kind=kCustom, calls=%fused_computation.4 | custom fusion | bytes 3145984 | tf_op jit(solution)/shard_map/scatter | solution.py:79
  12.9 11.7 %all-to-all-start = ((bf16[128,1,8,1024]{3,2,1,0:T(8,128)(2,1)}), bf16[128,1,8,1024]{3,2,1,0:T(8,128)(2,1)}, u32[]{:S(2)}, u32[]{:S(2)}) async-start(bf16[128,1,8,1024]{3,2,1,0:T(8,128)(2,1)} %bitcast.9), calls=%async_computation | async-start | bytes 4194304 | tf_op jit(solution)/shard_map/all_to_all | solution.py:82
  24.6 0.5 multiply_reduce_fusion
  25.1 28.8 %all-to-all-done = bf16[128,1,8,1024]{3,2,1,0:T(8,128)(2,1)} async-done(((bf16[128,1,8,1024]{3,2,1,0:T(8,128)(2,1)}), bf16[128,1,8,1024]{3,2,1,0:T(8,128)(2,1)}, u32[]{:S(2)}, u32[]{:S(2)}) %all-to-all-start) | async-done | bytes 2097184 | tf_op jit(solution)/shard_map/all_to_all | solution.py:82
  53.9 1.6 broadcast.103.clone
  55.4 11.1 %while.24 = (s32[]{:T(128)}, bf16[2,512,1024]{2,1,0:T(8,128)(2,1)}, f32[2,512]{1,0:T(2,128)S(1)}, bf16[2,512,1024]{2,1,0:T(8,128)(2,1)}, bf16[1024,1024]{1,0:T(8...) while((s32[]{:T(128)}, bf16[2,512,1024]{2,1,0:T(8,128)(2,1)}, f32[2,512]{1,0:T(2,128)S(1)}, ...), condition=%wide.region_7.8_spmd, body=%wide.region_4.7_spmd.sunk | while | flops 2154298880 | bytes 12615785 | solution.py:48
  55.4 2.6 %fusion.74 = (f32[512]{0:T(512)S(1)}, f32[512,1024]{1,0:T(8,128)S(1)}) fusion(f32[1024]{0:T(1024)S(1)} %get-tuple-element.215, bf16[1024,1024]{1,0:T(8,128)(2,1)S(1)} %get-tuple-element.214, bf16[2,512,1024]{2,1,0:T(8,128)(2,1)} %get-tuple-element.213, s32[]{:T(128)S(6)} %copy.47), kind=kOutput, calls=%fused_computation.9.clone.1 | convolution fusion | flops 1075314176 | bytes 5249028 | tf_op jit(solution)/shard_map/while/body/eval_jaxpr/dot_general | solution.py:16
  58.0 0.6 fusion.75
  58.6 2.3 %fusion.76 = bf16[2,512,1024]{2,1,0:T(8,128)(2,1)} fusion(bf16[2,512,1024]{2,1,0:T(8,128)(2,1)} %get-tuple-element.203, s32[]{:T(128)S(6)} %copy.47, bf16[1024,1024]{1,0:T(8,128)(2,1)S(1)} %get-tuple-element.214, f32[512,1024]{1,0:T(8,128)S(1)} %get-tuple-element.184, f32[512]{0:T(512)S(1)} %fusion.75, f32[512]{0:T(512)S(1)} %get-tuple-element.185, ...), kind=kOutput, calls=%fused_computation.13.clone.1 | convolution fusion | flops 1076887552 | bytes 5251076 | tf_op jit(solution)/shard_map/while/body/eval_jaxpr/dot_general | solution.py:23
  61.0 2.6 %fusion.74 = (f32[512]{0:T(512)S(1)}, f32[512,1024]{1,0:T(8,128)S(1)}) fusion(f32[1024]{0:T(1024)S(1)} %get-tuple-element.215, bf16[1024,1024]{1,0:T(8,128)(2,1)S(1)} %get-tuple-element.214, bf16[2,512,1024]{2,1,0:T(8,128)(2,1)} %get-tuple-element.213, s32[]{:T(128)S(6)} %copy.47), kind=kOutput, calls=%fused_computation.9.clone.1 | convolution fusion | flops 1075314176 | bytes 5249028 | tf_op jit(solution)/shard_map/while/body/eval_jaxpr/dot_general | solution.py:16
  63.6 0.6 fusion.75
  64.2 2.3 %fusion.76 = bf16[2,512,1024]{2,1,0:T(8,128)(2,1)} fusion(bf16[2,512,1024]{2,1,0:T(8,128)(2,1)} %get-tuple-element.203, s32[]{:T(128)S(6)} %copy.47, bf16[1024,1024]{1,0:T(8,128)(2,1)S(1)} %get-tuple-element.214, f32[512,1024]{1,0:T(8,128)S(1)} %get-tuple-element.184, f32[512]{0:T(512)S(1)} %fusion.75, f32[512]{0:T(512)S(1)} %get-tuple-element.185, ...), kind=kOutput, calls=%fused_computation.13.clone.1 | convolution fusion | flops 1076887552 | bytes 5251076 | tf_op jit(solution)/shard_map/while/body/eval_jaxpr/dot_general | solution.py:23
  66.6 13.8 %all_to_all.30 = f32[128,1,8]{2,1,0:T(1,128)S(1)} all-to-all(f32[128,1,8]{2,1,0:T(1,128)S(1)} %bitcast.133), channel_id=1, replica_groups=mesh['cluster'=8,'slab'=16] {'cluster','slab'}, dimensions={0} | all-to-all | bytes 8192 | tf_op jit(solution)/shard_map/all_to_all | solution.py:89
  80.5 4.6 %all-to-all-start.2 = ((bf16[128,1,8,1024]{3,2,1,0:T(8,128)(2,1)}), bf16[128,1,8,1024]{3,2,1,0:T(8,128)(2,1)S(1)}, u32[]{:S(2)}, u32[]{:S(2)}) async-start(bf16[128,1,8,1024]{3,2,1,0:T(8,128)(2,1)} %bitcast.17), calls=%async_computation.2 | async-start | bytes 4194304 | tf_op jit(solution)/shard_map/all_to_all | solution.py:86
  85.1 0.6 gather_fusion
  85.8 29.0 %all-to-all-done.2 = bf16[128,1,8,1024]{3,2,1,0:T(8,128)(2,1)S(1)} async-done(((bf16[128,1,8,1024]{3,2,1,0:T(8,128)(2,1)}), bf16[128,1,8,1024]{3,2,1,0:T(8,128)(2,1)S(1)}, u32[]{:S(2)}, u32[]{:S(2)}) %all-to-all-start.2) | async-done | bytes 2097184 | tf_op jit(solution)/shard_map/all_to_all | solution.py:86
  114.8 0.6 gather_fusion.1
  115.4 0.3 fusion.31
  115.7 0.1 broadcast_in_dim.32
  115.9 1.6 broadcast.105
  117.4 8.1 %scatter_fusion.1 = bf16[128,8,1024]{2,1,0:T(8,128)(2,1)} fusion(bf16[128,8,1024]{2,1,0:T(8,128)(2,1)} %broadcast.105, s32[64]{0:T(128)S(1)} %fusion.46, bf16[64,8,1024]{2,1,0:T(8,128)(2,1)S(1)} %bitcast.127), kind=kCustom, calls=%fused_computation.5 | custom fusion | bytes 3145984 | tf_op jit(solution)/shard_map/scatter | solution.py:79
  125.6 5.8 %all-to-all-start.3 = ((bf16[128,1,8,1024]{3,2,1,0:T(8,128)(2,1)}), bf16[128,1,8,1024]{3,2,1,0:T(8,128)(2,1)}, u32[]{:S(2)}, u32[]{:S(2)}) async-start(bf16[128,1,8,1024]{3,2,1,0:T(8,128)(2,1)} %bitcast.24), calls=%async_computation.3 | async-start | bytes 4194304 | tf_op jit(solution)/shard_map/all_to_all | solution.py:82
  131.4 29.3 %all-to-all-done.3 = bf16[128,1,8,1024]{3,2,1,0:T(8,128)(2,1)} async-done(((bf16[128,1,8,1024]{3,2,1,0:T(8,128)(2,1)}), bf16[128,1,8,1024]{3,2,1,0:T(8,128)(2,1)}, u32[]{:S(2)}, u32[]{:S(2)}) %all-to-all-start.3) | async-done | bytes 2097184 | tf_op jit(solution)/shard_map/all_to_all | solution.py:82
  160.6 1.6 broadcast.103
  162.2 11.1 %while.25 = (s32[]{:T(128)}, bf16[2,512,1024]{2,1,0:T(8,128)(2,1)}, f32[2,512]{1,0:T(2,128)S(1)}, bf16[2,512,1024]{2,1,0:T(8,128)(2,1)}, bf16[1024,1024]{1,0:T(8...) while((s32[]{:T(128)}, bf16[2,512,1024]{2,1,0:T(8,128)(2,1)}, f32[2,512]{1,0:T(2,128)S(1)}, ...), condition=%wide.region_12.13_spmd, body=%wide.region_9.12_spmd.sunk | while | flops 2154298880 | bytes 12615785 | solution.py:48
  162.2 2.6 %fusion.80 = (f32[512]{0:T(512)S(1)}, f32[512,1024]{1,0:T(8,128)S(1)}) fusion(f32[1024]{0:T(1024)S(1)} %get-tuple-element.239, bf16[1024,1024]{1,0:T(8,128)(2,1)S(1)} %get-tuple-element.238, bf16[2,512,1024]{2,1,0:T(8,128)(2,1)} %get-tuple-element.237, s32[]{:T(128)S(6)} %copy.57), kind=kOutput, calls=%fused_computation.26.clone.1 | convolution fusion | flops 1075314176 | bytes 5249028 | tf_op jit(solution)/shard_map/while/body/eval_jaxpr/dot_general | solution.py:16
  164.8 0.6 fusion.81
  165.4 2.3 %fusion.82 = bf16[2,512,1024]{2,1,0:T(8,128)(2,1)} fusion(bf16[2,512,1024]{2,1,0:T(8,128)(2,1)} %get-tuple-element.227, s32[]{:T(128)S(6)} %copy.57, bf16[1024,1024]{1,0:T(8,128)(2,1)S(1)} %get-tuple-element.238, f32[512,1024]{1,0:T(8,128)S(1)} %get-tuple-element.192, f32[512]{0:T(512)S(1)} %fusion.81, f32[512]{0:T(512)S(1)} %get-tuple-element.193, ...), kind=kOutput, calls=%fused_computation.30.clone.1 | convolution fusion | flops 1076887552 | bytes 5251076 | tf_op jit(solution)/shard_map/while/body/eval_jaxpr/dot_general | solution.py:23
  167.8 2.6 %fusion.80 = (f32[512]{0:T(512)S(1)}, f32[512,1024]{1,0:T(8,128)S(1)}) fusion(f32[1024]{0:T(1024)S(1)} %get-tuple-element.239, bf16[1024,1024]{1,0:T(8,128)(2,1)S(1)} %get-tuple-element.238, bf16[2,512,1024]{2,1,0:T(8,128)(2,1)} %get-tuple-element.237, s32[]{:T(128)S(6)} %copy.57), kind=kOutput, calls=%fused_computation.26.clone.1 | convolution fusion | flops 1075314176 | bytes 5249028 | tf_op jit(solution)/shard_map/while/body/eval_jaxpr/dot_general | solution.py:16
  170.4 0.6 fusion.81
  170.9 2.3 %fusion.82 = bf16[2,512,1024]{2,1,0:T(8,128)(2,1)} fusion(bf16[2,512,1024]{2,1,0:T(8,128)(2,1)} %get-tuple-element.227, s32[]{:T(128)S(6)} %copy.57, bf16[1024,1024]{1,0:T(8,128)(2,1)S(1)} %get-tuple-element.238, f32[512,1024]{1,0:T(8,128)S(1)} %get-tuple-element.192, f32[512]{0:T(512)S(1)} %fusion.81, f32[512]{0:T(512)S(1)} %get-tuple-element.193, ...), kind=kOutput, calls=%fused_computation.30.clone.1 | convolution fusion | flops 1076887552 | bytes 5251076 | tf_op jit(solution)/shard_map/while/body/eval_jaxpr/dot_general | solution.py:23
  173.4 13.8 %all_to_all.31 = f32[128,1,8]{2,1,0:T(1,128)S(1)} all-to-all(f32[128,1,8]{2,1,0:T(1,128)S(1)} %bitcast.134), channel_id=1, replica_groups=mesh['cluster'=8,'slab'=16] {'cluster','slab'}, dimensions={0} | all-to-all | bytes 8192 | tf_op jit(solution)/shard_map/all_to_all | solution.py:89
  187.2 4.6 %all-to-all-start.5 = ((bf16[128,1,8,1024]{3,2,1,0:T(8,128)(2,1)}), bf16[128,1,8,1024]{3,2,1,0:T(8,128)(2,1)S(1)}, u32[]{:S(2)}, u32[]{:S(2)}) async-start(bf16[128,1,8,1024]{3,2,1,0:T(8,128)(2,1)} %bitcast.31), calls=%async_computation.5 | async-start | bytes 4194304 | tf_op jit(solution)/shard_map/all_to_all | solution.py:86
  191.9 1.2 multiply_reduce_fusion.2
  193.4 0.4 multiply_reduce_fusion.1
  193.8 0.1 mul.101
  193.9 0.6 gather_fusion.2
  194.8 0.6 pad_maximum_fusion
  195.4 26.2 %all-to-all-done.5 = bf16[128,1,8,1024]{3,2,1,0:T(8,128)(2,1)S(1)} async-done(((bf16[128,1,8,1024]{3,2,1,0:T(8,128)(2,1)}), bf16[128,1,8,1024]{3,2,1,0:T(8,128)(2,1)S(1)}, u32[]{:S(2)}, u32[]{:S(2)}) %all-to-all-start.5) | async-done | bytes 2097184 | tf_op jit(solution)/shard_map/all_to_all | solution.py:86
  221.6 0.6 gather_fusion.3
  222.2 1.1 fusion.38
  (31 shorter events, 0.9 us)
Async XLA Ops:
  12.9 11.7 %copy-start = (bf16[1,1024,1024]{2,1,0:T(8,128)(2,1)S(1)}, bf16[1,1024,1024]{2,1,0:T(8,128)(2,1)}, u32[]{:S(2)}) copy-start(bf16[1,1024,1024]{2,1,0:T(8,128)(2,1)} %param.9) | copy-start | bytes 6291460
  12.9 41.0 %all-to-all-start = ((bf16[128,1,8,1024]{3,2,1,0:T(8,128)(2,1)}), bf16[128,1,8,1024]{3,2,1,0:T(8,128)(2,1)}, u32[]{:S(2)}, u32[]{:S(2)}) async-start(bf16[128,1,8,1024]{3,2,1,0:T(8,128)(2,1)} %bitcast.9), calls=%async_computation | async-start | bytes 4194304 | tf_op jit(solution)/shard_map/all_to_all | solution.py:82
  80.5 34.4 %all-to-all-start.2 = ((bf16[128,1,8,1024]{3,2,1,0:T(8,128)(2,1)}), bf16[128,1,8,1024]{3,2,1,0:T(8,128)(2,1)S(1)}, u32[]{:S(2)}, u32[]{:S(2)}) async-start(bf16[128,1,8,1024]{3,2,1,0:T(8,128)(2,1)} %bitcast.17), calls=%async_computation.2 | async-start | bytes 4194304 | tf_op jit(solution)/shard_map/all_to_all | solution.py:86
  125.6 35.1 %all-to-all-start.3 = ((bf16[128,1,8,1024]{3,2,1,0:T(8,128)(2,1)}), bf16[128,1,8,1024]{3,2,1,0:T(8,128)(2,1)}, u32[]{:S(2)}, u32[]{:S(2)}) async-start(bf16[128,1,8,1024]{3,2,1,0:T(8,128)(2,1)} %bitcast.24), calls=%async_computation.3 | async-start | bytes 4194304 | tf_op jit(solution)/shard_map/all_to_all | solution.py:82
  131.4 30.8 %copy-start.1 = (bf16[1,1024,1024]{2,1,0:T(8,128)(2,1)S(1)}, bf16[1,1024,1024]{2,1,0:T(8,128)(2,1)}, u32[]{:S(2)}) copy-start(bf16[1,1024,1024]{2,1,0:T(8,128)(2,1)} %param.9) | copy-start | bytes 6291460
  187.2 34.4 %all-to-all-start.5 = ((bf16[128,1,8,1024]{3,2,1,0:T(8,128)(2,1)}), bf16[128,1,8,1024]{3,2,1,0:T(8,128)(2,1)S(1)}, u32[]{:S(2)}, u32[]{:S(2)}) async-start(bf16[128,1,8,1024]{3,2,1,0:T(8,128)(2,1)} %bitcast.31), calls=%async_computation.5 | async-start | bytes 4194304 | tf_op jit(solution)/shard_map/all_to_all | solution.py:86
where the time goes:
time: 225 us; the launch traced here: 223 us
  waiting for transfers between devices  113 us (50%)
  blocking collectives  27.7 us (12%)
  local copies, waits for them, and re-layouts  27.4 us (12%)
  starting transfers between devices  26.8 us (12%)
  matrix products  19.7 us (9%)
  other arithmetic  7.62 us (3%)
    all_to_all x2, waiting for transfers between devices, local(): lax.all_to_all(outgoing, ('cluster', 'slab'), split_axis=0, concat_axis=0...  58 us
    all_to_all x2, waiting for transfers between devices, local(): lax.all_to_all(shifted_parts, ('cluster', 'slab'), split_axis=0, concat_a...  55.3 us
    all_to_all x2, blocking collectives, local(): lax.all_to_all(log_weights, ('cluster', 'slab'), split_axis=0, concat_axi...  27.7 us
    all_to_all x2, starting transfers between devices, local(): lax.all_to_all(outgoing, ('cluster', 'slab'), split_axis=0, concat_axis=0...  17.5 us
    scatter x2, local copies, waits for them, and re-layouts, local(): outgoing = outgoing.at[slot_index].set(messages)  16.3 us
    dot_general x4, matrix products, partials(): lax.dot_general(query_rows, cluster_rows, (((1,), (1,)), ((), ())), prefe...  10.4 us
    all_to_all x2, starting transfers between devices, local(): lax.all_to_all(shifted_parts, ('cluster', 'slab'), split_axis=0, concat_a...  9.3 us
    dot_general x4, matrix products, partials(): jnp.dot(weights.astype(jnp.bfloat16), cluster_rows, preferred_element_typ...  9.26 us
  transfers between devices with their start and end apart: 4, of which 4 were waited for; matrix products, arithmetic and copies ran while one was open for 2% of the time, Pallas kernels for 0%

commit v1 on v0

v1 whole, which is shorter than its diff:
```python
import functools
import math

import jax
import jax.numpy as jnp
from jax import lax
from jax.experimental import pallas as pl
from jax.experimental.pallas import tpu as pltpu
from jax.sharding import PartitionSpec as P

STEPS = 2
INV_WIDTH = 1.0 / 16.0
LANES = 128
VMEM_LIMIT = 48 * 1024 * 1024


def whole(space):
    return pl.BlockSpec(memory_space=space)


def params():
    return pltpu.CompilerParams(vmem_limit_bytes=VMEM_LIMIT)


def scatter_kernel(pairs_ref, table_ref, blocks_ref, out_ref):
    def body(block, carry):
        rows = blocks_ref[block]
        out_ref[table_ref[pairs_ref[2 * block]]] = rows
        out_ref[table_ref[pairs_ref[2 * block + 1]]] = rows
        return carry

    lax.fori_loop(0, blocks_ref.shape[0], body, 0, unroll=4)


def scatter_blocks(blocks, pairs, table):
    _, rows, features = blocks.shape
    return pl.pallas_call(
        scatter_kernel,
        out_shape=jax.ShapeDtypeStruct((table.shape[0], rows, features), jnp.bfloat16),
        in_specs=[whole(pltpu.SMEM), whole(pltpu.SMEM), whole(pltpu.VMEM)],
        out_specs=whole(pltpu.VMEM),
        compiler_params=params(),
    )(pairs, table, blocks)


def score_kernel(arrived_ref, cluster_ref, norms_ref, out_ref):
    slots, rows, features = arrived_ref.shape
    cluster = cluster_ref[...]
    flat = arrived_ref[...].astype(jnp.float32).reshape(slots * rows, features).astype(jnp.bfloat16)
    products = lax.dot_general(
        flat, cluster, (((1,), (1,)), ((), ())), preferred_element_type=jnp.float32
    )
    scores = (products - norms_ref[...]) * INV_WIDTH
    row_top = jnp.max(scores, axis=1, keepdims=True)
    weights = jnp.exp(scores - row_top)
    totals = jnp.sum(weights, axis=1, keepdims=True)
    summed = jnp.dot(weights.astype(jnp.bfloat16), cluster, preferred_element_type=jnp.float32)
    part = summed * (1.0 / totals)
    out_ref[:, :, :features] = part.reshape(slots, rows, features).astype(jnp.bfloat16)
    log_weight = row_top + jnp.log(totals)
    first = log_weight.astype(jnp.bfloat16).astype(jnp.float32)
    rest = log_weight - first
    second = rest.astype(jnp.bfloat16).astype(jnp.float32)
    third = rest - second
    lane = lax.broadcasted_iota(jnp.int32, (slots * rows, LANES), 1)
    terms = jnp.where(lane == 0, first, jnp.where(lane == 1, second, third))
    out_ref[:, :, features:] = terms.reshape(slots, rows, LANES).astype(jnp.bfloat16)


def score_slots(arrived, cluster_rows, half_norms, group=32):
    slots, rows, features = arrived.shape
    references = cluster_rows.shape[0]
    return pl.pallas_call(
        score_kernel,
        out_shape=jax.ShapeDtypeStruct((slots, rows, features + LANES), jnp.bfloat16),
        grid=(slots // group,),
        in_specs=[
            pl.BlockSpec((group, rows, features), lambda i: (i, 0, 0)),
            pl.BlockSpec((references, features), lambda i: (0, 0)),
            pl.BlockSpec((1, references), lambda i: (0, 0)),
        ],
        out_specs=pl.BlockSpec((group, rows, features + LANES), lambda i: (i, 0, 0)),
        compiler_params=params(),
    )(arrived, cluster_rows, half_norms)


def combine_kernel(
    log_count, pairs_ref, table_ref, blocks_ref, returned_ref, mixed_ref, density_ref, *send_refs
):
    features = blocks_ref.shape[2]

    def read(slot):
        part = returned_ref[slot].astype(jnp.float32)
        terms = part[:, features:]
        return part[:, :features], terms[:, 0:1] + terms[:, 1:2] + terms[:, 2:3]

    def body(block, carry):
        first_slot = table_ref[pairs_ref[2 * block]]
        second_slot = table_ref[pairs_ref[2 * block + 1]]
        first_part, first_log = read(first_slot)
        second_part, second_log = read(second_slot)
        both_top = jnp.maximum(first_log, second_log)
        first_share = jnp.exp(first_log - both_top)
        second_share = jnp.exp(second_log - both_top)
        pair_total = first_share + second_share
        inverse = 1.0 / pair_total
        mixed = (
            (first_share * inverse) * first_part + (second_share * inverse) * second_part
        ).astype(jnp.bfloat16)
        squares = jnp.sum(
            jnp.square(blocks_ref[block].astype(jnp.float32)), axis=1, keepdims=True
        )
        density = both_top + jnp.log(pair_total) - 0.5 * INV_WIDTH * squares - log_count
        density_ref[block] = jnp.broadcast_to(density, density_ref.shape[1:])
        mixed_ref[block] = mixed
        for send_ref in send_refs:
            send_ref[first_slot] = mixed
            send_ref[second_slot] = mixed
        return carry

    lax.fori_loop(0, blocks_ref.shape[0], body, 0, unroll=4)


def combine(blocks, returned, pairs, table, log_count, send):
    count, rows, features = blocks.shape
    outs = [
        jax.ShapeDtypeStruct(blocks.shape, jnp.bfloat16),
        jax.ShapeDtypeStruct((count, rows, LANES), jnp.float32),
    ]
    if send:
        outs.append(jax.ShapeDtypeStruct((table.shape[0], rows, features), jnp.bfloat16))
    return pl.pallas_call(
        functools.partial(combine_kernel, log_count),
        out_shape=outs,
        in_specs=[whole(pltpu.SMEM), whole(pltpu.SMEM), whole(pltpu.VMEM), whole(pltpu.VMEM)],
        out_specs=[whole(pltpu.VMEM)] * len(outs),
        compiler_params=params(),
    )(pairs, table, blocks, returned)


def exchange(array):
    return lax.all_to_all(array, ("cluster", "slab"), split_axis=0, concat_axis=0, tiled=True)


def local(queries, corpus, block_pairs, owner_table):
    cluster_rows = corpus[0]
    references = cluster_rows.shape[0]
    log_count = math.log(2.0 * references)
    half_norms = 0.5 * jnp.sum(jnp.square(cluster_rows.astype(jnp.float32)), axis=1)[None, :]
    pairs = block_pairs.reshape(-1)
    current = queries
    outgoing = scatter_blocks(current, pairs, owner_table)
    densities = []
    for step in range(STEPS):
        answers = score_slots(exchange(outgoing), cluster_rows, half_norms)
        current, density, *outgoing = combine(
            current, exchange(answers), pairs, owner_table, log_count, step < STEPS - 1
        )
        outgoing = outgoing[0] if outgoing else None
        densities.append(density[:, :, 0].reshape(-1))
    return (current, jnp.stack(densities))


def solution(mesh):
    return jax.shard_map(
        local,
        mesh=mesh,
        in_specs=(
            P(("cluster", "slab"), None, None),
            P(("cluster", "slab"), None, None),
            P(("cluster", "slab"), None),
            P(),
        ),
        out_specs=(P(("cluster", "slab"), None, None), P(None, ("cluster", "slab"))),
        check_vma=False,
    )
```

time: 225 us -> 177 us (0.79)
  waiting for transfers between devices: 113 us -> 61.1 us
  blocking collectives: 27.7 us -> 71.6 us
  local copies, waits for them, and re-layouts: 27.4 us -> 4.27 us
  Pallas kernels: 0 us -> 20.6 us
  matrix products: 19.7 us -> 0 us
  starting transfers between devices: 26.8 us -> 16.3 us
  other arithmetic: 7.62 us -> 1.07 us
    all_to_all x4 -> x2, waiting for transfers between devices: 113 us -> 61.1 us  [exchange(): lax.all_to_all(array, ('cluster', 'slab'), split_axis=0, concat_axis=0, t...]
    all_to_all x2, blocking collectives: 27.7 us -> 71.6 us  [exchange(): lax.all_to_all(array, ('cluster', 'slab'), split_axis=0, concat_axis=0, t...]
    pallas_call x0 -> x5, Pallas kernels: none -> 20.6 us  [the longest x2 15 us: score_slots(): pl.pallas_call(score_kernel, out_shape=jax.ShapeDtypeStruct((slots, rows,...]
    dot_general x8 -> x0, matrix products: 19.7 us -> none  [the longest x4 10.4 us: partials(): lax.dot_general(query_rows, cluster_rows, (((1,), (1,)), ((), ())), prefe...]
    scatter x2 -> x0, local copies, waits for them, and re-layouts: 16.3 us -> none  [local(): outgoing = outgoing.at[slot_index].set(messages)]
    all_to_all x4 -> x2, starting transfers between devices: 26.8 us -> 16.3 us  [exchange(): lax.all_to_all(array, ('cluster', 'slab'), split_axis=0, concat_axis=0, t...]
    another operation x10 -> x2, local copies, waits for them, and re-layouts: 6.59 us -> 0.17 us  [local(): return (current, jnp.stack(densities))]
    reduce_sum x9 -> x1, other arithmetic: 5.55 us -> 0.48 us  [local(): jnp.sum(jnp.square(cluster_rows.astype(jnp.float32)), axis=1)[None, :]]
  transfers between devices with their start and end apart: 4 -> 2, of which waited for: 4 -> 2; matrix products, arithmetic and copies ran while one was open for 2% -> 0% of each run, Pallas kernels for 0% -> 0%
where the time goes in v1:
time: 177 us; the launch traced here: 176 us
  blocking collectives  71.6 us (40%)
  waiting for transfers between devices  61.1 us (35%)
  Pallas kernels  20.6 us (12%)
  starting transfers between devices  16.3 us (9%)
  local copies, waits for them, and re-layouts  4.27 us (2%)
    all_to_all x2, blocking collectives, exchange(): lax.all_to_all(array, ('cluster', 'slab'), split_axis=0, concat_axis=0, t...  71.6 us
    all_to_all x2, waiting for transfers between devices, exchange(): lax.all_to_all(array, ('cluster', 'slab'), split_axis=0, concat_axis=0, t...  61.1 us
    all_to_all x2, starting transfers between devices, exchange(): lax.all_to_all(array, ('cluster', 'slab'), split_axis=0, concat_axis=0, t...  16.3 us
    pallas_call x2, Pallas kernels, score_slots(): pl.pallas_call(score_kernel, out_shape=jax.ShapeDtypeStruct((slots, rows,...  15 us
    pallas_call x2, Pallas kernels, combine(): pl.pallas_call(functools.partial(combine_kernel, log_count), out_shape=ou...  4.98 us
    unnamed x13, local copies, waits for them, and re-layouts  3.79 us
  transfers between devices with their start and end apart: 2, of which 2 were waited for; matrix products, arithmetic and copies ran while one was open for 0% of the time, Pallas kernels for 0%

profile of v1, /device:TPU:0, one launch (start us, length us, event | category | flops | bytes accessed | tf_op | source)
XLA Modules:
  0.0 175.7 jit_solution(16147668360581345555)
XLA Ops:
  0.6 0.8 copy.7
  1.4 0.1 reshape.17.pairs_ref
  1.5 0.0 copy-start.2
  1.5 1.0 copy-done.2
  2.5 0.0 copy-start.4
  2.5 0.7 copy-done.4
  3.2 0.7 shard_map.59
  3.9 0.0 copy-start.1
  3.9 1.3 copy-done.1
  5.2 0.0 copy-start
  5.2 11.7 %all-to-all-start = ((bf16[128,8,1024]{2,1,0:T(8,128)(2,1)}), bf16[128,8,1024]{2,1,0:T(8,128)(2,1)}, u32[]{:S(2)}, u32[]{:S(2)}) async-start(bf16[128,8,1024]{2,1,0:T(8,128)(2,1)} %copy-done.1), calls=%async_computation | async-start | bytes 4194304 | tf_op jit(solution)/shard_map/all_to_all | solution.py:142
  16.9 0.0 copy-done
  16.9 0.5 multiply_reduce_fusion
  17.4 28.8 %all-to-all-done.arrived_ref = bf16[128,8,1024]{2,1,0:T(8,128)(2,1)} async-done(((bf16[128,8,1024]{2,1,0:T(8,128)(2,1)}), bf16[128,8,1024]{2,1,0:T(8,128)(2,1)}, u32[]{:S(2)}, u32[]{:S(2)}) %all-to-all-start) | async-done | bytes 2097184 | tf_op jit(solution)/shard_map/all_to_all | solution.py:142
  46.2 8.0 %shard_map.60 = bf16[128,8,1152]{2,1,0:T(8,128)(2,1)} custom-call(bf16[128,8,1024]{2,1,0:T(8,128)(2,1)} %all-to-all-done.arrived_ref, bf16[1024,1024]{1,0:T(8,128)(2,1)S(1)} %bitcast.3, f32[1,1024]{1,0:T(1,128)S(1)} %bitcast.5), custom_call_target="tpu_custom_call" | custom-call | tf_op jit(solution)/shard_map/pallas_call | solution.py:73
  54.2 0.0 copy-start.3
  54.2 0.0 copy-start.5
  54.2 37.5 %all_to_all.20.returned_ref = bf16[128,8,1152]{2,1,0:T(8,128)(2,1)S(1)} all-to-all(bf16[128,8,1152]{2,1,0:T(8,128)(2,1)} %shard_map.60), channel_id=1, replica_groups=mesh['cluster'=8,'slab'=16] {'cluster','slab'}, dimensions={0} | all-to-all | bytes 4718592 | tf_op jit(solution)/shard_map/all_to_all | solution.py:142
  91.7 0.0 copy-done.3
  91.7 0.0 copy-done.5
  91.7 2.1 %shard_map.61 = (bf16[32,8,1024]{2,1,0:T(8,128)(2,1)S(1)}, f32[32,8,128]{2,1,0:T(8,128)S(1)}, bf16[128,8,1024]{2,1,0:T(8,128)(2,1)S(1)}) custom-call(s32[64]{0:T(128)S(1)} %reshape.17.pairs_ref, s32[128]{0:T(128)S(1)} %copy-done.5, bf16[32,8,1024]{2,1,0:T(8,128)(2,1)S(1)} %copy-done.3, bf16[128,8,1152]{2,1,0:T(8,128)(2,1)S(1)} %all_to_all.20.returned_ref), custom_call_target="tpu_custom_call" | custom-call | tf_op jit(solution)/shard_map/pallas_call | solution.py:132
  93.8 34.1 %all_to_all.21.arrived_ref = bf16[128,8,1024]{2,1,0:T(8,128)(2,1)S(1)} all-to-all(bf16[128,8,1024]{2,1,0:T(8,128)(2,1)S(1)} %get-tuple-element.8), channel_id=1, replica_groups=mesh['cluster'=8,'slab'=16] {'cluster','slab'}, dimensions={0} | all-to-all | bytes 4194304 | tf_op jit(solution)/shard_map/all_to_all | solution.py:142
  127.9 6.9 %shard_map.62 = bf16[128,8,1152]{2,1,0:T(8,128)(2,1)} custom-call(bf16[128,8,1024]{2,1,0:T(8,128)(2,1)S(1)} %all_to_all.21.arrived_ref, bf16[1024,1024]{1,0:T(8,128)(2,1)S(1)} %bitcast.4, f32[1,1024]{1,0:T(1,128)S(1)} %bitcast.6), custom_call_target="tpu_custom_call" | custom-call | tf_op jit(solution)/shard_map/pallas_call | solution.py:73
  134.9 4.7 %all-to-all-start.3 = ((bf16[128,8,1152]{2,1,0:T(8,128)(2,1)}), bf16[128,8,1152]{2,1,0:T(8,128)(2,1)S(1)}, u32[]{:S(2)}, u32[]{:S(2)}) async-start(bf16[128,8,1152]{2,1,0:T(8,128)(2,1)} %shard_map.62), calls=%async_computation.3 | async-start | bytes 4718592 | tf_op jit(solution)/shard_map/all_to_all | solution.py:142
  139.5 0.1 slice_reduce_fusion.1
  139.6 0.1 stack_reshape_squeeze.6
  139.7 32.3 %all-to-all-done.3.returned_ref = bf16[128,8,1152]{2,1,0:T(8,128)(2,1)S(1)} async-done(((bf16[128,8,1152]{2,1,0:T(8,128)(2,1)}), bf16[128,8,1152]{2,1,0:T(8,128)(2,1)S(1)}, u32[]{:S(2)}, u32[]{:S(2)}) %all-to-all-start.3) | async-done | bytes 2359328 | tf_op jit(solution)/shard_map/all_to_all | solution.py:142
  172.0 2.9 %shard_map.63 = (bf16[32,8,1024]{2,1,0:T(8,128)(2,1)}, f32[32,8,128]{2,1,0:T(8,128)S(1)}) custom-call(s32[64]{0:T(128)S(1)} %reshape.17.pairs_ref, s32[128]{0:T(128)S(1)} %copy-done.5, bf16[32,8,1024]{2,1,0:T(8,128)(2,1)S(1)} %get-tuple-element.7.blocks_ref, bf16[128,8,1152]{2,1,0:T(8,128)(2,1)S(1)} %all-to-all-done.3.returned_ref), custom_call_target="tpu_custom_call" | custom-call | tf_op jit(solution)/shard_map/pallas_call | solution.py:132
  174.9 0.1 slice_reduce_fusion
  175.0 0.1 stack_reshape_squeeze.7
  175.1 0.6 pad_maximum_fusion
  (1 shorter events, 0.0 us)
Async XLA Ops:
  1.5 1.0 copy-start.2
  2.5 0.7 copy-start.4
  3.9 1.3 copy-start.1
  5.2 11.7 %copy-start = (bf16[1,1024,1024]{2,1,0:T(8,128)(2,1)S(1)}, bf16[1,1024,1024]{2,1,0:T(8,128)(2,1)}, u32[]{:S(2)}) copy-start(bf16[1,1024,1024]{2,1,0:T(8,128)(2,1)} %param.5) | copy-start | bytes 6291460
  5.2 41.0 %all-to-all-start = ((bf16[128,8,1024]{2,1,0:T(8,128)(2,1)}), bf16[128,8,1024]{2,1,0:T(8,128)(2,1)}, u32[]{:S(2)}, u32[]{:S(2)}) async-start(bf16[128,8,1024]{2,1,0:T(8,128)(2,1)} %copy-done.1), calls=%async_computation | async-start | bytes 4194304 | tf_op jit(solution)/shard_map/all_to_all | solution.py:142
  54.2 37.5 %copy-start.3 = (bf16[32,8,1024]{2,1,0:T(8,128)(2,1)S(1)}, bf16[32,8,1024]{2,1,0:T(8,128)(2,1)}, u32[]{:S(2)}) copy-start(bf16[32,8,1024]{2,1,0:T(8,128)(2,1)} %blocks_ref.3) | copy-start | bytes 1572868
  54.2 37.5 %copy-start.5 = (s32[128]{0:T(128)S(1)}, s32[128]{0:T(128)}, u32[]{:S(2)}) copy-start(s32[128]{0:T(128)} %table_ref.5) | copy-start | bytes 1540
  134.9 37.1 %all-to-all-start.3 = ((bf16[128,8,1152]{2,1,0:T(8,128)(2,1)}), bf16[128,8,1152]{2,1,0:T(8,128)(2,1)S(1)}, u32[]{:S(2)}, u32[]{:S(2)}) async-start(bf16[128,8,1152]{2,1,0:T(8,128)(2,1)} %shard_map.62), calls=%async_computation.3 | async-start | bytes 4718592 | tf_op jit(solution)/shard_map/all_to_all | solution.py:142

commit v2 on v1

v2 whole, which is shorter than its diff:
```python
import functools
import math

import jax
import jax.numpy as jnp
from jax import lax
from jax.experimental import pallas as pl
from jax.experimental.pallas import tpu as pltpu
from jax.sharding import PartitionSpec as P

STEPS = 2
INV_WIDTH = 1.0 / 16.0
LANES = 128
VMEM_LIMIT = 48 * 1024 * 1024
AXES = ("cluster", "slab")
SIDE = 4
CORES = 2
DEPTH = 4
SLABS = SIDE * SIDE
CLUSTER_DEVICES = DEPTH * CORES


def slab_order(core):
    order = [(a, (a + b) % SIDE) for b in range(SIDE) for a in range(SIDE)]
    return [x * SIDE + y if core == 0 else y * SIDE + x for x, y in order]


def slab_groups():
    return [
        [cluster * SLABS + slab for slab in slab_order(cluster % CORES)]
        for cluster in range(CLUSTER_DEVICES)
    ]


def slab_places(core):
    places = [0] * SLABS
    for place, slab in enumerate(slab_order(core)):
        places[slab] = place
    return places


def exchange_slabs(array):
    return lax.all_to_all(
        array, AXES, split_axis=0, concat_axis=0, tiled=True, axis_index_groups=slab_groups()
    )


def shift_depth(array, shift):
    pairs = []
    for z in range(DEPTH):
        for core in range(CORES):
            for slab in range(SLABS):
                source = (z * CORES + core) * SLABS + slab
                target = ((z + shift) % DEPTH * CORES + core) * SLABS + slab
                pairs.append((source, target))
    return lax.ppermute(array, AXES, pairs)


def swap_cores(array):
    pairs = []
    for cluster in range(CLUSTER_DEVICES):
        for slab in range(SLABS):
            pairs.append((cluster * SLABS + slab, (cluster ^ 1) * SLABS + slab))
    return lax.ppermute(array, AXES, pairs)


def whole(space):
    return pl.BlockSpec(memory_space=space)


SMEM, VMEM = whole(pltpu.SMEM), whole(pltpu.VMEM)


def params():
    return pltpu.CompilerParams(vmem_limit_bytes=VMEM_LIMIT)


def fill_kernel(pairs_ref, table_ref, places_ref, blocks_ref, out_ref, slots_ref, counts_ref):
    count, rows, features = blocks_ref.shape
    per_slab = 2 * count // SLABS

    def clear(place, carry):
        counts_ref[place] = 0
        return carry

    lax.fori_loop(0, SLABS, clear, 0)

    def body(block, carry):
        values = blocks_ref[block]
        for side in range(2):
            message = 2 * block + side
            entry = table_ref[pairs_ref[message]]
            place = places_ref[lax.rem(entry, SLABS)]
            rank = counts_ref[place]
            counts_ref[place] = rank + 1
            slot = place * per_slab + rank
            slots_ref[message] = slot
            out_ref[slot, :, :features] = values
            target = lax.div(entry, SLABS).astype(jnp.float32)
            out_ref[slot, :, features:] = jnp.full((rows, LANES), target, jnp.float32).astype(
                jnp.bfloat16
            )
        return carry

    lax.fori_loop(0, count, body, 0, unroll=4)


def fill(blocks, pairs, table, places):
    count, rows, features = blocks.shape
    return pl.pallas_call(
        fill_kernel,
        out_shape=[
            jax.ShapeDtypeStruct((2 * count, rows, features + LANES), jnp.bfloat16),
            jax.ShapeDtypeStruct((2 * count,), jnp.int32),
        ],
        in_specs=[SMEM, SMEM, SMEM, VMEM],
        out_specs=[VMEM, SMEM],
        scratch_shapes=[pltpu.SMEM((SLABS,), jnp.int32)],
        compiler_params=params(),
    )(pairs, table, places, blocks)


def sort_kernel(origin_ref, arrived_ref, *out_refs):
    size, _, features = out_refs[0].shape
    for shift, out_ref in enumerate(out_refs):

        def body(index, carry, shift=shift, out_ref=out_ref):
            out_ref[index] = arrived_ref[origin_ref[shift * size + index], :, :features]
            return carry

        lax.fori_loop(0, size, body, 0, unroll=4)


def sort_by_depth(arrived, origin, features):
    total, rows, _ = arrived.shape
    part = jax.ShapeDtypeStruct((total // DEPTH, rows, features), jnp.bfloat16)
    return pl.pallas_call(
        sort_kernel,
        out_shape=[part] * DEPTH,
        in_specs=[SMEM, VMEM],
        out_specs=[VMEM] * DEPTH,
        compiler_params=params(),
    )(origin, arrived)


def unsort_kernel(origin_ref, *refs):
    part_refs, out_ref = refs[:-1], refs[-1]
    size = part_refs[0].shape[0]
    for shift, part_ref in enumerate(part_refs):

        def body(index, carry, shift=shift, part_ref=part_ref):
            out_ref[origin_ref[shift * size + index]] = part_ref[index]
            return carry

        lax.fori_loop(0, size, body, 0, unroll=4)


def unsort(parts, origin):
    size, rows, width = parts[0].shape
    return pl.pallas_call(
        unsort_kernel,
        out_shape=jax.ShapeDtypeStruct((DEPTH * size, rows, width), jnp.bfloat16),
        in_specs=[SMEM] + [VMEM] * DEPTH,
        out_specs=VMEM,
        compiler_params=params(),
    )(origin, *parts)


def score(flat, cluster, norms):
    products = lax.dot_general(
        flat, cluster, (((1,), (1,)), ((), ())), preferred_element_type=jnp.float32
    )
    scores = (products - norms) * INV_WIDTH
    row_top = jnp.max(scores, axis=1, keepdims=True)
    weights = jnp.exp(scores - row_top)
    totals = jnp.sum(weights, axis=1, keepdims=True)
    summed = jnp.dot(weights.astype(jnp.bfloat16), cluster, preferred_element_type=jnp.float32)
    log_weight = row_top + jnp.log(totals)
    first = log_weight.astype(jnp.bfloat16).astype(jnp.float32)
    rest = log_weight - first
    second = rest.astype(jnp.bfloat16).astype(jnp.float32)
    third = rest - second
    lane = lax.broadcasted_iota(jnp.int32, (flat.shape[0], LANES), 1)
    terms = jnp.where(lane == 0, first, jnp.where(lane == 1, second, third))
    return summed * (1.0 / totals), terms


def score_kernel(*refs):
    part_refs, refs = refs[:DEPTH], refs[DEPTH:]
    cluster_refs, norm_refs, out_refs = refs[:CORES], refs[CORES : 2 * CORES], refs[2 * CORES :]
    size, rows, features = part_refs[0].shape
    half = size // CORES
    for side in range(CORES):
        span = slice(side * half, (side + 1) * half)
        flat = jnp.concatenate(
            [
                part_ref[span].astype(jnp.float32).reshape(half * rows, features)
                for part_ref in part_refs
            ]
        ).astype(jnp.bfloat16)
        part, terms = score(flat, cluster_refs[side][...], norm_refs[side][...])
        for shift, out_ref in enumerate(out_refs):
            lines = slice(shift * half * rows, (shift + 1) * half * rows)
            out_ref[span, :, :features] = (
                part[lines].reshape(half, rows, features).astype(jnp.bfloat16)
            )
            out_ref[span, :, features:] = (
                terms[lines].reshape(half, rows, LANES).astype(jnp.bfloat16)
            )


def score_parts(parts, clusters, norms):
    size, rows, features = parts[0].shape
    out = jax.ShapeDtypeStruct((size, rows, features + LANES), jnp.bfloat16)
    return pl.pallas_call(
        score_kernel,
        out_shape=[out] * DEPTH,
        in_specs=[VMEM] * (DEPTH + 2 * CORES),
        out_specs=[VMEM] * DEPTH,
        compiler_params=params(),
    )(*parts, *clusters, *norms)


def combine_kernel(log_count, slots_ref, blocks_ref, returned_ref, mixed_ref, density_ref, *send_refs):
    features = blocks_ref.shape[2]

    def read(slot):
        part = returned_ref[slot].astype(jnp.float32)
        terms = part[:, features:]
        return part[:, :features], terms[:, 0:1] + terms[:, 1:2] + terms[:, 2:3]

    def body(block, carry):
        first_slot, second_slot = slots_ref[2 * block], slots_ref[2 * block + 1]
        first_part, first_log = read(first_slot)
        second_part, second_log = read(second_slot)
        both_top = jnp.maximum(first_log, second_log)
        first_share = jnp.exp(first_log - both_top)
        second_share = jnp.exp(second_log - both_top)
        pair_total = first_share + second_share
        inverse = 1.0 / pair_total
        mixed = (
            (first_share * inverse) * first_part + (second_share * inverse) * second_part
        ).astype(jnp.bfloat16)
        squares = jnp.sum(
            jnp.square(blocks_ref[block].astype(jnp.float32)), axis=1, keepdims=True
        )
        density = both_top + jnp.log(pair_total) - 0.5 * INV_WIDTH * squares - log_count
        density_ref[block] = jnp.broadcast_to(density, density_ref.shape[1:])
        mixed_ref[block] = mixed
        for send_ref in send_refs:
            send_ref[first_slot] = mixed
            send_ref[second_slot] = mixed
        return carry

    lax.fori_loop(0, blocks_ref.shape[0], body, 0, unroll=4)


def combine(blocks, returned, slots, log_count, send):
    count, rows, features = blocks.shape
    outs = [
        jax.ShapeDtypeStruct(blocks.shape, jnp.bfloat16),
        jax.ShapeDtypeStruct((count, rows, LANES), jnp.float32),
    ]
    if send:
        outs.append(jax.ShapeDtypeStruct((2 * count, rows, features), jnp.bfloat16))
    return pl.pallas_call(
        functools.partial(combine_kernel, log_count),
        out_shape=outs,
        in_specs=[SMEM, VMEM, VMEM],
        out_specs=[VMEM] * len(outs),
        compiler_params=params(),
    )(slots, blocks, returned)


def half_norms_of(cluster_rows):
    return 0.5 * jnp.sum(jnp.square(cluster_rows.astype(jnp.float32)), axis=1)[None, :]


def sorted_origins(arrived, features, depth, core):
    targets = arrived[:, 0, features].astype(jnp.int32)
    total = targets.shape[0]
    per_cluster = total // CLUSTER_DEVICES
    order = jnp.arange(total, dtype=jnp.int32)
    earlier = (targets[:, None] == targets[None, :]) & (order[None, :] < order[:, None])
    rank = jnp.sum(earlier.astype(jnp.int32), axis=1)
    shift = (targets // CORES - depth) % DEPTH
    side = (targets % CORES) ^ core
    slot = (shift * CORES + side) * per_cluster + rank
    return jnp.sum(jnp.where(slot[None, :] == order[:, None], order[None, :], 0), axis=1)


def local(queries, corpus, block_pairs, owner_table):
    features = queries.shape[2]
    cluster_index = lax.axis_index("cluster").astype(jnp.int32)
    depth, core = cluster_index // CORES, cluster_index % CORES
    places = jnp.where(
        core == 0,
        jnp.array(slab_places(0), jnp.int32),
        jnp.array(slab_places(1), jnp.int32),
    )
    own = corpus[0]
    other = swap_cores(own)
    clusters = (own, other)
    norms = (half_norms_of(own), half_norms_of(other))
    log_count = math.log(2.0 * own.shape[0])
    current = queries
    outgoing, slots = fill(current, block_pairs.reshape(-1), owner_table, places)
    origin = None
    densities = []
    for step in range(STEPS):
        arrived = exchange_slabs(outgoing)
        if step == 0:
            origin = sorted_origins(arrived, features, depth, core)
        parts = sort_by_depth(arrived, origin, features)
        parts = [parts[0]] + [shift_depth(parts[k], k) for k in range(1, DEPTH)]
        answers = score_parts(parts, clusters, norms)
        answers = [answers[0]] + [shift_depth(answers[k], -k) for k in range(1, DEPTH)]
        returned = exchange_slabs(unsort(answers, origin))
        current, density, *outgoing = combine(
            current, returned, slots, log_count, step < STEPS - 1
        )
        outgoing = outgoing[0] if outgoing else None
        densities.append(density[:, :, 0].reshape(-1))
    return (current, jnp.stack(densities))


def solution(mesh):
    return jax.shard_map(
        local,
        mesh=mesh,
        in_specs=(
            P(("cluster", "slab"), None, None),
            P(("cluster", "slab"), None, None),
            P(("cluster", "slab"), None),
            P(),
        ),
        out_specs=(P(("cluster", "slab"), None, None), P(None, ("cluster", "slab"))),
        check_vma=False,
    )
```

time: 177 us -> 184 us (1.040)
  blocking collectives: 71.6 us -> 42.6 us
  waiting for transfers between devices: 61.1 us -> 82.4 us
  starting transfers between devices: 16.3 us -> 28.7 us
  other arithmetic: 1.07 us -> 5.36 us
    ppermute x0 -> x13, waiting for transfers between devices: none -> 47 us  [the longest x12 47 us: shift_depth(): return lax.ppermute(array, AXES, pairs)]
    all_to_all x2, blocking collectives: 71.6 us -> 42.6 us  [exchange_slabs(): lax.all_to_all(array, AXES, split_axis=0, concat_axis=0, tiled=True, axis...]
    all_to_all x2, waiting for transfers between devices: 61.1 us -> 35.4 us  [exchange_slabs(): lax.all_to_all(array, AXES, split_axis=0, concat_axis=0, tiled=True, axis...]
    ppermute x0 -> x13, starting transfers between devices: none -> 17.2 us  [the longest x12 17.2 us: shift_depth(): return lax.ppermute(array, AXES, pairs)]
    all_to_all x2, starting transfers between devices: 16.3 us -> 11.4 us  [exchange_slabs(): lax.all_to_all(array, AXES, split_axis=0, concat_axis=0, tiled=True, axis...]
    reduce_sum x1 -> x4, other arithmetic: 0.48 us -> 2.84 us  [the longest x2 2.54 us: half_norms_of(): jnp.sum(jnp.square(cluster_rows.astype(jnp.float32)), axis=1)[None, :]]
    pallas_call x3 -> x7, Pallas kernels: 15.7 us -> 14.5 us  [the longest x2 8.84 us: score_parts(): pl.pallas_call(score_kernel, out_shape=[out] * DEPTH, in_specs=[VMEM] * (...]
    unnamed x13 -> x11, local copies, waits for them, and re-layouts: 3.79 us -> 3.6 us
  transfers between devices with their start and end apart: 2 -> 15, of which waited for: 2 -> 10; matrix products, arithmetic and copies ran while one was open for 0% -> 3% of each run, Pallas kernels for 0% -> 1%
where the time goes in v2:
time: 184 us; the launch traced here: 183 us
  waiting for transfers between devices  82.4 us (45%)
  blocking collectives  42.6 us (23%)
  starting transfers between devices  28.7 us (16%)
  Pallas kernels  19.5 us (11%)
  other arithmetic  5.36 us (3%)
  local copies, waits for them, and re-layouts  4.09 us (2%)
    ppermute x12, waiting for transfers between devices, shift_depth(): return lax.ppermute(array, AXES, pairs)  47 us
    all_to_all x2, blocking collectives, exchange_slabs(): lax.all_to_all(array, AXES, split_axis=0, concat_axis=0, tiled=True, axis...  42.6 us
    all_to_all x2, waiting for transfers between devices, exchange_slabs(): lax.all_to_all(array, AXES, split_axis=0, concat_axis=0, tiled=True, axis...  35.4 us
    ppermute x12, starting transfers between devices, shift_depth(): return lax.ppermute(array, AXES, pairs)  17.2 us
    all_to_all x2, starting transfers between devices, exchange_slabs(): lax.all_to_all(array, AXES, split_axis=0, concat_axis=0, tiled=True, axis...  11.4 us
    pallas_call x2, Pallas kernels, score_parts(): pl.pallas_call(score_kernel, out_shape=[out] * DEPTH, in_specs=[VMEM] * (...  8.84 us
    pallas_call x2, Pallas kernels, combine(): pl.pallas_call(functools.partial(combine_kernel, log_count), out_shape=ou...  4.93 us
  transfers between devices with their start and end apart: 15, of which 10 were waited for; matrix products, arithmetic and copies ran while one was open for 3% of the time, Pallas kernels for 1%

profile of v2, /device:TPU:0, one launch (start us, length us, event | category | flops | bytes accessed | tf_op | source)
XLA Modules:
  0.0 183.4 jit_solution(18063491389444798490)
XLA Ops:
  0.7 0.9 copy.10
  1.6 0.1 reshape.87.pairs_ref
  1.7 0.7 broadcast_select_fusion.places_ref
  2.4 1.0 copy-done.1
  3.5 0.7 copy-done.4
  4.1 1.8 shard_map.77
  5.9 1.0 copy-done.3
  6.9 7.1 %all-to-all-start = ((bf16[64,8,1152]{2,1,0:T(8,128)(2,1)}), bf16[64,8,1152]{2,1,0:T(8,128)(2,1)S(1)}, u32[]{:S(2)}, u32[]{:S(2)}) async-start(bf16[64,8,1152]{2,1,0:T(8,128)(2,1)} %copy-done.3), calls=%async_computation | async-start | bytes 2359296 | tf_op jit(solution)/shard_map/all_to_all | solution.py:43
  14.1 0.5 multiply_reduce_fusion.1
  14.5 17.9 %all-to-all-done.arrived_ref = bf16[64,8,1152]{2,1,0:T(8,128)(2,1)S(1)} async-done(((bf16[64,8,1152]{2,1,0:T(8,128)(2,1)}), bf16[64,8,1152]{2,1,0:T(8,128)(2,1)S(1)}, u32[]{:S(2)}, u32[]{:S(2)}) %all-to-all-start) | async-done | bytes 1179680 | tf_op jit(solution)/shard_map/all_to_all | solution.py:43
  32.4 1.2 fusion
  33.6 0.2 convert_reduce_fusion
  33.8 0.1 select_reduce_fusion.origin_ref
  34.0 0.7 shard_map.78
  34.7 2.0 %collective-permute-start = (bf16[16,8,1024]{2,1,0:T(8,128)(2,1)S(1)}, bf16[16,8,1024]{2,1,0:T(8,128)(2,1)S(1)}, u32[]{:S(2)}, u32[]{:S(2)}) collective-permute-start(bf16[16,8,1024]{2,1,0:T(8,128)(2,1)S(1)} %get-tuple-element.28), channel_id=1, source_target_pairs={{0,32},{1,33},{2,34},{3,35},{4,36},{5,37},{6,38},{7,39},{8,40},{9,... | collective-permute-start | bytes 786440 | tf_op jit(solution)/shard_map/ppermute | solution.py:56
  36.7 3.6 %collective-permute-start.1 = (bf16[16,8,1024]{2,1,0:T(8,128)(2,1)S(1)}, bf16[16,8,1024]{2,1,0:T(8,128)(2,1)S(1)}, u32[]{:S(2)}, u32[]{:S(2)}) collective-permute-start(bf16[16,8,1024]{2,1,0:T(8,128)(2,1)S(1)} %get-tuple-element.29), channel_id=1, source_target_pairs={{0,64},{1,65},{2,66},{3,67},{4,68},{5,69},{6,70},{7,71},{8,72},{9,... | collective-permute-start | bytes 786440 | tf_op jit(solution)/shard_map/ppermute | solution.py:56
  40.2 1.0 collective-permute-start.2
  41.3 2.1 %multiply_reduce_fusion = f32[1024]{0:T(1024)S(1)} fusion(bf16[1024,1024]{1,0:T(8,128)(2,1)} %collective-permute-done.3.refs_5_), kind=kLoop, calls=%fused_computation | loop fusion | flops 3144704 | bytes 2101248 | tf_op jit(solution)/shard_map/reduce_sum | solution.py:276
  43.3 1.8 collective-permute-done.refs_1_
  45.1 6.3 %collective-permute-done.1.refs_2_ = bf16[16,8,1024]{2,1,0:T(8,128)(2,1)S(1)} collective-permute-done((bf16[16,8,1024]{2,1,0:T(8,128)(2,1)S(1)}, bf16[16,8,1024]{2,1,0:T(8,128)(2,1)S(1)}, u32[]{:S(2)}, u32[]{:S(2)}) %collective-permute-start.1) | collective-permute-done | bytes 262176 | tf_op jit(solution)/shard_map/ppermute | solution.py:56
  51.4 4.4 %shard_map.79 = (bf16[16,8,1152]{2,1,0:T(8,128)(2,1)S(1)}, bf16[16,8,1152]{2,1,0:T(8,128)(2,1)S(1)}, bf16[16,8,1152]{2,1,0:T(8,128)(2,1)S(1)}, bf16[16,8,1152]{2,1,0:T(8,128)(2,1)S(1)}) custom-call(bf16[16,8,1024]{2,1,0:T(8,128)(2,1)S(1)} %get-tuple-element.27.refs_0_, bf16[16,8,1024]{2,1,0:T(8,128)(2,1)S(1)} %collective-permute-done.refs_1_, ...), custom_call_target="tpu_custom_call" | custom-call | tf_op jit(solution)/shard_map/pallas_call | solution.py:215
  55.9 2.2 %collective-permute-start.4 = (bf16[16,8,1152]{2,1,0:T(8,128)(2,1)S(1)}, bf16[16,8,1152]{2,1,0:T(8,128)(2,1)S(1)}, u32[]{:S(2)}, u32[]{:S(2)}) collective-permute-start(bf16[16,8,1152]{2,1,0:T(8,128)(2,1)S(1)} %get-tuple-element.32), channel_id=1, source_target_pairs={{0,96},{1,97},{2,98},{3,99},{4,100},{5,101},{6,102},{7,103},{8,104... | collective-permute-start | bytes 884744 | tf_op jit(solution)/shard_map/ppermute | solution.py:56
  58.1 1.1 collective-permute-start.5
  59.2 0.4 collective-permute-start.6
  59.6 11.3 %collective-permute-done.4.refs_1_ = bf16[16,8,1152]{2,1,0:T(8,128)(2,1)S(1)} collective-permute-done((bf16[16,8,1152]{2,1,0:T(8,128)(2,1)S(1)}, bf16[16,8,1152]{2,1,0:T(8,128)(2,1)S(1)}, u32[]{:S(2)}, u32[]{:S(2)}) %collective-permute-start.4) | collective-permute-done | bytes 294944 | tf_op jit(solution)/shard_map/ppermute | solution.py:56
  70.9 3.7 %collective-permute-done.6.refs_3_ = bf16[16,8,1152]{2,1,0:T(8,128)(2,1)S(1)} collective-permute-done((bf16[16,8,1152]{2,1,0:T(8,128)(2,1)S(1)}, bf16[16,8,1152]{2,1,0:T(8,128)(2,1)S(1)}, u32[]{:S(2)}, u32[]{:S(2)}) %collective-permute-start.6) | collective-permute-done | bytes 294944 | tf_op jit(solution)/shard_map/ppermute | solution.py:56
  74.6 0.7 shard_map.80
  75.3 23.8 %all_to_all.20.returned_ref = bf16[64,8,1152]{2,1,0:T(8,128)(2,1)S(1)} all-to-all(bf16[64,8,1152]{2,1,0:T(8,128)(2,1)S(1)} %shard_map.80), channel_id=1, replica_groups={{0,5,10,15,1,6,11,12,2,7,8,13,3,4,9,14},{16,21,26,31,20,25,30,19,24,29,..., dimensions={0} | all-to-all | bytes 2359296 | tf_op jit(solution)/shard_map/all_to_all | solution.py:43
  99.1 2.1 %shard_map.81 = (bf16[32,8,1024]{2,1,0:T(8,128)(2,1)S(1)}, f32[32,8,128]{2,1,0:T(8,128)S(1)}, bf16[64,8,1024]{2,1,0:T(8,128)(2,1)S(1)}) custom-call(s32[64]{0:T(128)S(1)} %get-tuple-element.25.slots_ref, bf16[32,8,1024]{2,1,0:T(8,128)(2,1)S(1)} %copy-done.2, bf16[64,8,1152]{2,1,0:T(8,128)(2,1)S(1)} %all_to_all.20.returned_ref), custom_call_target="tpu_custom_call" | custom-call | tf_op jit(solution)/shard_map/pallas_call | solution.py:266
  101.2 18.7 %all_to_all.21.arrived_ref = bf16[64,8,1024]{2,1,0:T(8,128)(2,1)S(1)} all-to-all(bf16[64,8,1024]{2,1,0:T(8,128)(2,1)S(1)} %get-tuple-element.36), channel_id=1, replica_groups={{0,5,10,15,1,6,11,12,2,7,8,13,3,4,9,14},{16,21,26,31,20,25,30,19,24,29,..., dimensions={0} | all-to-all | bytes 2097152 | tf_op jit(solution)/shard_map/all_to_all | solution.py:43
  120.0 0.7 shard_map.82
  120.7 0.9 collective-permute-start.8
  121.6 2.5 %collective-permute-start.9 = (bf16[16,8,1024]{2,1,0:T(8,128)(2,1)S(1)}, bf16[16,8,1024]{2,1,0:T(8,128)(2,1)S(1)}, u32[]{:S(2)}, u32[]{:S(2)}) collective-permute-start(bf16[16,8,1024]{2,1,0:T(8,128)(2,1)S(1)} %get-tuple-element.40), channel_id=1, source_target_pairs={{0,96},{1,97},{2,98},{3,99},{4,100},{5,101},{6,102},{7,103},{8,104... | collective-permute-start | bytes 786440 | tf_op jit(solution)/shard_map/ppermute | solution.py:56
  124.2 9.2 %collective-permute-done.7.refs_1_ = bf16[16,8,1024]{2,1,0:T(8,128)(2,1)S(1)} collective-permute-done((bf16[16,8,1024]{2,1,0:T(8,128)(2,1)S(1)}, bf16[16,8,1024]{2,1,0:T(8,128)(2,1)S(1)}, u32[]{:S(2)}, u32[]{:S(2)}) %collective-permute-start.7) | collective-permute-done | bytes 262176 | tf_op jit(solution)/shard_map/ppermute | solution.py:56
  133.3 0.6 collective-permute-done.9.refs_3_
  133.9 4.4 %shard_map.83 = (bf16[16,8,1152]{2,1,0:T(8,128)(2,1)S(1)}, bf16[16,8,1152]{2,1,0:T(8,128)(2,1)S(1)}, bf16[16,8,1152]{2,1,0:T(8,128)(2,1)S(1)}, bf16[16,8,1152]{2,1,0:T(8,128)(2,1)S(1)}) custom-call(bf16[16,8,1024]{2,1,0:T(8,128)(2,1)S(1)} %get-tuple-element.37.refs_0_, bf16[16,8,1024]{2,1,0:T(8,128)(2,1)S(1)} %collective-permute-done.7.refs_1_, ...), custom_call_target="tpu_custom_call" | custom-call | tf_op jit(solution)/shard_map/pallas_call | solution.py:215
  138.4 2.4 %collective-permute-start.10 = (bf16[16,8,1152]{2,1,0:T(8,128)(2,1)S(1)}, bf16[16,8,1152]{2,1,0:T(8,128)(2,1)S(1)}, u32[]{:S(2)}, u32[]{:S(2)}) collective-permute-start(bf16[16,8,1152]{2,1,0:T(8,128)(2,1)S(1)} %get-tuple-element.42), channel_id=1, source_target_pairs={{0,96},{1,97},{2,98},{3,99},{4,100},{5,101},{6,102},{7,103},{8,104... | collective-permute-start | bytes 884744 | tf_op jit(solution)/shard_map/ppermute | solution.py:56
  140.8 0.9 collective-permute-start.12
  141.7 10.8 %collective-permute-done.10.refs_1_ = bf16[16,8,1152]{2,1,0:T(8,128)(2,1)S(1)} collective-permute-done((bf16[16,8,1152]{2,1,0:T(8,128)(2,1)S(1)}, bf16[16,8,1152]{2,1,0:T(8,128)(2,1)S(1)}, u32[]{:S(2)}, u32[]{:S(2)}) %collective-permute-start.10) | collective-permute-done | bytes 294944 | tf_op jit(solution)/shard_map/ppermute | solution.py:56
  152.5 3.4 %collective-permute-done.12.refs_3_ = bf16[16,8,1152]{2,1,0:T(8,128)(2,1)S(1)} collective-permute-done((bf16[16,8,1152]{2,1,0:T(8,128)(2,1)S(1)}, bf16[16,8,1152]{2,1,0:T(8,128)(2,1)S(1)}, u32[]{:S(2)}, u32[]{:S(2)}) %collective-permute-start.12) | collective-permute-done | bytes 294944 | tf_op jit(solution)/shard_map/ppermute | solution.py:56
  155.9 1.8 shard_map.84
  157.7 4.3 %all-to-all-start.3 = ((bf16[64,8,1152]{2,1,0:T(8,128)(2,1)}), bf16[64,8,1152]{2,1,0:T(8,128)(2,1)S(1)}, u32[]{:S(2)}, u32[]{:S(2)}) async-start(bf16[64,8,1152]{2,1,0:T(8,128)(2,1)} %shard_map.84), calls=%async_computation.3 | async-start | bytes 2359296 | tf_op jit(solution)/shard_map/all_to_all | solution.py:43
  162.0 0.1 slice_reduce_fusion.1
  162.1 0.1 stack_reshape_squeeze.6
  162.2 17.5 %all-to-all-done.3.returned_ref = bf16[64,8,1152]{2,1,0:T(8,128)(2,1)S(1)} async-done(((bf16[64,8,1152]{2,1,0:T(8,128)(2,1)}), bf16[64,8,1152]{2,1,0:T(8,128)(2,1)S(1)}, u32[]{:S(2)}, u32[]{:S(2)}) %all-to-all-start.3) | async-done | bytes 1179680 | tf_op jit(solution)/shard_map/all_to_all | solution.py:43
  179.7 2.9 %shard_map.85 = (bf16[32,8,1024]{2,1,0:T(8,128)(2,1)}, f32[32,8,128]{2,1,0:T(8,128)S(1)}) custom-call(s32[64]{0:T(128)S(1)} %get-tuple-element.25.slots_ref, bf16[32,8,1024]{2,1,0:T(8,128)(2,1)S(1)} %get-tuple-element.35.blocks_ref, bf16[64,8,1152]{2,1,0:T(8,128)(2,1)S(1)} %all-to-all-done.3.returned_ref), custom_call_target="tpu_custom_call" | custom-call | tf_op jit(solution)/shard_map/pallas_call | solution.py:266
  182.6 0.1 slice_reduce_fusion
  182.8 0.6 pad_maximum_fusion
  (19 shorter events, 0.3 us)
Async XLA Ops:
  0.6 13.4 %copy-start = (bf16[1,1024,1024]{2,1,0:T(8,128)(2,1)S(1)}, bf16[1,1024,1024]{2,1,0:T(8,128)(2,1)}, u32[]{:S(2)}) copy-start(bf16[1,1024,1024]{2,1,0:T(8,128)(2,1)} %param.7) | copy-start | bytes 6291460
  0.6 40.6 %collective-permute-start.3 = (bf16[1024,1024]{1,0:T(8,128)(2,1)}, bf16[1024,1024]{1,0:T(8,128)(2,1)}, u32[]{:S(2)}, u32[]{:S(2)}) collective-permute-start(bf16[1024,1024]{1,0:T(8,128)(2,1)} %bitcast.4), channel_id=1, source_target_pairs={{0,16},{1,17},{2,18},{3,19},{4,20},{5,21},{6,22},{7,23},{8,24},{9,... | collective-permute-start | bytes 6291464 | tf_op jit(solution)/shard_map/ppermute | solution.py:64
  2.4 1.0 copy-start.1
  3.5 0.7 copy-start.4
  5.9 1.0 copy-start.3
  6.9 25.5 %all-to-all-start = ((bf16[64,8,1152]{2,1,0:T(8,128)(2,1)}), bf16[64,8,1152]{2,1,0:T(8,128)(2,1)S(1)}, u32[]{:S(2)}, u32[]{:S(2)}) async-start(bf16[64,8,1152]{2,1,0:T(8,128)(2,1)} %copy-done.3), calls=%async_computation | async-start | bytes 2359296 | tf_op jit(solution)/shard_map/all_to_all | solution.py:43
  34.7 10.4 %collective-permute-start = (bf16[16,8,1024]{2,1,0:T(8,128)(2,1)S(1)}, bf16[16,8,1024]{2,1,0:T(8,128)(2,1)S(1)}, u32[]{:S(2)}, u32[]{:S(2)}) collective-permute-start(bf16[16,8,1024]{2,1,0:T(8,128)(2,1)S(1)} %get-tuple-element.28), channel_id=1, source_target_pairs={{0,32},{1,33},{2,34},{3,35},{4,36},{5,37},{6,38},{7,39},{8,40},{9,... | collective-permute-start | bytes 786440 | tf_op jit(solution)/shard_map/ppermute | solution.py:56
  36.7 14.8 %collective-permute-start.1 = (bf16[16,8,1024]{2,1,0:T(8,128)(2,1)S(1)}, bf16[16,8,1024]{2,1,0:T(8,128)(2,1)S(1)}, u32[]{:S(2)}, u32[]{:S(2)}) collective-permute-start(bf16[16,8,1024]{2,1,0:T(8,128)(2,1)S(1)} %get-tuple-element.29), channel_id=1, source_target_pairs={{0,64},{1,65},{2,66},{3,67},{4,68},{5,69},{6,70},{7,71},{8,72},{9,... | collective-permute-start | bytes 786440 | tf_op jit(solution)/shard_map/ppermute | solution.py:56
  40.2 11.2 %collective-permute-start.2 = (bf16[16,8,1024]{2,1,0:T(8,128)(2,1)S(1)}, bf16[16,8,1024]{2,1,0:T(8,128)(2,1)S(1)}, u32[]{:S(2)}, u32[]{:S(2)}) collective-permute-start(bf16[16,8,1024]{2,1,0:T(8,128)(2,1)S(1)} %get-tuple-element.30), channel_id=1, source_target_pairs={{0,96},{1,97},{2,98},{3,99},{4,100},{5,101},{6,102},{7,103},{8,104... | collective-permute-start | bytes 786440 | tf_op jit(solution)/shard_map/ppermute | solution.py:56
  55.9 15.0 %collective-permute-start.4 = (bf16[16,8,1152]{2,1,0:T(8,128)(2,1)S(1)}, bf16[16,8,1152]{2,1,0:T(8,128)(2,1)S(1)}, u32[]{:S(2)}, u32[]{:S(2)}) collective-permute-start(bf16[16,8,1152]{2,1,0:T(8,128)(2,1)S(1)} %get-tuple-element.32), channel_id=1, source_target_pairs={{0,96},{1,97},{2,98},{3,99},{4,100},{5,101},{6,102},{7,103},{8,104... | collective-permute-start | bytes 884744 | tf_op jit(solution)/shard_map/ppermute | solution.py:56
  58.1 12.8 %collective-permute-start.5 = (bf16[16,8,1152]{2,1,0:T(8,128)(2,1)S(1)}, bf16[16,8,1152]{2,1,0:T(8,128)(2,1)S(1)}, u32[]{:S(2)}, u32[]{:S(2)}) collective-permute-start(bf16[16,8,1152]{2,1,0:T(8,128)(2,1)S(1)} %get-tuple-element.33), channel_id=1, source_target_pairs={{0,64},{1,65},{2,66},{3,67},{4,68},{5,69},{6,70},{7,71},{8,72},{9,... | collective-permute-start | bytes 884744 | tf_op jit(solution)/shard_map/ppermute | solution.py:56
  59.2 15.3 %collective-permute-start.6 = (bf16[16,8,1152]{2,1,0:T(8,128)(2,1)S(1)}, bf16[16,8,1152]{2,1,0:T(8,128)(2,1)S(1)}, u32[]{:S(2)}, u32[]{:S(2)}) collective-permute-start(bf16[16,8,1152]{2,1,0:T(8,128)(2,1)S(1)} %get-tuple-element.34), channel_id=1, source_target_pairs={{0,32},{1,33},{2,34},{3,35},{4,36},{5,37},{6,38},{7,39},{8,40},{9,... | collective-permute-start | bytes 884744 | tf_op jit(solution)/shard_map/ppermute | solution.py:56
  74.6 24.6 %copy-start.2 = (bf16[32,8,1024]{2,1,0:T(8,128)(2,1)S(1)}, bf16[32,8,1024]{2,1,0:T(8,128)(2,1)}, u32[]{:S(2)}) copy-start(bf16[32,8,1024]{2,1,0:T(8,128)(2,1)} %blocks_ref.3) | copy-start | bytes 1572868
  120.7 12.6 %collective-permute-start.7 = (bf16[16,8,1024]{2,1,0:T(8,128)(2,1)S(1)}, bf16[16,8,1024]{2,1,0:T(8,128)(2,1)S(1)}, u32[]{:S(2)}, u32[]{:S(2)}) collective-permute-start(bf16[16,8,1024]{2,1,0:T(8,128)(2,1)S(1)} %get-tuple-element.38), channel_id=1, source_target_pairs={{0,32},{1,33},{2,34},{3,35},{4,36},{5,37},{6,38},{7,39},{8,40},{9,... | collective-permute-start | bytes 786440 | tf_op jit(solution)/shard_map/ppermute | solution.py:56
  120.7 12.6 %collective-permute-start.8 = (bf16[16,8,1024]{2,1,0:T(8,128)(2,1)S(1)}, bf16[16,8,1024]{2,1,0:T(8,128)(2,1)S(1)}, u32[]{:S(2)}, u32[]{:S(2)}) collective-permute-start(bf16[16,8,1024]{2,1,0:T(8,128)(2,1)S(1)} %get-tuple-element.39), channel_id=1, source_target_pairs={{0,64},{1,65},{2,66},{3,67},{4,68},{5,69},{6,70},{7,71},{8,72},{9,... | collective-permute-start | bytes 786440 | tf_op jit(solution)/shard_map/ppermute | solution.py:56
  121.6 12.3 %collective-permute-start.9 = (bf16[16,8,1024]{2,1,0:T(8,128)(2,1)S(1)}, bf16[16,8,1024]{2,1,0:T(8,128)(2,1)S(1)}, u32[]{:S(2)}, u32[]{:S(2)}) collective-permute-start(bf16[16,8,1024]{2,1,0:T(8,128)(2,1)S(1)} %get-tuple-element.40), channel_id=1, source_target_pairs={{0,96},{1,97},{2,98},{3,99},{4,100},{5,101},{6,102},{7,103},{8,104... | collective-permute-start | bytes 786440 | tf_op jit(solution)/shard_map/ppermute | solution.py:56
  138.4 14.1 %collective-permute-start.10 = (bf16[16,8,1152]{2,1,0:T(8,128)(2,1)S(1)}, bf16[16,8,1152]{2,1,0:T(8,128)(2,1)S(1)}, u32[]{:S(2)}, u32[]{:S(2)}) collective-permute-start(bf16[16,8,1152]{2,1,0:T(8,128)(2,1)S(1)} %get-tuple-element.42), channel_id=1, source_target_pairs={{0,96},{1,97},{2,98},{3,99},{4,100},{5,101},{6,102},{7,103},{8,104... | collective-permute-start | bytes 884744 | tf_op jit(solution)/shard_map/ppermute | solution.py:56
  140.8 11.7 %collective-permute-start.11 = (bf16[16,8,1152]{2,1,0:T(8,128)(2,1)S(1)}, bf16[16,8,1152]{2,1,0:T(8,128)(2,1)S(1)}, u32[]{:S(2)}, u32[]{:S(2)}) collective-permute-start(bf16[16,8,1152]{2,1,0:T(8,128)(2,1)S(1)} %get-tuple-element.43), channel_id=1, source_target_pairs={{0,64},{1,65},{2,66},{3,67},{4,68},{5,69},{6,70},{7,71},{8,72},{9,... | collective-permute-start | bytes 884744 | tf_op jit(solution)/shard_map/ppermute | solution.py:56
  140.8 15.1 %collective-permute-start.12 = (bf16[16,8,1152]{2,1,0:T(8,128)(2,1)S(1)}, bf16[16,8,1152]{2,1,0:T(8,128)(2,1)S(1)}, u32[]{:S(2)}, u32[]{:S(2)}) collective-permute-start(bf16[16,8,1152]{2,1,0:T(8,128)(2,1)S(1)} %get-tuple-element.44), channel_id=1, source_target_pairs={{0,32},{1,33},{2,34},{3,35},{4,36},{5,37},{6,38},{7,39},{8,40},{9,... | collective-permute-start | bytes 884744 | tf_op jit(solution)/shard_map/ppermute | solution.py:56
  157.7 22.0 %all-to-all-start.3 = ((bf16[64,8,1152]{2,1,0:T(8,128)(2,1)}), bf16[64,8,1152]{2,1,0:T(8,128)(2,1)S(1)}, u32[]{:S(2)}, u32[]{:S(2)}) async-start(bf16[64,8,1152]{2,1,0:T(8,128)(2,1)} %shard_map.84), calls=%async_computation.3 | async-start | bytes 2359296 | tf_op jit(solution)/shard_map/all_to_all | solution.py:43

commit v3 on v2

--- a/solution.py
+++ b/solution.py
@@ -18,6 +18,7 @@
 DEPTH = 4
 SLABS = SIDE * SIDE
 CLUSTER_DEVICES = DEPTH * CORES
+SHIFTS = (0, 1, 3, 2)
 
 
 def slab_order(core):
@@ -30,13 +31,6 @@
         [cluster * SLABS + slab for slab in slab_order(cluster % CORES)]
         for cluster in range(CLUSTER_DEVICES)
     ]
-
-
-def slab_places(core):
-    places = [0] * SLABS
-    for place, slab in enumerate(slab_order(core)):
-        places[slab] = place
-    return places
 
 
 def exchange_slabs(array):
@@ -75,7 +69,14 @@
     return pltpu.CompilerParams(vmem_limit_bytes=VMEM_LIMIT)
 
 
-def fill_kernel(pairs_ref, table_ref, places_ref, blocks_ref, out_ref, slots_ref, counts_ref):
+def slab_place(slab, core):
+    x, y = lax.div(slab, SIDE), lax.rem(slab, SIDE)
+    first, second = jnp.where(core == 0, x, y), jnp.where(core == 0, y, x)
+    return lax.rem(second - first + SIDE, SIDE) * SIDE + first
+
+
+def fill_kernel(pairs_ref, table_ref, blocks_ref, out_ref, slots_ref, counts_ref):
+    core = lax.rem(lax.axis_index("cluster").astype(jnp.int32), CORES)
     count, rows, features = blocks_ref.shape
     per_slab = 2 * count // SLABS
 
@@ -88,13 +89,12 @@
     def body(block, carry):
         values = blocks_ref[block]
         for side in range(2):
-            message = 2 * block + side
-            entry = table_ref[pairs_ref[message]]
-            place = places_ref[lax.rem(entry, SLABS)]
+            entry = table_ref[pairs_ref[side, block]]
+            place = slab_place(lax.rem(entry, SLABS), core)
             rank = counts_ref[place]
             counts_ref[place] = rank + 1
             slot = place * per_slab + rank
-            slots_ref[message] = slot
+            slots_ref[2 * block + side] = slot
             out_ref[slot, :, :features] = values
             target = lax.div(entry, SLABS).astype(jnp.float32)
             out_ref[slot, :, features:] = jnp.full((rows, LANES), target, jnp.float32).astype(
@@ -105,7 +105,7 @@
     lax.fori_loop(0, count, body, 0, unroll=4)
 
 
-def fill(blocks, pairs, table, places):
+def fill(blocks, pairs, table):
     count, rows, features = blocks.shape
     return pl.pallas_call(
         fill_kernel,
@@ -113,19 +113,19 @@
             jax.ShapeDtypeStruct((2 * count, rows, features + LANES), jnp.bfloat16),
             jax.ShapeDtypeStruct((2 * count,), jnp.int32),
         ],
-        in_specs=[SMEM, SMEM, SMEM, VMEM],
+        in_specs=[SMEM, SMEM, VMEM],
         out_specs=[VMEM, SMEM],
         scratch_shapes=[pltpu.SMEM((SLABS,), jnp.int32)],
         compiler_params=params(),
-    )(pairs, table, places, blocks)
+    )(pairs, table, blocks)
 
 
 def sort_kernel(origin_ref, arrived_ref, *out_refs):
     size, _, features = out_refs[0].shape
-    for shift, out_ref in enumerate(out_refs):
-
-        def body(index, carry, shift=shift, out_ref=out_ref):
-            out_ref[index] = arrived_ref[origin_ref[shift * size + index], :, :features]
+    for place, out_ref in enumerate(out_refs):
+
+        def body(index, carry, place=place, out_ref=out_ref):
+            out_ref[index] = arrived_ref[origin_ref[place * size + index], :, :features]
             return carry
 
         lax.fori_loop(0, size, body, 0, unroll=4)
@@ -146,10 +146,10 @@
 def unsort_kernel(origin_ref, *refs):
     part_refs, out_ref = refs[:-1], refs[-1]
     size = part_refs[0].shape[0]
-    for shift, part_ref in enumerate(part_refs):
-
-        def body(index, carry, shift=shift, part_ref=part_ref):
-            out_ref[origin_ref[shift * size + index]] = part_ref[index]
+    for place, part_ref in enumerate(part_refs):
+
+        def body(index, carry, place=place, part_ref=part_ref):
+            out_ref[origin_ref[place * size + index]] = part_ref[index]
             return carry
 
         lax.fori_loop(0, size, body, 0, unroll=4)
@@ -185,8 +185,8 @@
     return summed * (1.0 / totals), terms
 
 
-def score_kernel(*refs):
-    part_refs, refs = refs[:DEPTH], refs[DEPTH:]
+def score_kernel(count, *refs):
+    part_refs, refs = refs[:count], refs[count:]
     cluster_refs, norm_refs, out_refs = refs[:CORES], refs[CORES : 2 * CORES], refs[2 * CORES :]
     size, rows, features = part_refs[0].shape
     half = size // CORES
@@ -199,8 +199,8 @@
             ]
         ).astype(jnp.bfloat16)
         part, terms = score(flat, cluster_refs[side][...], norm_refs[side][...])
-        for shift, out_ref in enumerate(out_refs):
-            lines = slice(shift * half * rows, (shift + 1) * half * rows)
+        for place, out_ref in enumerate(out_refs):
+            lines = slice(place * half * rows, (place + 1) * half * rows)
             out_ref[span, :, :features] = (
                 part[lines].reshape(half, rows, features).astype(jnp.bfloat16)
             )
@@ -210,14 +210,22 @@
 
 
 def score_parts(parts, clusters, norms):
+    count = len(parts)
     size, rows, features = parts[0].shape
+    references = clusters[0].shape[0]
+    total = count * size * rows
     out = jax.ShapeDtypeStruct((size, rows, features + LANES), jnp.bfloat16)
     return pl.pallas_call(
-        score_kernel,
-        out_shape=[out] * DEPTH,
-        in_specs=[VMEM] * (DEPTH + 2 * CORES),
-        out_specs=[VMEM] * DEPTH,
-        compiler_params=params(),
+        functools.partial(score_kernel, count),
+        out_shape=[out] * count,
+        in_specs=[VMEM] * (count + 2 * CORES),
+        out_specs=[VMEM] * count,
+        compiler_params=params(),
+        cost_estimate=pl.CostEstimate(
+            flops=4 * total * references * features,
+            bytes_accessed=2 * (2 * total * features + CORES * references * features),
+            transcendentals=total * references,
+        ),
     )(*parts, *clusters, *norms)
 
 
@@ -229,7 +237,7 @@
         terms = part[:, features:]
         return part[:, :features], terms[:, 0:1] + terms[:, 1:2] + terms[:, 2:3]
 
-    def body(block, carry):
+    def body(block, densities):
         first_slot, second_slot = slots_ref[2 * block], slots_ref[2 * block + 1]
         first_part, first_log = read(first_slot)
         second_part, second_log = read(second_slot)
@@ -245,21 +253,23 @@
             jnp.square(blocks_ref[block].astype(jnp.float32)), axis=1, keepdims=True
         )
         density = both_top + jnp.log(pair_total) - 0.5 * INV_WIDTH * squares - log_count
-        density_ref[block] = jnp.broadcast_to(density, density_ref.shape[1:])
         mixed_ref[block] = mixed
         for send_ref in send_refs:
             send_ref[first_slot] = mixed
             send_ref[second_slot] = mixed
-        return carry
-
-    lax.fori_loop(0, blocks_ref.shape[0], body, 0, unroll=4)
+        return jnp.where(lane == block, density, densities)
+
+    lane = lax.broadcasted_iota(jnp.int32, density_ref.shape, 1)
+    density_ref[...] = lax.fori_loop(
+        0, blocks_ref.shape[0], body, jnp.zeros(density_ref.shape, jnp.float32), unroll=4
+    )
 
 
 def combine(blocks, returned, slots, log_count, send):
     count, rows, features = blocks.shape
     outs = [
         jax.ShapeDtypeStruct(blocks.shape, jnp.bfloat16),
-        jax.ShapeDtypeStruct((count, rows, LANES), jnp.float32),
+        jax.ShapeDtypeStruct((rows, LANES), jnp.float32),
     ]
     if send:
         outs.append(jax.ShapeDtypeStruct((2 * count, rows, features), jnp.bfloat16))
@@ -284,8 +294,9 @@
     earlier = (targets[:, None] == targets[None, :]) & (order[None, :] < order[:, None])
     rank = jnp.sum(earlier.astype(jnp.int32), axis=1)
     shift = (targets // CORES - depth) % DEPTH
+    place = shift ^ (shift >> 1)
     side = (targets % CORES) ^ core
-    slot = (shift * CORES + side) * per_cluster + rank
+    slot = (place * CORES + side) * per_cluster + rank
     return jnp.sum(jnp.where(slot[None, :] == order[:, None], order[None, :], 0), axis=1)
 
 
@@ -293,18 +304,13 @@
     features = queries.shape[2]
     cluster_index = lax.axis_index("cluster").astype(jnp.int32)
     depth, core = cluster_index // CORES, cluster_index % CORES
-    places = jnp.where(
-        core == 0,
-        jnp.array(slab_places(0), jnp.int32),
-        jnp.array(slab_places(1), jnp.int32),
-    )
     own = corpus[0]
     other = swap_cores(own)
     clusters = (own, other)
     norms = (half_norms_of(own), half_norms_of(other))
     log_count = math.log(2.0 * own.shape[0])
     current = queries
-    outgoing, slots = fill(current, block_pairs.reshape(-1), owner_table, places)
+    outgoing, slots = fill(current, block_pairs.T, owner_table)
     origin = None
     densities = []
     for step in range(STEPS):
@@ -312,15 +318,17 @@
         if step == 0:
             origin = sorted_origins(arrived, features, depth, core)
         parts = sort_by_depth(arrived, origin, features)
-        parts = [parts[0]] + [shift_depth(parts[k], k) for k in range(1, DEPTH)]
-        answers = score_parts(parts, clusters, norms)
-        answers = [answers[0]] + [shift_depth(answers[k], -k) for k in range(1, DEPTH)]
+        parts = [parts[0]] + [shift_depth(p, k) for p, k in zip(parts[1:], SHIFTS[1:])]
+        answers = score_parts(parts[:-1], clusters, norms)
+        last, _ = lax.optimization_barrier((parts[-1], answers[0]))
+        answers += score_parts([last], clusters, norms)
+        answers = [answers[0]] + [shift_depth(a, -k) for a, k in zip(answers[1:], SHIFTS[1:])]
         returned = exchange_slabs(unsort(answers, origin))
         current, density, *outgoing = combine(
             current, returned, slots, log_count, step < STEPS - 1
         )
         outgoing = outgoing[0] if outgoing else None
-        densities.append(density[:, :, 0].reshape(-1))
+        densities.append(density[:, : queries.shape[0]].T.reshape(-1))
     return (current, jnp.stack(densities))
 
 

time: 184 us -> 176 us (0.957)
  waiting for transfers between devices: 82.4 us -> 60.6 us
  Pallas kernels: 19.5 us -> 28.1 us
  starting transfers between devices: 28.7 us -> 32.7 us
    ppermute x12, waiting for transfers between devices: 47 us -> 30.1 us  [shift_depth(): return lax.ppermute(array, AXES, pairs)]
    pallas_call x2 -> x4, Pallas kernels: 8.84 us -> 17 us  [score_parts(): pl.pallas_call(functools.partial(score_kernel, count), out_shape=[out] *...]
    all_to_all x2, waiting for transfers between devices: 35.4 us -> 30.5 us  [exchange_slabs(): lax.all_to_all(array, AXES, split_axis=0, concat_axis=0, tiled=True, axis...]
    ppermute x12, starting transfers between devices: 17.2 us -> 21.4 us  [shift_depth(): return lax.ppermute(array, AXES, pairs)]
    all_to_all x2, blocking collectives: 42.6 us -> 44.4 us  [exchange_slabs(): lax.all_to_all(array, AXES, split_axis=0, concat_axis=0, tiled=True, axis...]
  transfers between devices with their start and end apart: 15 -> 15, of which waited for: 10 -> 11; matrix products, arithmetic and copies ran while one was open for 3% -> 2% of each run, Pallas kernels for 1% -> 7%
where the time goes in v3:
time: 176 us; the launch traced here: 175 us
  waiting for transfers between devices  60.6 us (34%)
  blocking collectives  44.4 us (25%)
  starting transfers between devices  32.7 us (19%)
  Pallas kernels  28.1 us (16%)
  other arithmetic  4.69 us (3%)
  local copies, waits for them, and re-layouts  3.85 us (2%)
    all_to_all x2, blocking collectives, exchange_slabs(): lax.all_to_all(array, AXES, split_axis=0, concat_axis=0, tiled=True, axis...  44.4 us
    all_to_all x2, waiting for transfers between devices, exchange_slabs(): lax.all_to_all(array, AXES, split_axis=0, concat_axis=0, tiled=True, axis...  30.5 us
    ppermute x12, waiting for transfers between devices, shift_depth(): return lax.ppermute(array, AXES, pairs)  30.1 us
    ppermute x12, starting transfers between devices, shift_depth(): return lax.ppermute(array, AXES, pairs)  21.4 us
    pallas_call x4, Pallas kernels, score_parts(): pl.pallas_call(functools.partial(score_kernel, count), out_shape=[out] *...  17 us
    all_to_all x2, starting transfers between devices, exchange_slabs(): lax.all_to_all(array, AXES, split_axis=0, concat_axis=0, tiled=True, axis...  11.2 us
    pallas_call x2, Pallas kernels, combine(): pl.pallas_call(functools.partial(combine_kernel, log_count), out_shape=ou...  4.94 us
  transfers between devices with their start and end apart: 15, of which 11 were waited for; matrix products, arithmetic and copies ran while one was open for 2% of the time, Pallas kernels for 7%

profile of v3, /device:TPU:0, one launch (start us, length us, event | category | flops | bytes accessed | tf_op | source)
XLA Modules:
  0.0 175.1 jit_solution(9582015871261929403)
XLA Ops:
  0.7 1.2 copy-done.1
  1.9 0.7 copy-done.4
  2.6 0.7 copy-done.5
  3.2 2.2 %shard_map.59 = (bf16[64,8,1152]{2,1,0:T(8,128)(2,1)S(1)}, s32[64]{0:T(128)S(1)}) custom-call(s32[2,32]{1,0:T(2,128)S(1)} %bitcast.22, s32[128]{0:T(128)S(1)} %copy-done.5, bf16[32,8,1024]{2,1,0:T(8,128)(2,1)S(1)} %copy-done.1), custom_call_target="tpu_custom_call" | custom-call | tf_op jit(solution)/shard_map/pallas_call | solution.py:110
  5.4 1.0 copy-done.3
  6.4 7.1 %all-to-all-start = ((bf16[64,8,1152]{2,1,0:T(8,128)(2,1)}), bf16[64,8,1152]{2,1,0:T(8,128)(2,1)S(1)}, u32[]{:S(2)}, u32[]{:S(2)}) async-start(bf16[64,8,1152]{2,1,0:T(8,128)(2,1)} %copy-done.3), calls=%async_computation | async-start | bytes 2359296 | tf_op jit(solution)/shard_map/all_to_all | solution.py:37
  13.6 0.5 multiply_reduce_fusion.1
  14.1 17.8 %all-to-all-done.arrived_ref = bf16[64,8,1152]{2,1,0:T(8,128)(2,1)S(1)} async-done(((bf16[64,8,1152]{2,1,0:T(8,128)(2,1)}), bf16[64,8,1152]{2,1,0:T(8,128)(2,1)S(1)}, u32[]{:S(2)}, u32[]{:S(2)}) %all-to-all-start) | async-done | bytes 1179680 | tf_op jit(solution)/shard_map/all_to_all | solution.py:37
  31.9 1.2 fusion
  33.2 0.2 convert_reduce_fusion
  33.4 0.1 select_reduce_fusion.origin_ref
  33.5 0.7 shard_map.60
  34.2 2.0 %collective-permute-start = (bf16[16,8,1024]{2,1,0:T(8,128)(2,1)S(1)}, bf16[16,8,1024]{2,1,0:T(8,128)(2,1)S(1)}, u32[]{:S(2)}, u32[]{:S(2)}) collective-permute-start(bf16[16,8,1024]{2,1,0:T(8,128)(2,1)S(1)} %get-tuple-element.28), channel_id=1, source_target_pairs={{0,32},{1,33},{2,34},{3,35},{4,36},{5,37},{6,38},{7,39},{8,40},{9,... | collective-permute-start | bytes 786440 | tf_op jit(solution)/shard_map/ppermute | solution.py:50
  36.2 2.2 %collective-permute-start.1 = (bf16[16,8,1024]{2,1,0:T(8,128)(2,1)S(1)}, bf16[16,8,1024]{2,1,0:T(8,128)(2,1)S(1)}, u32[]{:S(2)}, u32[]{:S(2)}) collective-permute-start(bf16[16,8,1024]{2,1,0:T(8,128)(2,1)S(1)} %get-tuple-element.29), channel_id=1, source_target_pairs={{0,96},{1,97},{2,98},{3,99},{4,100},{5,101},{6,102},{7,103},{8,104... | collective-permute-start | bytes 786440 | tf_op jit(solution)/shard_map/ppermute | solution.py:50
  38.4 1.8 %collective-permute-start.5 = (bf16[16,8,1024]{2,1,0:T(8,128)(2,1)S(1)}, bf16[16,8,1024]{2,1,0:T(8,128)(2,1)S(1)}, u32[]{:S(2)}, u32[]{:S(2)}) collective-permute-start(bf16[16,8,1024]{2,1,0:T(8,128)(2,1)S(1)} %get-tuple-element.33), channel_id=1, source_target_pairs={{0,64},{1,65},{2,66},{3,67},{4,68},{5,69},{6,70},{7,71},{8,72},{9,... | collective-permute-start | bytes 786440 | tf_op jit(solution)/shard_map/ppermute | solution.py:50
  40.2 2.1 %multiply_reduce_fusion = f32[1024]{0:T(1024)S(1)} fusion(bf16[1024,1024]{1,0:T(8,128)(2,1)} %collective-permute-done.2.refs_4_.refs_2_), kind=kLoop, calls=%fused_computation | loop fusion | flops 3144704 | bytes 2101248 | tf_op jit(solution)/shard_map/reduce_sum | solution.py:286
  42.3 2.4 %collective-permute-done.refs_1_ = bf16[16,8,1024]{2,1,0:T(8,128)(2,1)S(1)} collective-permute-done((bf16[16,8,1024]{2,1,0:T(8,128)(2,1)S(1)}, bf16[16,8,1024]{2,1,0:T(8,128)(2,1)S(1)}, u32[]{:S(2)}, u32[]{:S(2)}) %collective-permute-start) | collective-permute-done | bytes 262176 | tf_op jit(solution)/shard_map/ppermute | solution.py:50
  44.7 4.5 %collective-permute-done.1.refs_2_ = bf16[16,8,1024]{2,1,0:T(8,128)(2,1)S(1)} collective-permute-done((bf16[16,8,1024]{2,1,0:T(8,128)(2,1)S(1)}, bf16[16,8,1024]{2,1,0:T(8,128)(2,1)S(1)}, u32[]{:S(2)}, u32[]{:S(2)}) %collective-permute-start.1) | collective-permute-done | bytes 262176 | tf_op jit(solution)/shard_map/ppermute | solution.py:50
  49.2 4.4 %shard_map.61 = (bf16[16,8,1152]{2,1,0:T(8,128)(2,1)S(1)}, bf16[16,8,1152]{2,1,0:T(8,128)(2,1)S(1)}, bf16[16,8,1152]{2,1,0:T(8,128)(2,1)S(1)}) custom-call(bf16[16,8,1024]{2,1,0:T(8,128)(2,1)S(1)} %get-tuple-element.27.refs_0_, bf16[16,8,1024]{2,1,0:T(8,128)(2,1)S(1)} %collective-permute-done.refs_1_, ...), custom_call_target="tpu_custom_call" | custom-call | flops 1610612736 | bytes 5767168 | tf_op jit(solution)/shard_map/pallas_call | solution.py:218
  53.6 4.1 %shard_map.62 = bf16[16,8,1152]{2,1,0:T(8,128)(2,1)S(1)} custom-call(bf16[16,8,1024]{2,1,0:T(8,128)(2,1)S(1)} %collective-permute-done.5.refs_0_, bf16[1024,1024]{1,0:T(8,128)(2,1)S(1)} %bitcast.11, bf16[1024,1024]{1,0:T(8,128)(2,1)} %collective-permute-done.2.refs_4_.refs_2_, f32[1,1024]{1,0:T(1,128)S(1)} %bitcast.15, f32[1,1024]{1,0:T(1,128)S(1)} %bitcast.19), custom_call_target="tpu_custom_call" | custom-call | flops 536870912 | bytes 4718592 | tf_op jit(solution)/shard_map/pallas_call | solution.py:218
  57.7 2.3 %collective-permute-start.6 = (bf16[16,8,1152]{2,1,0:T(8,128)(2,1)S(1)}, bf16[16,8,1152]{2,1,0:T(8,128)(2,1)S(1)}, u32[]{:S(2)}, u32[]{:S(2)}) collective-permute-start(bf16[16,8,1152]{2,1,0:T(8,128)(2,1)S(1)} %shard_map.62), channel_id=1, source_target_pairs={{0,64},{1,65},{2,66},{3,67},{4,68},{5,69},{6,70},{7,71},{8,72},{9,... | collective-permute-start | bytes 884744 | tf_op jit(solution)/shard_map/ppermute | solution.py:50
  60.0 1.5 collective-permute-start.3
  61.5 0.8 collective-permute-start.4
  62.3 5.0 %collective-permute-done.6.refs_3_ = bf16[16,8,1152]{2,1,0:T(8,128)(2,1)S(1)} collective-permute-done((bf16[16,8,1152]{2,1,0:T(8,128)(2,1)S(1)}, bf16[16,8,1152]{2,1,0:T(8,128)(2,1)S(1)}, u32[]{:S(2)}, u32[]{:S(2)}) %collective-permute-start.6) | collective-permute-done | bytes 294944 | tf_op jit(solution)/shard_map/ppermute | solution.py:50
  67.3 2.9 %collective-permute-done.3.refs_1_ = bf16[16,8,1152]{2,1,0:T(8,128)(2,1)S(1)} collective-permute-done((bf16[16,8,1152]{2,1,0:T(8,128)(2,1)S(1)}, bf16[16,8,1152]{2,1,0:T(8,128)(2,1)S(1)}, u32[]{:S(2)}, u32[]{:S(2)}) %collective-permute-start.3) | collective-permute-done | bytes 294944 | tf_op jit(solution)/shard_map/ppermute | solution.py:50
  70.2 0.2 collective-permute-done.4.refs_2_
  70.3 0.7 shard_map.63
  71.1 27.1 %all_to_all.20.returned_ref = bf16[64,8,1152]{2,1,0:T(8,128)(2,1)S(1)} all-to-all(bf16[64,8,1152]{2,1,0:T(8,128)(2,1)S(1)} %shard_map.63), channel_id=1, replica_groups={{0,5,10,15,1,6,11,12,2,7,8,13,3,4,9,14},{16,21,26,31,20,25,30,19,24,29,..., dimensions={0} | all-to-all | bytes 2359296 | tf_op jit(solution)/shard_map/all_to_all | solution.py:37
  98.2 2.1 %shard_map.64 = (bf16[32,8,1024]{2,1,0:T(8,128)(2,1)S(1)}, f32[8,128]{1,0:T(8,128)S(1)}, bf16[64,8,1024]{2,1,0:T(8,128)(2,1)S(1)}) custom-call(s32[64]{0:T(128)S(1)} %get-tuple-element.25.slots_ref, bf16[32,8,1024]{2,1,0:T(8,128)(2,1)S(1)} %copy-done.2, bf16[64,8,1152]{2,1,0:T(8,128)(2,1)S(1)} %all_to_all.20.returned_ref), custom_call_target="tpu_custom_call" | custom-call | tf_op jit(solution)/shard_map/pallas_call | solution.py:276
  100.3 17.3 %all_to_all.21.arrived_ref = bf16[64,8,1024]{2,1,0:T(8,128)(2,1)S(1)} all-to-all(bf16[64,8,1024]{2,1,0:T(8,128)(2,1)S(1)} %get-tuple-element.36), channel_id=1, replica_groups={{0,5,10,15,1,6,11,12,2,7,8,13,3,4,9,14},{16,21,26,31,20,25,30,19,24,29,..., dimensions={0} | all-to-all | bytes 2097152 | tf_op jit(solution)/shard_map/all_to_all | solution.py:37
  117.6 0.7 shard_map.65
  118.3 3.1 %collective-permute-start.7 = (bf16[16,8,1024]{2,1,0:T(8,128)(2,1)S(1)}, bf16[16,8,1024]{2,1,0:T(8,128)(2,1)S(1)}, u32[]{:S(2)}, u32[]{:S(2)}) collective-permute-start(bf16[16,8,1024]{2,1,0:T(8,128)(2,1)S(1)} %get-tuple-element.38), channel_id=1, source_target_pairs={{0,32},{1,33},{2,34},{3,35},{4,36},{5,37},{6,38},{7,39},{8,40},{9,... | collective-permute-start | bytes 786440 | tf_op jit(solution)/shard_map/ppermute | solution.py:50
  121.4 1.8 %collective-permute-start.8 = (bf16[16,8,1024]{2,1,0:T(8,128)(2,1)S(1)}, bf16[16,8,1024]{2,1,0:T(8,128)(2,1)S(1)}, u32[]{:S(2)}, u32[]{:S(2)}) collective-permute-start(bf16[16,8,1024]{2,1,0:T(8,128)(2,1)S(1)} %get-tuple-element.39), channel_id=1, source_target_pairs={{0,96},{1,97},{2,98},{3,99},{4,100},{5,101},{6,102},{7,103},{8,104... | collective-permute-start | bytes 786440 | tf_op jit(solution)/shard_map/ppermute | solution.py:50
  123.2 1.4 collective-permute-start.11
  124.6 5.7 %collective-permute-done.7.refs_1_ = bf16[16,8,1024]{2,1,0:T(8,128)(2,1)S(1)} collective-permute-done((bf16[16,8,1024]{2,1,0:T(8,128)(2,1)S(1)}, bf16[16,8,1024]{2,1,0:T(8,128)(2,1)S(1)}, u32[]{:S(2)}, u32[]{:S(2)}) %collective-permute-start.7) | collective-permute-done | bytes 262176 | tf_op jit(solution)/shard_map/ppermute | solution.py:50
  130.3 1.5 collective-permute-done.8.refs_2_
  131.8 4.4 %shard_map.66 = (bf16[16,8,1152]{2,1,0:T(8,128)(2,1)S(1)}, bf16[16,8,1152]{2,1,0:T(8,128)(2,1)S(1)}, bf16[16,8,1152]{2,1,0:T(8,128)(2,1)S(1)}) custom-call(bf16[16,8,1024]{2,1,0:T(8,128)(2,1)S(1)} %get-tuple-element.37.refs_0_, bf16[16,8,1024]{2,1,0:T(8,128)(2,1)S(1)} %collective-permute-done.7.refs_1_, ...), custom_call_target="tpu_custom_call" | custom-call | flops 1610612736 | bytes 5767168 | tf_op jit(solution)/shard_map/pallas_call | solution.py:218
  136.2 4.1 %shard_map.67 = bf16[16,8,1152]{2,1,0:T(8,128)(2,1)S(1)} custom-call(bf16[16,8,1024]{2,1,0:T(8,128)(2,1)S(1)} %collective-permute-done.11.refs_0_, bf16[1024,1024]{1,0:T(8,128)(2,1)S(1)} %bitcast.13, bf16[1024,1024]{1,0:T(8,128)(2,1)} %collective-permute-done.2.refs_4_.refs_2_, f32[1,1024]{1,0:T(1,128)S(1)} %bitcast.17, f32[1,1024]{1,0:T(1,128)S(1)} %bitcast.21), custom_call_target="tpu_custom_call" | custom-call | flops 536870912 | bytes 4718592 | tf_op jit(solution)/shard_map/pallas_call | solution.py:218
  140.3 0.9 collective-permute-start.12
  141.2 3.0 %collective-permute-start.9 = (bf16[16,8,1152]{2,1,0:T(8,128)(2,1)S(1)}, bf16[16,8,1152]{2,1,0:T(8,128)(2,1)S(1)}, u32[]{:S(2)}, u32[]{:S(2)}) collective-permute-start(bf16[16,8,1152]{2,1,0:T(8,128)(2,1)S(1)} %get-tuple-element.41), channel_id=1, source_target_pairs={{0,96},{1,97},{2,98},{3,99},{4,100},{5,101},{6,102},{7,103},{8,104... | collective-permute-start | bytes 884744 | tf_op jit(solution)/shard_map/ppermute | solution.py:50
  144.1 0.8 collective-permute-start.10
  144.9 3.7 %collective-permute-done.12.refs_3_ = bf16[16,8,1152]{2,1,0:T(8,128)(2,1)S(1)} collective-permute-done((bf16[16,8,1152]{2,1,0:T(8,128)(2,1)S(1)}, bf16[16,8,1152]{2,1,0:T(8,128)(2,1)S(1)}, u32[]{:S(2)}, u32[]{:S(2)}) %collective-permute-start.12) | collective-permute-done | bytes 294944 | tf_op jit(solution)/shard_map/ppermute | solution.py:50
  148.6 4.2 %collective-permute-done.9.refs_1_ = bf16[16,8,1152]{2,1,0:T(8,128)(2,1)S(1)} collective-permute-done((bf16[16,8,1152]{2,1,0:T(8,128)(2,1)S(1)}, bf16[16,8,1152]{2,1,0:T(8,128)(2,1)S(1)}, u32[]{:S(2)}, u32[]{:S(2)}) %collective-permute-start.9) | collective-permute-done | bytes 294944 | tf_op jit(solution)/shard_map/ppermute | solution.py:50
  152.8 1.8 %shard_map.68 = bf16[64,8,1152]{2,1,0:T(8,128)(2,1)} custom-call(s32[64]{0:T(128)S(1)} %select_reduce_fusion.origin_ref, bf16[16,8,1152]{2,1,0:T(8,128)(2,1)S(1)} %get-tuple-element.40.refs_0_, bf16[16,8,1152]{2,1,0:T(8,128)(2,1)S(1)} %collective-permute-done.9.refs_1_, bf16[16,8,1152]{2,1,0:T(8,128)(2,1)S(1)} %collective-permute-done.10.refs_2_, ...), custom_call_target="tpu_custom_call" | custom-call | tf_op jit(solution)/shard_map/pallas_call | solution.py:160
  154.6 4.1 %all-to-all-start.3 = ((bf16[64,8,1152]{2,1,0:T(8,128)(2,1)}), bf16[64,8,1152]{2,1,0:T(8,128)(2,1)S(1)}, u32[]{:S(2)}, u32[]{:S(2)}) async-start(bf16[64,8,1152]{2,1,0:T(8,128)(2,1)} %shard_map.68), calls=%async_computation.3 | async-start | bytes 2359296 | tf_op jit(solution)/shard_map/all_to_all | solution.py:37
  158.9 12.6 %all-to-all-done.3.returned_ref = bf16[64,8,1152]{2,1,0:T(8,128)(2,1)S(1)} async-done(((bf16[64,8,1152]{2,1,0:T(8,128)(2,1)}), bf16[64,8,1152]{2,1,0:T(8,128)(2,1)S(1)}, u32[]{:S(2)}, u32[]{:S(2)}) %all-to-all-start.3) | async-done | bytes 1179680 | tf_op jit(solution)/shard_map/all_to_all | solution.py:37
  171.5 2.9 %shard_map.69 = (bf16[32,8,1024]{2,1,0:T(8,128)(2,1)}, f32[8,128]{1,0:T(8,128)S(1)}) custom-call(s32[64]{0:T(128)S(1)} %get-tuple-element.25.slots_ref, bf16[32,8,1024]{2,1,0:T(8,128)(2,1)S(1)} %get-tuple-element.35.blocks_ref, bf16[64,8,1152]{2,1,0:T(8,128)(2,1)S(1)} %all-to-all-done.3.returned_ref), custom_call_target="tpu_custom_call" | custom-call | tf_op jit(solution)/shard_map/pallas_call | solution.py:276
  174.5 0.6 pad_maximum_fusion
  (22 shorter events, 0.5 us)
Async XLA Ops:
  0.6 13.0 %copy-start = (bf16[1,1024,1024]{2,1,0:T(8,128)(2,1)S(1)}, bf16[1,1024,1024]{2,1,0:T(8,128)(2,1)}, u32[]{:S(2)}) copy-start(bf16[1,1024,1024]{2,1,0:T(8,128)(2,1)} %param.5) | copy-start | bytes 6291460
  0.6 39.6 %collective-permute-start.2 = (bf16[1024,1024]{1,0:T(8,128)(2,1)}, bf16[1024,1024]{1,0:T(8,128)(2,1)}, u32[]{:S(2)}, u32[]{:S(2)}) collective-permute-start(bf16[1024,1024]{1,0:T(8,128)(2,1)} %bitcast.9), channel_id=1, source_target_pairs={{0,16},{1,17},{2,18},{3,19},{4,20},{5,21},{6,22},{7,23},{8,24},{9,... | collective-permute-start | bytes 6291464 | tf_op jit(solution)/shard_map/ppermute | solution.py:58
  0.7 1.2 copy-start.1
  1.9 0.7 copy-start.4
  2.6 0.7 copy-start.5
  5.4 1.0 copy-start.3
  6.4 25.5 %all-to-all-start = ((bf16[64,8,1152]{2,1,0:T(8,128)(2,1)}), bf16[64,8,1152]{2,1,0:T(8,128)(2,1)S(1)}, u32[]{:S(2)}, u32[]{:S(2)}) async-start(bf16[64,8,1152]{2,1,0:T(8,128)(2,1)} %copy-done.3), calls=%async_computation | async-start | bytes 2359296 | tf_op jit(solution)/shard_map/all_to_all | solution.py:37
  34.2 10.4 %collective-permute-start = (bf16[16,8,1024]{2,1,0:T(8,128)(2,1)S(1)}, bf16[16,8,1024]{2,1,0:T(8,128)(2,1)S(1)}, u32[]{:S(2)}, u32[]{:S(2)}) collective-permute-start(bf16[16,8,1024]{2,1,0:T(8,128)(2,1)S(1)} %get-tuple-element.28), channel_id=1, source_target_pairs={{0,32},{1,33},{2,34},{3,35},{4,36},{5,37},{6,38},{7,39},{8,40},{9,... | collective-permute-start | bytes 786440 | tf_op jit(solution)/shard_map/ppermute | solution.py:50
  36.2 13.0 %collective-permute-start.1 = (bf16[16,8,1024]{2,1,0:T(8,128)(2,1)S(1)}, bf16[16,8,1024]{2,1,0:T(8,128)(2,1)S(1)}, u32[]{:S(2)}, u32[]{:S(2)}) collective-permute-start(bf16[16,8,1024]{2,1,0:T(8,128)(2,1)S(1)} %get-tuple-element.29), channel_id=1, source_target_pairs={{0,96},{1,97},{2,98},{3,99},{4,100},{5,101},{6,102},{7,103},{8,104... | collective-permute-start | bytes 786440 | tf_op jit(solution)/shard_map/ppermute | solution.py:50
  38.4 15.2 %collective-permute-start.5 = (bf16[16,8,1024]{2,1,0:T(8,128)(2,1)S(1)}, bf16[16,8,1024]{2,1,0:T(8,128)(2,1)S(1)}, u32[]{:S(2)}, u32[]{:S(2)}) collective-permute-start(bf16[16,8,1024]{2,1,0:T(8,128)(2,1)S(1)} %get-tuple-element.33), channel_id=1, source_target_pairs={{0,64},{1,65},{2,66},{3,67},{4,68},{5,69},{6,70},{7,71},{8,72},{9,... | collective-permute-start | bytes 786440 | tf_op jit(solution)/shard_map/ppermute | solution.py:50
  57.7 9.6 %collective-permute-start.6 = (bf16[16,8,1152]{2,1,0:T(8,128)(2,1)S(1)}, bf16[16,8,1152]{2,1,0:T(8,128)(2,1)S(1)}, u32[]{:S(2)}, u32[]{:S(2)}) collective-permute-start(bf16[16,8,1152]{2,1,0:T(8,128)(2,1)S(1)} %shard_map.62), channel_id=1, source_target_pairs={{0,64},{1,65},{2,66},{3,67},{4,68},{5,69},{6,70},{7,71},{8,72},{9,... | collective-permute-start | bytes 884744 | tf_op jit(solution)/shard_map/ppermute | solution.py:50
  60.0 10.2 %collective-permute-start.3 = (bf16[16,8,1152]{2,1,0:T(8,128)(2,1)S(1)}, bf16[16,8,1152]{2,1,0:T(8,128)(2,1)S(1)}, u32[]{:S(2)}, u32[]{:S(2)}) collective-permute-start(bf16[16,8,1152]{2,1,0:T(8,128)(2,1)S(1)} %get-tuple-element.31), channel_id=1, source_target_pairs={{0,96},{1,97},{2,98},{3,99},{4,100},{5,101},{6,102},{7,103},{8,104... | collective-permute-start | bytes 884744 | tf_op jit(solution)/shard_map/ppermute | solution.py:50
  61.5 36.7 %copy-start.2 = (bf16[32,8,1024]{2,1,0:T(8,128)(2,1)S(1)}, bf16[32,8,1024]{2,1,0:T(8,128)(2,1)}, u32[]{:S(2)}) copy-start(bf16[32,8,1024]{2,1,0:T(8,128)(2,1)} %blocks_ref.3) | copy-start | bytes 1572868
  61.5 8.8 %collective-permute-start.4 = (bf16[16,8,1152]{2,1,0:T(8,128)(2,1)S(1)}, bf16[16,8,1152]{2,1,0:T(8,128)(2,1)S(1)}, u32[]{:S(2)}, u32[]{:S(2)}) collective-permute-start(bf16[16,8,1152]{2,1,0:T(8,128)(2,1)S(1)} %get-tuple-element.32), channel_id=1, source_target_pairs={{0,32},{1,33},{2,34},{3,35},{4,36},{5,37},{6,38},{7,39},{8,40},{9,... | collective-permute-start | bytes 884744 | tf_op jit(solution)/shard_map/ppermute | solution.py:50
  118.3 12.0 %collective-permute-start.7 = (bf16[16,8,1024]{2,1,0:T(8,128)(2,1)S(1)}, bf16[16,8,1024]{2,1,0:T(8,128)(2,1)S(1)}, u32[]{:S(2)}, u32[]{:S(2)}) collective-permute-start(bf16[16,8,1024]{2,1,0:T(8,128)(2,1)S(1)} %get-tuple-element.38), channel_id=1, source_target_pairs={{0,32},{1,33},{2,34},{3,35},{4,36},{5,37},{6,38},{7,39},{8,40},{9,... | collective-permute-start | bytes 786440 | tf_op jit(solution)/shard_map/ppermute | solution.py:50
  121.4 10.4 %collective-permute-start.8 = (bf16[16,8,1024]{2,1,0:T(8,128)(2,1)S(1)}, bf16[16,8,1024]{2,1,0:T(8,128)(2,1)S(1)}, u32[]{:S(2)}, u32[]{:S(2)}) collective-permute-start(bf16[16,8,1024]{2,1,0:T(8,128)(2,1)S(1)} %get-tuple-element.39), channel_id=1, source_target_pairs={{0,96},{1,97},{2,98},{3,99},{4,100},{5,101},{6,102},{7,103},{8,104... | collective-permute-start | bytes 786440 | tf_op jit(solution)/shard_map/ppermute | solution.py:50
  123.2 13.0 %collective-permute-start.11 = (bf16[16,8,1024]{2,1,0:T(8,128)(2,1)S(1)}, bf16[16,8,1024]{2,1,0:T(8,128)(2,1)S(1)}, u32[]{:S(2)}, u32[]{:S(2)}) collective-permute-start(bf16[16,8,1024]{2,1,0:T(8,128)(2,1)S(1)} %get-tuple-element.43), channel_id=1, source_target_pairs={{0,64},{1,65},{2,66},{3,67},{4,68},{5,69},{6,70},{7,71},{8,72},{9,... | collective-permute-start | bytes 786440 | tf_op jit(solution)/shard_map/ppermute | solution.py:50
  140.3 8.3 %collective-permute-start.12 = (bf16[16,8,1152]{2,1,0:T(8,128)(2,1)S(1)}, bf16[16,8,1152]{2,1,0:T(8,128)(2,1)S(1)}, u32[]{:S(2)}, u32[]{:S(2)}) collective-permute-start(bf16[16,8,1152]{2,1,0:T(8,128)(2,1)S(1)} %shard_map.67), channel_id=1, source_target_pairs={{0,64},{1,65},{2,66},{3,67},{4,68},{5,69},{6,70},{7,71},{8,72},{9,... | collective-permute-start | bytes 884744 | tf_op jit(solution)/shard_map/ppermute | solution.py:50
  141.2 11.6 %collective-permute-start.9 = (bf16[16,8,1152]{2,1,0:T(8,128)(2,1)S(1)}, bf16[16,8,1152]{2,1,0:T(8,128)(2,1)S(1)}, u32[]{:S(2)}, u32[]{:S(2)}) collective-permute-start(bf16[16,8,1152]{2,1,0:T(8,128)(2,1)S(1)} %get-tuple-element.41), channel_id=1, source_target_pairs={{0,96},{1,97},{2,98},{3,99},{4,100},{5,101},{6,102},{7,103},{8,104... | collective-permute-start | bytes 884744 | tf_op jit(solution)/shard_map/ppermute | solution.py:50
  144.1 8.7 %collective-permute-start.10 = (bf16[16,8,1152]{2,1,0:T(8,128)(2,1)S(1)}, bf16[16,8,1152]{2,1,0:T(8,128)(2,1)S(1)}, u32[]{:S(2)}, u32[]{:S(2)}) collective-permute-start(bf16[16,8,1152]{2,1,0:T(8,128)(2,1)S(1)} %get-tuple-element.42), channel_id=1, source_target_pairs={{0,32},{1,33},{2,34},{3,35},{4,36},{5,37},{6,38},{7,39},{8,40},{9,... | collective-permute-start | bytes 884744 | tf_op jit(solution)/shard_map/ppermute | solution.py:50
  154.6 16.9 %all-to-all-start.3 = ((bf16[64,8,1152]{2,1,0:T(8,128)(2,1)}), bf16[64,8,1152]{2,1,0:T(8,128)(2,1)S(1)}, u32[]{:S(2)}, u32[]{:S(2)}) async-start(bf16[64,8,1152]{2,1,0:T(8,128)(2,1)} %shard_map.68), calls=%async_computation.3 | async-start | bytes 2359296 | tf_op jit(solution)/shard_map/all_to_all | solution.py:37

commit v4 on v3

--- a/solution.py
+++ b/solution.py
@@ -19,6 +19,7 @@
 SLABS = SIDE * SIDE
 CLUSTER_DEVICES = DEPTH * CORES
 SHIFTS = (0, 1, 3, 2)
+TERM_LANES = 8
 
 
 def slab_order(core):
@@ -75,64 +76,128 @@
     return lax.rem(second - first + SIDE, SIDE) * SIDE + first
 
 
-def fill_kernel(pairs_ref, table_ref, blocks_ref, out_ref, slots_ref, counts_ref):
+def fill_kernel(
+    pairs_hbm, table_hbm, blocks_ref, out_ref, slots_ref,
+    pairs_ref, table_ref, counts_ref, targets_ref, notes_ref, input_sems, copy_sems, note_sem,
+):
+    count, tiles = blocks_ref.shape[:2]
+    per_slab = 2 * count // SLABS
     core = lax.rem(lax.axis_index("cluster").astype(jnp.int32), CORES)
-    count, rows, features = blocks_ref.shape
-    per_slab = 2 * count // SLABS
+    inputs = [
+        pltpu.make_async_copy(pairs_hbm, pairs_ref, input_sems.at[0]),
+        pltpu.make_async_copy(table_hbm, table_ref, input_sems.at[1]),
+    ]
+    for copy in inputs:
+        copy.start()
 
     def clear(place, carry):
         counts_ref[place] = 0
         return carry
 
     lax.fori_loop(0, SLABS, clear, 0)
-
-    def body(block, carry):
-        values = blocks_ref[block]
+    for copy in inputs:
+        copy.wait()
+
+    def message_copy(message, slot):
+        place, rank = lax.div(slot, per_slab), lax.rem(slot, per_slab)
+        return pltpu.make_async_copy(
+            blocks_ref.at[lax.div(message, 2)],
+            out_ref.at[place, pl.ds(rank * tiles, tiles)],
+            copy_sems.at[message],
+        )
+
+    def send(block, carry):
         for side in range(2):
             entry = table_ref[pairs_ref[side, block]]
             place = slab_place(lax.rem(entry, SLABS), core)
             rank = counts_ref[place]
             counts_ref[place] = rank + 1
             slot = place * per_slab + rank
-            slots_ref[2 * block + side] = slot
-            out_ref[slot, :, :features] = values
-            target = lax.div(entry, SLABS).astype(jnp.float32)
-            out_ref[slot, :, features:] = jnp.full((rows, LANES), target, jnp.float32).astype(
-                jnp.bfloat16
-            )
+            message = 2 * block + side
+            slots_ref[message] = slot
+            targets_ref[slot] = lax.div(entry, SLABS)
+            message_copy(message, slot).start()
         return carry
 
-    lax.fori_loop(0, count, body, 0, unroll=4)
+    lax.fori_loop(0, count, send, 0, unroll=2)
+    lane = lax.broadcasted_iota(jnp.int32, notes_ref.shape[1:], 1)
+
+    def note(place, carry):
+        tile = jnp.zeros(notes_ref.shape[1:], jnp.int32)
+        for rank in range(per_slab):
+            tile = jnp.where(lane == rank, targets_ref[place * per_slab + rank], tile)
+        notes_ref[place] = tile.astype(jnp.float32).astype(jnp.bfloat16)
+        return carry
+
+    lax.fori_loop(0, SLABS, note, 0, unroll=2)
+    note_copy = pltpu.make_async_copy(notes_ref, out_ref.at[:, per_slab * tiles], note_sem)
+    note_copy.start()
+
+    def wait(message, carry):
+        message_copy(message, slots_ref[message]).wait()
+        return carry
+
+    lax.fori_loop(0, 2 * count, wait, 0, unroll=2)
+    note_copy.wait()
 
 
 def fill(blocks, pairs, table):
     count, rows, features = blocks.shape
-    return pl.pallas_call(
+    tiles = features // LANES
+    chunk = 2 * count // SLABS * tiles + 1
+    tiled = blocks.reshape(count, rows, tiles, LANES).transpose(0, 2, 1, 3)
+    hbm = whole(pltpu.HBM)
+    out, slots = pl.pallas_call(
         fill_kernel,
         out_shape=[
-            jax.ShapeDtypeStruct((2 * count, rows, features + LANES), jnp.bfloat16),
+            jax.ShapeDtypeStruct((SLABS, chunk, rows, LANES), jnp.bfloat16),
             jax.ShapeDtypeStruct((2 * count,), jnp.int32),
         ],
-        in_specs=[SMEM, SMEM, VMEM],
-        out_specs=[VMEM, SMEM],
-        scratch_shapes=[pltpu.SMEM((SLABS,), jnp.int32)],
+        in_specs=[hbm, hbm, hbm],
+        out_specs=[hbm, SMEM],
+        scratch_shapes=[
+            pltpu.SMEM(pairs.shape, jnp.int32),
+            pltpu.SMEM(table.shape, jnp.int32),
+            pltpu.SMEM((SLABS,), jnp.int32),
+            pltpu.SMEM((2 * count,), jnp.int32),
+            pltpu.VMEM((SLABS, rows, LANES), jnp.bfloat16),
+            pltpu.SemaphoreType.DMA((2,)),
+            pltpu.SemaphoreType.DMA((2 * count,)),
+            pltpu.SemaphoreType.DMA,
+        ],
         compiler_params=params(),
-    )(pairs, table, blocks)
+    )(pairs, table, tiled)
+    return out.reshape(SLABS * chunk, rows, LANES), slots
+
+
+def chunk_base(message, per_slab, tiles):
+    place, rank = lax.div(message, per_slab), lax.rem(message, per_slab)
+    first = place * (per_slab * tiles + 1)
+    return first + rank * tiles, first + per_slab * tiles, rank
 
 
 def sort_kernel(origin_ref, arrived_ref, *out_refs):
     size, _, features = out_refs[0].shape
+    tiles = features // LANES
+    per_slab = DEPTH * size // SLABS
+    chunked = arrived_ref.shape[2] != features
     for place, out_ref in enumerate(out_refs):
 
         def body(index, carry, place=place, out_ref=out_ref):
-            out_ref[index] = arrived_ref[origin_ref[place * size + index], :, :features]
+            origin = origin_ref[place * size + index]
+            if not chunked:
+                out_ref[index] = arrived_ref[origin]
+                return carry
+            base, _, _ = chunk_base(origin, per_slab, tiles)
+            for tile in range(tiles):
+                out_ref[index, :, tile * LANES : (tile + 1) * LANES] = arrived_ref[base + tile]
             return carry
 
         lax.fori_loop(0, size, body, 0, unroll=4)
 
 
 def sort_by_depth(arrived, origin, features):
-    total, rows, _ = arrived.shape
+    total, rows = origin.shape[0], arrived.shape[1]
     part = jax.ShapeDtypeStruct((total // DEPTH, rows, features), jnp.bfloat16)
     return pl.pallas_call(
         sort_kernel,
@@ -144,24 +209,47 @@
 
 
 def unsort_kernel(origin_ref, *refs):
-    part_refs, out_ref = refs[:-1], refs[-1]
-    size = part_refs[0].shape[0]
+    part_refs, out_ref, logs_ref = refs[:DEPTH], refs[DEPTH], refs[DEPTH + 1]
+    size, _, features = part_refs[0].shape
+    size -= 1
+    tiles = features // LANES
+    total = DEPTH * size
+    per_slab = total // SLABS
     for place, part_ref in enumerate(part_refs):
-
-        def body(index, carry, place=place, part_ref=part_ref):
-            out_ref[origin_ref[place * size + index]] = part_ref[index]
+        terms = part_ref[size, :, :LANES].astype(jnp.float32)
+
+        def body(index, carry, place=place, part_ref=part_ref, terms=terms):
+            origin = origin_ref[place * size + index]
+            base, _, rank = chunk_base(origin, per_slab, tiles)
+            for tile in range(tiles):
+                out_ref[base + tile] = part_ref[index, :, tile * LANES : (tile + 1) * LANES]
+            shift = lax.rem((rank - index) * TERM_LANES + LANES, LANES)
+            logs_ref[origin] = pltpu.roll(terms, shift, 1)
             return carry
 
         lax.fori_loop(0, size, body, 0, unroll=4)
+    lane = lax.broadcasted_iota(jnp.int32, logs_ref.shape[1:], 1) // TERM_LANES
+
+    def pack(place, carry):
+        tile = logs_ref[place * per_slab]
+        for rank in range(1, per_slab):
+            tile = jnp.where(lane == rank, logs_ref[place * per_slab + rank], tile)
+        out_ref[place * (per_slab * tiles + 1) + per_slab * tiles] = tile.astype(jnp.bfloat16)
+        return carry
+
+    lax.fori_loop(0, SLABS, pack, 0, unroll=2)
 
 
 def unsort(parts, origin):
-    size, rows, width = parts[0].shape
+    size, rows, features = parts[0].shape
+    total = origin.shape[0]
+    chunk = total // SLABS * (features // LANES) + 1
     return pl.pallas_call(
         unsort_kernel,
-        out_shape=jax.ShapeDtypeStruct((DEPTH * size, rows, width), jnp.bfloat16),
+        out_shape=jax.ShapeDtypeStruct((SLABS * chunk, rows, LANES), jnp.bfloat16),
         in_specs=[SMEM] + [VMEM] * DEPTH,
         out_specs=VMEM,
+        scratch_shapes=[pltpu.VMEM((total, rows, LANES), jnp.float32)],
         compiler_params=params(),
     )(origin, *parts)
 
@@ -180,16 +268,18 @@
     rest = log_weight - first
     second = rest.astype(jnp.bfloat16).astype(jnp.float32)
     third = rest - second
-    lane = lax.broadcasted_iota(jnp.int32, (flat.shape[0], LANES), 1)
+    lane = lax.broadcasted_iota(jnp.int32, (flat.shape[0], LANES), 1) % TERM_LANES
     terms = jnp.where(lane == 0, first, jnp.where(lane == 1, second, third))
     return summed * (1.0 / totals), terms
 
 
-def score_kernel(count, *refs):
-    part_refs, refs = refs[:count], refs[count:]
+def score_kernel(*refs):
+    part_refs, refs = refs[:DEPTH], refs[DEPTH:]
     cluster_refs, norm_refs, out_refs = refs[:CORES], refs[CORES : 2 * CORES], refs[2 * CORES :]
     size, rows, features = part_refs[0].shape
     half = size // CORES
+    lane = lax.broadcasted_iota(jnp.int32, (rows, LANES), 1) // TERM_LANES
+    shared = [jnp.zeros((rows, LANES), jnp.float32)] * DEPTH
     for side in range(CORES):
         span = slice(side * half, (side + 1) * half)
         flat = jnp.concatenate(
@@ -200,26 +290,28 @@
         ).astype(jnp.bfloat16)
         part, terms = score(flat, cluster_refs[side][...], norm_refs[side][...])
         for place, out_ref in enumerate(out_refs):
-            lines = slice(place * half * rows, (place + 1) * half * rows)
-            out_ref[span, :, :features] = (
-                part[lines].reshape(half, rows, features).astype(jnp.bfloat16)
-            )
-            out_ref[span, :, features:] = (
-                terms[lines].reshape(half, rows, LANES).astype(jnp.bfloat16)
-            )
+            first = place * half * rows
+            lines = part[first : first + half * rows]
+            out_ref[span] = lines.reshape(half, rows, features).astype(jnp.bfloat16)
+            for index in range(half):
+                line = first + index * rows
+                shared[place] = jnp.where(
+                    lane == side * half + index, terms[line : line + rows], shared[place]
+                )
+    for place, out_ref in enumerate(out_refs):
+        out_ref[size, :, :LANES] = shared[place].astype(jnp.bfloat16)
 
 
 def score_parts(parts, clusters, norms):
-    count = len(parts)
     size, rows, features = parts[0].shape
     references = clusters[0].shape[0]
-    total = count * size * rows
-    out = jax.ShapeDtypeStruct((size, rows, features + LANES), jnp.bfloat16)
+    total = DEPTH * size * rows
+    out = jax.ShapeDtypeStruct((size + 1, rows, features), jnp.bfloat16)
     return pl.pallas_call(
-        functools.partial(score_kernel, count),
-        out_shape=[out] * count,
-        in_specs=[VMEM] * (count + 2 * CORES),
-        out_specs=[VMEM] * count,
+        score_kernel,
+        out_shape=[out] * DEPTH,
+        in_specs=[VMEM] * (DEPTH + 2 * CORES),
+        out_specs=[VMEM] * DEPTH,
         compiler_params=params(),
         cost_estimate=pl.CostEstimate(
             flops=4 * total * references * features,
@@ -230,12 +322,16 @@
 
 
 def combine_kernel(log_count, slots_ref, blocks_ref, returned_ref, mixed_ref, density_ref, *send_refs):
-    features = blocks_ref.shape[2]
+    count, _, features = blocks_ref.shape
+    tiles = features // LANES
+    per_slab = 2 * count // SLABS
 
     def read(slot):
-        part = returned_ref[slot].astype(jnp.float32)
-        terms = part[:, features:]
-        return part[:, :features], terms[:, 0:1] + terms[:, 1:2] + terms[:, 2:3]
+        base, last, rank = chunk_base(slot, per_slab, tiles)
+        part = returned_ref[pl.ds(base, tiles)].astype(jnp.float32)
+        terms = returned_ref[last].astype(jnp.float32)
+        terms = pltpu.roll(terms, lax.rem(LANES - rank * TERM_LANES, LANES), 1)
+        return part, terms[:, 0:1] + terms[:, 1:2] + terms[:, 2:3]
 
     def body(block, densities):
         first_slot, second_slot = slots_ref[2 * block], slots_ref[2 * block + 1]
@@ -247,16 +343,19 @@
         pair_total = first_share + second_share
         inverse = 1.0 / pair_total
         mixed = (
-            (first_share * inverse) * first_part + (second_share * inverse) * second_part
+            (first_share * inverse)[None] * first_part
+            + (second_share * inverse)[None] * second_part
         ).astype(jnp.bfloat16)
         squares = jnp.sum(
             jnp.square(blocks_ref[block].astype(jnp.float32)), axis=1, keepdims=True
         )
         density = both_top + jnp.log(pair_total) - 0.5 * INV_WIDTH * squares - log_count
-        mixed_ref[block] = mixed
-        for send_ref in send_refs:
-            send_ref[first_slot] = mixed
-            send_ref[second_slot] = mixed
+        for tile in range(tiles):
+            lanes = slice(tile * LANES, (tile + 1) * LANES)
+            mixed_ref[block, :, lanes] = mixed[tile]
+            for send_ref in send_refs:
+                send_ref[first_slot, :, lanes] = mixed[tile]
+                send_ref[second_slot, :, lanes] = mixed[tile]
         return jnp.where(lane == block, density, densities)
 
     lane = lax.broadcasted_iota(jnp.int32, density_ref.shape, 1)
@@ -286,9 +385,9 @@
     return 0.5 * jnp.sum(jnp.square(cluster_rows.astype(jnp.float32)), axis=1)[None, :]
 
 
-def sorted_origins(arrived, features, depth, core):
-    targets = arrived[:, 0, features].astype(jnp.int32)
-    total = targets.shape[0]
+def sorted_origins(arrived, total, depth, core):
+    chunks = arrived.reshape(SLABS, -1, *arrived.shape[1:])
+    targets = chunks[:, -1, 0, : total // SLABS].reshape(-1).astype(jnp.int32)
     per_cluster = total // CLUSTER_DEVICES
     order = jnp.arange(total, dtype=jnp.int32)
     earlier = (targets[:, None] == targets[None, :]) & (order[None, :] < order[:, None])
@@ -316,12 +415,10 @@
     for step in range(STEPS):
         arrived = exchange_slabs(outgoing)
         if step == 0:
-            origin = sorted_origins(arrived, features, depth, core)
+            origin = sorted_origins(arrived, slots.shape[0], depth, core)
         parts = sort_by_depth(arrived, origin, features)
         parts = [parts[0]] + [shift_depth(p, k) for p, k in zip(parts[1:], SHIFTS[1:])]
-        answers = score_parts(parts[:-1], clusters, norms)
-        last, _ = lax.optimization_barrier((parts[-1], answers[0]))
-        answers += score_parts([last], clusters, norms)
+        answers = score_parts(parts, clusters, norms)
         answers = [answers[0]] + [shift_depth(a, -k) for a, k in zip(answers[1:], SHIFTS[1:])]
         returned = exchange_slabs(unsort(answers, origin))
         current, density, *outgoing = combine(

time: 176 us -> 170 us (0.966)
  blocking collectives: 44.4 us -> 37.8 us
  waiting for transfers between devices: 60.6 us -> 65.9 us
  starting transfers between devices: 32.7 us -> 30.6 us
    ppermute x12, waiting for transfers between devices: 30.1 us -> 36.8 us  [shift_depth(): return lax.ppermute(array, AXES, pairs)]
    all_to_all x2, blocking collectives: 44.4 us -> 37.8 us  [exchange_slabs(): lax.all_to_all(array, AXES, split_axis=0, concat_axis=0, tiled=True, axis...]
    ppermute x12, starting transfers between devices: 21.4 us -> 18.2 us  [shift_depth(): return lax.ppermute(array, AXES, pairs)]
    pallas_call x7 -> x5, Pallas kernels: 21.7 us -> 18.8 us  [the longest x2 8.85 us: score_parts(): pl.pallas_call(score_kernel, out_shape=[out] * DEPTH, in_specs=[VMEM] * (...]
    pallas_call x2, Pallas kernels: 4.94 us -> 6.75 us  [combine(): pl.pallas_call(functools.partial(combine_kernel, log_count), out_shape=ou...]
  transfers between devices with their start and end apart: 15 -> 15, of which waited for: 11 -> 11; matrix products, arithmetic and copies ran while one was open for 2% -> 2% of each run, Pallas kernels for 7% -> 4%
where the time goes in v4:
time: 170 us
  waiting for transfers between devices  65.9 us (39%)
  blocking collectives  37.8 us (22%)
  starting transfers between devices  30.6 us (18%)
  Pallas kernels  27.2 us (16%)
  local copies, waits for them, and re-layouts  3.92 us (2%)
  other arithmetic  3.47 us (2%)
    all_to_all x2, blocking collectives, exchange_slabs(): lax.all_to_all(array, AXES, split_axis=0, concat_axis=0, tiled=True, axis...  37.8 us
    ppermute x12, waiting for transfers between devices, shift_depth(): return lax.ppermute(array, AXES, pairs)  36.8 us
    all_to_all x2, waiting for transfers between devices, exchange_slabs(): lax.all_to_all(array, AXES, split_axis=0, concat_axis=0, tiled=True, axis...  29 us
    ppermute x12, starting transfers between devices, shift_depth(): return lax.ppermute(array, AXES, pairs)  18.2 us
    all_to_all x2, starting transfers between devices, exchange_slabs(): lax.all_to_all(array, AXES, split_axis=0, concat_axis=0, tiled=True, axis...  12.3 us
    pallas_call x2, Pallas kernels, score_parts(): pl.pallas_call(score_kernel, out_shape=[out] * DEPTH, in_specs=[VMEM] * (...  8.85 us
    pallas_call x2, Pallas kernels, combine(): pl.pallas_call(functools.partial(combine_kernel, log_count), out_shape=ou...  6.75 us
    pallas_call x1, Pallas kernels, fill(): pl.pallas_call(fill_kernel, out_shape=[jax.ShapeDtypeStruct((SLABS, chunk...  5.28 us
  transfers between devices with their start and end apart: 15, of which 11 were waited for; matrix products, arithmetic and copies ran while one was open for 2% of the time, Pallas kernels for 4%

profile of v4, /device:TPU:0, one launch (start us, length us, event | category | flops | bytes accessed | tf_op | source)
XLA Modules:
  0.0 169.7 jit_solution(13241912496796244136)
XLA Ops:
  0.6 0.1 collective-permute-start.3
  0.7 1.2 copy-done.1
  1.9 0.7 copy-done.4
  2.6 0.7 copy-done.5
  3.2 5.3 %shard_map.59 = (bf16[16,33,8,128]{3,2,1,0:T(8,128)(2,1)S(1)}, s32[64]{0:T(128)S(1)}) custom-call(s32[2,32]{1,0:T(2,128)S(1)} %bitcast.28, s32[128]{0:T(128)S(1)} %copy-done.5, bf16[32,8,8,128]{3,2,1,0:T(8,128)(2,1)S(1)} %bitcast.22), custom_call_target="tpu_custom_call" | custom-call | tf_op jit(solution)/shard_map/pallas_call | solution.py:150
  8.5 1.0 copy-done.3
  9.5 7.1 %all-to-all-start = ((bf16[528,8,128]{2,1,0:T(8,128)(2,1)}), bf16[528,8,128]{2,1,0:T(8,128)(2,1)S(1)}, u32[]{:S(2)}, u32[]{:S(2)}) async-start(bf16[528,8,128]{2,1,0:T(8,128)(2,1)} %bitcast.23), calls=%async_computation | async-start | bytes 2162688 | tf_op jit(solution)/shard_map/all_to_all | solution.py:38
  16.7 0.5 multiply_reduce_fusion.1
  17.2 16.8 %all-to-all-done.arrived_ref = bf16[528,8,128]{2,1,0:T(8,128)(2,1)S(1)} async-done(((bf16[528,8,128]{2,1,0:T(8,128)(2,1)}), bf16[528,8,128]{2,1,0:T(8,128)(2,1)S(1)}, u32[]{:S(2)}, u32[]{:S(2)}) %all-to-all-start) | async-done | bytes 1081376 | tf_op jit(solution)/shard_map/all_to_all | solution.py:38
  34.0 0.1 reshape.98
  34.1 0.2 convert_reduce_fusion
  34.3 0.1 select_reduce_fusion.origin_ref
  34.5 0.9 shard_map.60
  35.4 2.0 %collective-permute-start = (bf16[16,8,1024]{2,1,0:T(8,128)(2,1)S(1)}, bf16[16,8,1024]{2,1,0:T(8,128)(2,1)S(1)}, u32[]{:S(2)}, u32[]{:S(2)}) collective-permute-start(bf16[16,8,1024]{2,1,0:T(8,128)(2,1)S(1)} %get-tuple-element.28), channel_id=1, source_target_pairs={{0,32},{1,33},{2,34},{3,35},{4,36},{5,37},{6,38},{7,39},{8,40},{9,... | collective-permute-start | bytes 786440 | tf_op jit(solution)/shard_map/ppermute | solution.py:51
  37.3 2.2 %collective-permute-start.1 = (bf16[16,8,1024]{2,1,0:T(8,128)(2,1)S(1)}, bf16[16,8,1024]{2,1,0:T(8,128)(2,1)S(1)}, u32[]{:S(2)}, u32[]{:S(2)}) collective-permute-start(bf16[16,8,1024]{2,1,0:T(8,128)(2,1)S(1)} %get-tuple-element.29), channel_id=1, source_target_pairs={{0,96},{1,97},{2,98},{3,99},{4,100},{5,101},{6,102},{7,103},{8,104... | collective-permute-start | bytes 786440 | tf_op jit(solution)/shard_map/ppermute | solution.py:51
  39.5 1.8 %collective-permute-start.2 = (bf16[16,8,1024]{2,1,0:T(8,128)(2,1)S(1)}, bf16[16,8,1024]{2,1,0:T(8,128)(2,1)S(1)}, u32[]{:S(2)}, u32[]{:S(2)}) collective-permute-start(bf16[16,8,1024]{2,1,0:T(8,128)(2,1)S(1)} %get-tuple-element.30), channel_id=1, source_target_pairs={{0,64},{1,65},{2,66},{3,67},{4,68},{5,69},{6,70},{7,71},{8,72},{9,... | collective-permute-start | bytes 786440 | tf_op jit(solution)/shard_map/ppermute | solution.py:51
  41.3 2.1 %multiply_reduce_fusion = f32[1024]{0:T(1024)S(1)} fusion(bf16[1024,1024]{1,0:T(8,128)(2,1)} %collective-permute-done.3.refs_5_), kind=kLoop, calls=%fused_computation | loop fusion | flops 3144704 | bytes 2101248 | tf_op jit(solution)/shard_map/reduce_sum | solution.py:385
  43.4 2.4 %collective-permute-done.refs_1_ = bf16[16,8,1024]{2,1,0:T(8,128)(2,1)S(1)} collective-permute-done((bf16[16,8,1024]{2,1,0:T(8,128)(2,1)S(1)}, bf16[16,8,1024]{2,1,0:T(8,128)(2,1)S(1)}, u32[]{:S(2)}, u32[]{:S(2)}) %collective-permute-start) | collective-permute-done | bytes 262176 | tf_op jit(solution)/shard_map/ppermute | solution.py:51
  45.8 4.6 %collective-permute-done.1.refs_2_ = bf16[16,8,1024]{2,1,0:T(8,128)(2,1)S(1)} collective-permute-done((bf16[16,8,1024]{2,1,0:T(8,128)(2,1)S(1)}, bf16[16,8,1024]{2,1,0:T(8,128)(2,1)S(1)}, u32[]{:S(2)}, u32[]{:S(2)}) %collective-permute-start.1) | collective-permute-done | bytes 262176 | tf_op jit(solution)/shard_map/ppermute | solution.py:51
  50.4 1.8 %collective-permute-done.2.refs_3_ = bf16[16,8,1024]{2,1,0:T(8,128)(2,1)S(1)} collective-permute-done((bf16[16,8,1024]{2,1,0:T(8,128)(2,1)S(1)}, bf16[16,8,1024]{2,1,0:T(8,128)(2,1)S(1)}, u32[]{:S(2)}, u32[]{:S(2)}) %collective-permute-start.2) | collective-permute-done | bytes 262176 | tf_op jit(solution)/shard_map/ppermute | solution.py:51
  52.2 4.4 %shard_map.61 = (bf16[17,8,1024]{2,1,0:T(8,128)(2,1)S(1)}, bf16[17,8,1024]{2,1,0:T(8,128)(2,1)S(1)}, bf16[17,8,1024]{2,1,0:T(8,128)(2,1)S(1)}, bf16[17,8,1024]{2,1,0:T(8,128)(2,1)S(1)}) custom-call(bf16[16,8,1024]{2,1,0:T(8,128)(2,1)S(1)} %get-tuple-element.27.refs_0_, bf16[16,8,1024]{2,1,0:T(8,128)(2,1)S(1)} %collective-permute-done.refs_1_, ...), custom_call_target="tpu_custom_call" | custom-call | flops 2147483648 | bytes 6291456 | tf_op jit(solution)/shard_map/pallas_call | solution.py:310
  56.6 1.9 %collective-permute-start.4 = (bf16[17,8,1024]{2,1,0:T(8,128)(2,1)S(1)}, bf16[17,8,1024]{2,1,0:T(8,128)(2,1)S(1)}, u32[]{:S(2)}, u32[]{:S(2)}) collective-permute-start(bf16[17,8,1024]{2,1,0:T(8,128)(2,1)S(1)} %get-tuple-element.32), channel_id=1, source_target_pairs={{0,96},{1,97},{2,98},{3,99},{4,100},{5,101},{6,102},{7,103},{8,104... | collective-permute-start | bytes 835592 | tf_op jit(solution)/shard_map/ppermute | solution.py:51
  58.5 0.2 collective-permute-start.5
  58.7 1.4 collective-permute-start.6
  60.1 6.2 %collective-permute-done.4.refs_1_ = bf16[17,8,1024]{2,1,0:T(8,128)(2,1)S(1)} collective-permute-done((bf16[17,8,1024]{2,1,0:T(8,128)(2,1)S(1)}, bf16[17,8,1024]{2,1,0:T(8,128)(2,1)S(1)}, u32[]{:S(2)}, u32[]{:S(2)}) %collective-permute-start.4) | collective-permute-done | bytes 278560 | tf_op jit(solution)/shard_map/ppermute | solution.py:51
  66.2 5.3 %collective-permute-done.5.refs_2_ = bf16[17,8,1024]{2,1,0:T(8,128)(2,1)S(1)} collective-permute-done((bf16[17,8,1024]{2,1,0:T(8,128)(2,1)S(1)}, bf16[17,8,1024]{2,1,0:T(8,128)(2,1)S(1)}, u32[]{:S(2)}, u32[]{:S(2)}) %collective-permute-start.5) | collective-permute-done | bytes 278560 | tf_op jit(solution)/shard_map/ppermute | solution.py:51
  71.6 1.8 %shard_map.62 = bf16[528,8,128]{2,1,0:T(8,128)(2,1)S(1)} custom-call(s32[64]{0:T(128)S(1)} %select_reduce_fusion.origin_ref, bf16[17,8,1024]{2,1,0:T(8,128)(2,1)S(1)} %get-tuple-element.31.refs_0_, bf16[17,8,1024]{2,1,0:T(8,128)(2,1)S(1)} %collective-permute-done.4.refs_1_, bf16[17,8,1024]{2,1,0:T(8,128)(2,1)S(1)} %collective-permute-done.5.refs_2_, ...), custom_call_target="tpu_custom_call" | custom-call | tf_op jit(solution)/shard_map/pallas_call | solution.py:247
  73.4 21.8 %all_to_all.20.returned_ref = bf16[528,8,128]{2,1,0:T(8,128)(2,1)S(1)} all-to-all(bf16[528,8,128]{2,1,0:T(8,128)(2,1)S(1)} %shard_map.62), channel_id=1, replica_groups={{0,5,10,15,1,6,11,12,2,7,8,13,3,4,9,14},{16,21,26,31,20,25,30,19,24,29,..., dimensions={0} | all-to-all | bytes 2162688 | tf_op jit(solution)/shard_map/all_to_all | solution.py:38
  95.3 3.2 %shard_map.63 = (bf16[32,8,1024]{2,1,0:T(8,128)(2,1)S(1)}, f32[8,128]{1,0:T(8,128)S(1)}, bf16[64,8,1024]{2,1,0:T(8,128)(2,1)S(1)}) custom-call(s32[64]{0:T(128)S(1)} %get-tuple-element.25.slots_ref, bf16[32,8,1024]{2,1,0:T(8,128)(2,1)S(1)} %copy-done.2, bf16[528,8,128]{2,1,0:T(8,128)(2,1)S(1)} %all_to_all.20.returned_ref), custom_call_target="tpu_custom_call" | custom-call | tf_op jit(solution)/shard_map/pallas_call | solution.py:375
  98.5 16.0 %all_to_all.21.arrived_ref = bf16[64,8,1024]{2,1,0:T(8,128)(2,1)S(1)} all-to-all(bf16[64,8,1024]{2,1,0:T(8,128)(2,1)S(1)} %get-tuple-element.36), channel_id=1, replica_groups={{0,5,10,15,1,6,11,12,2,7,8,13,3,4,9,14},{16,21,26,31,20,25,30,19,24,29,..., dimensions={0} | all-to-all | bytes 2097152 | tf_op jit(solution)/shard_map/all_to_all | solution.py:38
  114.4 0.7 shard_map.64
  115.1 1.5 collective-permute-start.7
  116.7 1.8 %collective-permute-start.8 = (bf16[16,8,1024]{2,1,0:T(8,128)(2,1)S(1)}, bf16[16,8,1024]{2,1,0:T(8,128)(2,1)S(1)}, u32[]{:S(2)}, u32[]{:S(2)}) collective-permute-start(bf16[16,8,1024]{2,1,0:T(8,128)(2,1)S(1)} %get-tuple-element.39), channel_id=1, source_target_pairs={{0,96},{1,97},{2,98},{3,99},{4,100},{5,101},{6,102},{7,103},{8,104... | collective-permute-start | bytes 786440 | tf_op jit(solution)/shard_map/ppermute | solution.py:51
  118.4 1.6 collective-permute-start.9
  120.0 4.6 %collective-permute-done.7.refs_1_ = bf16[16,8,1024]{2,1,0:T(8,128)(2,1)S(1)} collective-permute-done((bf16[16,8,1024]{2,1,0:T(8,128)(2,1)S(1)}, bf16[16,8,1024]{2,1,0:T(8,128)(2,1)S(1)}, u32[]{:S(2)}, u32[]{:S(2)}) %collective-permute-start.7) | collective-permute-done | bytes 262176 | tf_op jit(solution)/shard_map/ppermute | solution.py:51
  124.6 2.8 %collective-permute-done.9.refs_3_ = bf16[16,8,1024]{2,1,0:T(8,128)(2,1)S(1)} collective-permute-done((bf16[16,8,1024]{2,1,0:T(8,128)(2,1)S(1)}, bf16[16,8,1024]{2,1,0:T(8,128)(2,1)S(1)}, u32[]{:S(2)}, u32[]{:S(2)}) %collective-permute-start.9) | collective-permute-done | bytes 262176 | tf_op jit(solution)/shard_map/ppermute | solution.py:51
  127.4 4.4 %shard_map.65 = (bf16[17,8,1024]{2,1,0:T(8,128)(2,1)S(1)}, bf16[17,8,1024]{2,1,0:T(8,128)(2,1)S(1)}, bf16[17,8,1024]{2,1,0:T(8,128)(2,1)S(1)}, bf16[17,8,1024]{2,1,0:T(8,128)(2,1)S(1)}) custom-call(bf16[16,8,1024]{2,1,0:T(8,128)(2,1)S(1)} %get-tuple-element.37.refs_0_, bf16[16,8,1024]{2,1,0:T(8,128)(2,1)S(1)} %collective-permute-done.7.refs_1_, ...), custom_call_target="tpu_custom_call" | custom-call | flops 2147483648 | bytes 6291456 | tf_op jit(solution)/shard_map/pallas_call | solution.py:310
  131.8 2.3 %collective-permute-start.10 = (bf16[17,8,1024]{2,1,0:T(8,128)(2,1)S(1)}, bf16[17,8,1024]{2,1,0:T(8,128)(2,1)S(1)}, u32[]{:S(2)}, u32[]{:S(2)}) collective-permute-start(bf16[17,8,1024]{2,1,0:T(8,128)(2,1)S(1)} %get-tuple-element.42), channel_id=1, source_target_pairs={{0,96},{1,97},{2,98},{3,99},{4,100},{5,101},{6,102},{7,103},{8,104... | collective-permute-start | bytes 835592 | tf_op jit(solution)/shard_map/ppermute | solution.py:51
  134.2 1.5 collective-permute-start.12
  135.7 3.5 %collective-permute-done.10.refs_1_ = bf16[17,8,1024]{2,1,0:T(8,128)(2,1)S(1)} collective-permute-done((bf16[17,8,1024]{2,1,0:T(8,128)(2,1)S(1)}, bf16[17,8,1024]{2,1,0:T(8,128)(2,1)S(1)}, u32[]{:S(2)}, u32[]{:S(2)}) %collective-permute-start.10) | collective-permute-done | bytes 278560 | tf_op jit(solution)/shard_map/ppermute | solution.py:51
  139.2 5.7 %collective-permute-done.11.refs_2_ = bf16[17,8,1024]{2,1,0:T(8,128)(2,1)S(1)} collective-permute-done((bf16[17,8,1024]{2,1,0:T(8,128)(2,1)S(1)}, bf16[17,8,1024]{2,1,0:T(8,128)(2,1)S(1)}, u32[]{:S(2)}, u32[]{:S(2)}) %collective-permute-start.11) | collective-permute-done | bytes 278560 | tf_op jit(solution)/shard_map/ppermute | solution.py:51
  144.9 2.8 %shard_map.66 = bf16[528,8,128]{2,1,0:T(8,128)(2,1)} custom-call(s32[64]{0:T(128)S(1)} %select_reduce_fusion.origin_ref, bf16[17,8,1024]{2,1,0:T(8,128)(2,1)S(1)} %get-tuple-element.41.refs_0_, bf16[17,8,1024]{2,1,0:T(8,128)(2,1)S(1)} %collective-permute-done.10.refs_1_, bf16[17,8,1024]{2,1,0:T(8,128)(2,1)S(1)} %collective-permute-done.11.refs_2_, ...), custom_call_target="tpu_custom_call" | custom-call | tf_op jit(solution)/shard_map/pallas_call | solution.py:247
  147.8 5.2 %all-to-all-start.3 = ((bf16[528,8,128]{2,1,0:T(8,128)(2,1)}), bf16[528,8,128]{2,1,0:T(8,128)(2,1)S(1)}, u32[]{:S(2)}, u32[]{:S(2)}) async-start(bf16[528,8,128]{2,1,0:T(8,128)(2,1)} %shard_map.66), calls=%async_computation.3 | async-start | bytes 2162688 | tf_op jit(solution)/shard_map/all_to_all | solution.py:38
  153.1 0.1 stack_reshape.6
  153.1 12.2 %all-to-all-done.3.returned_ref = bf16[528,8,128]{2,1,0:T(8,128)(2,1)S(1)} async-done(((bf16[528,8,128]{2,1,0:T(8,128)(2,1)}), bf16[528,8,128]{2,1,0:T(8,128)(2,1)S(1)}, u32[]{:S(2)}, u32[]{:S(2)}) %all-to-all-start.3) | async-done | bytes 1081376 | tf_op jit(solution)/shard_map/all_to_all | solution.py:38
  165.3 3.6 %shard_map.67 = (bf16[32,8,1024]{2,1,0:T(8,128)(2,1)}, f32[8,128]{1,0:T(8,128)S(1)}) custom-call(s32[64]{0:T(128)S(1)} %get-tuple-element.25.slots_ref, bf16[32,8,1024]{2,1,0:T(8,128)(2,1)S(1)} %get-tuple-element.35.blocks_ref, bf16[528,8,128]{2,1,0:T(8,128)(2,1)S(1)} %all-to-all-done.3.returned_ref), custom_call_target="tpu_custom_call" | custom-call | tf_op jit(solution)/shard_map/pallas_call | solution.py:375
  169.0 0.1 stack_reshape.7
  169.1 0.6 pad_maximum_fusion
  (22 shorter events, 0.2 us)
Async XLA Ops:
  0.6 16.1 %copy-start = (bf16[1,1024,1024]{2,1,0:T(8,128)(2,1)S(1)}, bf16[1,1024,1024]{2,1,0:T(8,128)(2,1)}, u32[]{:S(2)}) copy-start(bf16[1,1024,1024]{2,1,0:T(8,128)(2,1)} %param.5) | copy-start | bytes 6291460
  0.6 40.7 %collective-permute-start.3 = (bf16[1024,1024]{1,0:T(8,128)(2,1)}, bf16[1024,1024]{1,0:T(8,128)(2,1)}, u32[]{:S(2)}, u32[]{:S(2)}) collective-permute-start(bf16[1024,1024]{1,0:T(8,128)(2,1)} %bitcast.19), channel_id=1, source_target_pairs={{0,16},{1,17},{2,18},{3,19},{4,20},{5,21},{6,22},{7,23},{8,24},{9,... | collective-permute-start | bytes 6291464 | tf_op jit(solution)/shard_map/ppermute | solution.py:59
  0.7 1.2 copy-start.1
  1.9 0.7 copy-start.4
  2.6 0.7 copy-start.5
  8.5 1.0 copy-start.3
  9.5 24.5 %all-to-all-start = ((bf16[528,8,128]{2,1,0:T(8,128)(2,1)}), bf16[528,8,128]{2,1,0:T(8,128)(2,1)S(1)}, u32[]{:S(2)}, u32[]{:S(2)}) async-start(bf16[528,8,128]{2,1,0:T(8,128)(2,1)} %bitcast.23), calls=%async_computation | async-start | bytes 2162688 | tf_op jit(solution)/shard_map/all_to_all | solution.py:38
  35.4 10.4 %collective-permute-start = (bf16[16,8,1024]{2,1,0:T(8,128)(2,1)S(1)}, bf16[16,8,1024]{2,1,0:T(8,128)(2,1)S(1)}, u32[]{:S(2)}, u32[]{:S(2)}) collective-permute-start(bf16[16,8,1024]{2,1,0:T(8,128)(2,1)S(1)} %get-tuple-element.28), channel_id=1, source_target_pairs={{0,32},{1,33},{2,34},{3,35},{4,36},{5,37},{6,38},{7,39},{8,40},{9,... | collective-permute-start | bytes 786440 | tf_op jit(solution)/shard_map/ppermute | solution.py:51
  37.3 13.0 %collective-permute-start.1 = (bf16[16,8,1024]{2,1,0:T(8,128)(2,1)S(1)}, bf16[16,8,1024]{2,1,0:T(8,128)(2,1)S(1)}, u32[]{:S(2)}, u32[]{:S(2)}) collective-permute-start(bf16[16,8,1024]{2,1,0:T(8,128)(2,1)S(1)} %get-tuple-element.29), channel_id=1, source_target_pairs={{0,96},{1,97},{2,98},{3,99},{4,100},{5,101},{6,102},{7,103},{8,104... | collective-permute-start | bytes 786440 | tf_op jit(solution)/shard_map/ppermute | solution.py:51
  39.5 12.6 %collective-permute-start.2 = (bf16[16,8,1024]{2,1,0:T(8,128)(2,1)S(1)}, bf16[16,8,1024]{2,1,0:T(8,128)(2,1)S(1)}, u32[]{:S(2)}, u32[]{:S(2)}) collective-permute-start(bf16[16,8,1024]{2,1,0:T(8,128)(2,1)S(1)} %get-tuple-element.30), channel_id=1, source_target_pairs={{0,64},{1,65},{2,66},{3,67},{4,68},{5,69},{6,70},{7,71},{8,72},{9,... | collective-permute-start | bytes 786440 | tf_op jit(solution)/shard_map/ppermute | solution.py:51
  56.6 9.7 %collective-permute-start.4 = (bf16[17,8,1024]{2,1,0:T(8,128)(2,1)S(1)}, bf16[17,8,1024]{2,1,0:T(8,128)(2,1)S(1)}, u32[]{:S(2)}, u32[]{:S(2)}) collective-permute-start(bf16[17,8,1024]{2,1,0:T(8,128)(2,1)S(1)} %get-tuple-element.32), channel_id=1, source_target_pairs={{0,96},{1,97},{2,98},{3,99},{4,100},{5,101},{6,102},{7,103},{8,104... | collective-permute-start | bytes 835592 | tf_op jit(solution)/shard_map/ppermute | solution.py:51
  58.5 13.1 %collective-permute-start.5 = (bf16[17,8,1024]{2,1,0:T(8,128)(2,1)S(1)}, bf16[17,8,1024]{2,1,0:T(8,128)(2,1)S(1)}, u32[]{:S(2)}, u32[]{:S(2)}) collective-permute-start(bf16[17,8,1024]{2,1,0:T(8,128)(2,1)S(1)} %get-tuple-element.33), channel_id=1, source_target_pairs={{0,32},{1,33},{2,34},{3,35},{4,36},{5,37},{6,38},{7,39},{8,40},{9,... | collective-permute-start | bytes 835592 | tf_op jit(solution)/shard_map/ppermute | solution.py:51
  58.7 12.9 %collective-permute-start.6 = (bf16[17,8,1024]{2,1,0:T(8,128)(2,1)S(1)}, bf16[17,8,1024]{2,1,0:T(8,128)(2,1)S(1)}, u32[]{:S(2)}, u32[]{:S(2)}) collective-permute-start(bf16[17,8,1024]{2,1,0:T(8,128)(2,1)S(1)} %get-tuple-element.34), channel_id=1, source_target_pairs={{0,64},{1,65},{2,66},{3,67},{4,68},{5,69},{6,70},{7,71},{8,72},{9,... | collective-permute-start | bytes 835592 | tf_op jit(solution)/shard_map/ppermute | solution.py:51
  71.6 23.7 %copy-start.2 = (bf16[32,8,1024]{2,1,0:T(8,128)(2,1)S(1)}, bf16[32,8,1024]{2,1,0:T(8,128)(2,1)}, u32[]{:S(2)}) copy-start(bf16[32,8,1024]{2,1,0:T(8,128)(2,1)} %blocks_ref.1) | copy-start | bytes 1572868
  115.1 9.4 %collective-permute-start.7 = (bf16[16,8,1024]{2,1,0:T(8,128)(2,1)S(1)}, bf16[16,8,1024]{2,1,0:T(8,128)(2,1)S(1)}, u32[]{:S(2)}, u32[]{:S(2)}) collective-permute-start(bf16[16,8,1024]{2,1,0:T(8,128)(2,1)S(1)} %get-tuple-element.38), channel_id=1, source_target_pairs={{0,32},{1,33},{2,34},{3,35},{4,36},{5,37},{6,38},{7,39},{8,40},{9,... | collective-permute-start | bytes 786440 | tf_op jit(solution)/shard_map/ppermute | solution.py:51
  116.7 7.9 %collective-permute-start.8 = (bf16[16,8,1024]{2,1,0:T(8,128)(2,1)S(1)}, bf16[16,8,1024]{2,1,0:T(8,128)(2,1)S(1)}, u32[]{:S(2)}, u32[]{:S(2)}) collective-permute-start(bf16[16,8,1024]{2,1,0:T(8,128)(2,1)S(1)} %get-tuple-element.39), channel_id=1, source_target_pairs={{0,96},{1,97},{2,98},{3,99},{4,100},{5,101},{6,102},{7,103},{8,104... | collective-permute-start | bytes 786440 | tf_op jit(solution)/shard_map/ppermute | solution.py:51
  118.4 8.9 %collective-permute-start.9 = (bf16[16,8,1024]{2,1,0:T(8,128)(2,1)S(1)}, bf16[16,8,1024]{2,1,0:T(8,128)(2,1)S(1)}, u32[]{:S(2)}, u32[]{:S(2)}) collective-permute-start(bf16[16,8,1024]{2,1,0:T(8,128)(2,1)S(1)} %get-tuple-element.40), channel_id=1, source_target_pairs={{0,64},{1,65},{2,66},{3,67},{4,68},{5,69},{6,70},{7,71},{8,72},{9,... | collective-permute-start | bytes 786440 | tf_op jit(solution)/shard_map/ppermute | solution.py:51
  131.8 7.4 %collective-permute-start.10 = (bf16[17,8,1024]{2,1,0:T(8,128)(2,1)S(1)}, bf16[17,8,1024]{2,1,0:T(8,128)(2,1)S(1)}, u32[]{:S(2)}, u32[]{:S(2)}) collective-permute-start(bf16[17,8,1024]{2,1,0:T(8,128)(2,1)S(1)} %get-tuple-element.42), channel_id=1, source_target_pairs={{0,96},{1,97},{2,98},{3,99},{4,100},{5,101},{6,102},{7,103},{8,104... | collective-permute-start | bytes 835592 | tf_op jit(solution)/shard_map/ppermute | solution.py:51
  134.2 10.7 %collective-permute-start.11 = (bf16[17,8,1024]{2,1,0:T(8,128)(2,1)S(1)}, bf16[17,8,1024]{2,1,0:T(8,128)(2,1)S(1)}, u32[]{:S(2)}, u32[]{:S(2)}) collective-permute-start(bf16[17,8,1024]{2,1,0:T(8,128)(2,1)S(1)} %get-tuple-element.43), channel_id=1, source_target_pairs={{0,32},{1,33},{2,34},{3,35},{4,36},{5,37},{6,38},{7,39},{8,40},{9,... | collective-permute-start | bytes 835592 | tf_op jit(solution)/shard_map/ppermute | solution.py:51
  134.2 10.7 %collective-permute-start.12 = (bf16[17,8,1024]{2,1,0:T(8,128)(2,1)S(1)}, bf16[17,8,1024]{2,1,0:T(8,128)(2,1)S(1)}, u32[]{:S(2)}, u32[]{:S(2)}) collective-permute-start(bf16[17,8,1024]{2,1,0:T(8,128)(2,1)S(1)} %get-tuple-element.44), channel_id=1, source_target_pairs={{0,64},{1,65},{2,66},{3,67},{4,68},{5,69},{6,70},{7,71},{8,72},{9,... | collective-permute-start | bytes 835592 | tf_op jit(solution)/shard_map/ppermute | solution.py:51
  147.8 17.6 %all-to-all-start.3 = ((bf16[528,8,128]{2,1,0:T(8,128)(2,1)}), bf16[528,8,128]{2,1,0:T(8,128)(2,1)S(1)}, u32[]{:S(2)}, u32[]{:S(2)}) async-start(bf16[528,8,128]{2,1,0:T(8,128)(2,1)} %shard_map.66), calls=%async_computation.3 | async-start | bytes 2162688 | tf_op jit(solution)/shard_map/all_to_all | solution.py:38

commit v5 on v4

--- a/solution.py
+++ b/solution.py
@@ -20,6 +20,7 @@
 CLUSTER_DEVICES = DEPTH * CORES
 SHIFTS = (0, 1, 3, 2)
 TERM_LANES = 8
+TERMS = 3
 
 
 def slab_order(core):
@@ -78,9 +79,10 @@
 
 def fill_kernel(
     pairs_hbm, table_hbm, blocks_ref, out_ref, slots_ref,
-    pairs_ref, table_ref, counts_ref, targets_ref, notes_ref, input_sems, copy_sems, note_sem,
+    pairs_ref, table_ref, counts_ref, targets_ref, input_sems,
 ):
-    count, tiles = blocks_ref.shape[:2]
+    count, rows, features = blocks_ref.shape
+    tiles = features // LANES
     per_slab = 2 * count // SLABS
     core = lax.rem(lax.axis_index("cluster").astype(jnp.int32), CORES)
     inputs = [
@@ -89,85 +91,69 @@
     ]
     for copy in inputs:
         copy.start()
-
-    def clear(place, carry):
+    for place in range(SLABS):
         counts_ref[place] = 0
-        return carry
-
-    lax.fori_loop(0, SLABS, clear, 0)
     for copy in inputs:
         copy.wait()
 
-    def message_copy(message, slot):
-        place, rank = lax.div(slot, per_slab), lax.rem(slot, per_slab)
-        return pltpu.make_async_copy(
-            blocks_ref.at[lax.div(message, 2)],
-            out_ref.at[place, pl.ds(rank * tiles, tiles)],
-            copy_sems.at[message],
-        )
-
-    def send(block, carry):
+    def assign(block, carry):
         for side in range(2):
             entry = table_ref[pairs_ref[side, block]]
             place = slab_place(lax.rem(entry, SLABS), core)
             rank = counts_ref[place]
             counts_ref[place] = rank + 1
             slot = place * per_slab + rank
-            message = 2 * block + side
-            slots_ref[message] = slot
+            slots_ref[2 * block + side] = slot
             targets_ref[slot] = lax.div(entry, SLABS)
-            message_copy(message, slot).start()
         return carry
 
-    lax.fori_loop(0, count, send, 0, unroll=2)
-    lane = lax.broadcasted_iota(jnp.int32, notes_ref.shape[1:], 1)
+    lax.fori_loop(0, count, assign, 0, unroll=4)
+
+    def put(block, carry):
+        bases = [chunk_base(slots_ref[2 * block + side], per_slab, tiles)[0] for side in range(2)]
+        for tile in range(tiles):
+            values = blocks_ref[block, :, tile * LANES : (tile + 1) * LANES]
+            for base in bases:
+                out_ref[base + tile] = values
+        return carry
+
+    lax.fori_loop(0, count, put, 0, unroll=4)
+    lane = lax.broadcasted_iota(jnp.int32, (rows, LANES), 1)
 
     def note(place, carry):
-        tile = jnp.zeros(notes_ref.shape[1:], jnp.int32)
+        tile = jnp.zeros((rows, LANES), jnp.int32)
         for rank in range(per_slab):
             tile = jnp.where(lane == rank, targets_ref[place * per_slab + rank], tile)
-        notes_ref[place] = tile.astype(jnp.float32).astype(jnp.bfloat16)
+        tile = tile.astype(jnp.float32).astype(jnp.bfloat16)
+        out_ref[place * (per_slab * tiles + 1) + per_slab * tiles] = tile
         return carry
 
-    lax.fori_loop(0, SLABS, note, 0, unroll=2)
-    note_copy = pltpu.make_async_copy(notes_ref, out_ref.at[:, per_slab * tiles], note_sem)
-    note_copy.start()
-
-    def wait(message, carry):
-        message_copy(message, slots_ref[message]).wait()
-        return carry
-
-    lax.fori_loop(0, 2 * count, wait, 0, unroll=2)
-    note_copy.wait()
+    lax.fori_loop(0, SLABS, note, 0, unroll=4)
 
 
 def fill(blocks, pairs, table):
     count, rows, features = blocks.shape
-    tiles = features // LANES
-    chunk = 2 * count // SLABS * tiles + 1
-    tiled = blocks.reshape(count, rows, tiles, LANES).transpose(0, 2, 1, 3)
+    chunk = 2 * count // SLABS * (features // LANES) + 1
+    pairs = pltpu.with_memory_space_constraint(pairs, pltpu.HBM)
+    table = pltpu.with_memory_space_constraint(table, pltpu.HBM)
     hbm = whole(pltpu.HBM)
-    out, slots = pl.pallas_call(
+    return pl.pallas_call(
         fill_kernel,
         out_shape=[
-            jax.ShapeDtypeStruct((SLABS, chunk, rows, LANES), jnp.bfloat16),
+            jax.ShapeDtypeStruct((SLABS * chunk, rows, LANES), jnp.bfloat16),
             jax.ShapeDtypeStruct((2 * count,), jnp.int32),
         ],
-        in_specs=[hbm, hbm, hbm],
-        out_specs=[hbm, SMEM],
+        in_specs=[hbm, hbm, VMEM],
+        out_specs=[VMEM, SMEM],
         scratch_shapes=[
             pltpu.SMEM(pairs.shape, jnp.int32),
             pltpu.SMEM(table.shape, jnp.int32),
             pltpu.SMEM((SLABS,), jnp.int32),
             pltpu.SMEM((2 * count,), jnp.int32),
-            pltpu.VMEM((SLABS, rows, LANES), jnp.bfloat16),
             pltpu.SemaphoreType.DMA((2,)),
-            pltpu.SemaphoreType.DMA((2 * count,)),
-            pltpu.SemaphoreType.DMA,
         ],
         compiler_params=params(),
-    )(pairs, table, tiled)
-    return out.reshape(SLABS * chunk, rows, LANES), slots
+    )(pairs, table, blocks)
 
 
 def chunk_base(message, per_slab, tiles):
@@ -210,34 +196,32 @@
 
 def unsort_kernel(origin_ref, *refs):
     part_refs, out_ref, logs_ref = refs[:DEPTH], refs[DEPTH], refs[DEPTH + 1]
-    size, _, features = part_refs[0].shape
+    size, rows, features = part_refs[0].shape
     size -= 1
     tiles = features // LANES
     total = DEPTH * size
     per_slab = total // SLABS
+    lane = lax.broadcasted_iota(jnp.int32, (rows, LANES), 1)
+    halves = [lane < LANES // 2, lane >= LANES // 2]
     for place, part_ref in enumerate(part_refs):
-        terms = part_ref[size, :, :LANES].astype(jnp.float32)
-
-        def body(index, carry, place=place, part_ref=part_ref, terms=terms):
+        for index in range(size):
             origin = origin_ref[place * size + index]
-            base, _, rank = chunk_base(origin, per_slab, tiles)
+            base, _, _ = chunk_base(origin, per_slab, tiles)
             for tile in range(tiles):
                 out_ref[base + tile] = part_ref[index, :, tile * LANES : (tile + 1) * LANES]
-            shift = lax.rem((rank - index) * TERM_LANES + LANES, LANES)
-            logs_ref[origin] = pltpu.roll(terms, shift, 1)
-            return carry
-
-        lax.fori_loop(0, size, body, 0, unroll=4)
-    lane = lax.broadcasted_iota(jnp.int32, logs_ref.shape[1:], 1) // TERM_LANES
+            first = index // 2 * LANES
+            terms = part_ref[size, :, first : first + LANES].astype(jnp.float32)
+            logs_ref[origin] = jnp.where(halves[index % 2], terms, 0.0)
+    slot = lane % (LANES // 2) // TERM_LANES
 
     def pack(place, carry):
         tile = logs_ref[place * per_slab]
         for rank in range(1, per_slab):
-            tile = jnp.where(lane == rank, logs_ref[place * per_slab + rank], tile)
+            tile = jnp.where(slot == rank, logs_ref[place * per_slab + rank], tile)
         out_ref[place * (per_slab * tiles + 1) + per_slab * tiles] = tile.astype(jnp.bfloat16)
         return carry
 
-    lax.fori_loop(0, SLABS, pack, 0, unroll=2)
+    lax.fori_loop(0, SLABS, pack, 0, unroll=4)
 
 
 def unsort(parts, origin):
@@ -278,8 +262,7 @@
     cluster_refs, norm_refs, out_refs = refs[:CORES], refs[CORES : 2 * CORES], refs[2 * CORES :]
     size, rows, features = part_refs[0].shape
     half = size // CORES
-    lane = lax.broadcasted_iota(jnp.int32, (rows, LANES), 1) // TERM_LANES
-    shared = [jnp.zeros((rows, LANES), jnp.float32)] * DEPTH
+    first_half = lax.broadcasted_iota(jnp.int32, (rows, LANES), 1) < LANES // 2
     for side in range(CORES):
         span = slice(side * half, (side + 1) * half)
         flat = jnp.concatenate(
@@ -293,13 +276,13 @@
             first = place * half * rows
             lines = part[first : first + half * rows]
             out_ref[span] = lines.reshape(half, rows, features).astype(jnp.bfloat16)
-            for index in range(half):
+            for index in range(0, half, 2):
                 line = first + index * rows
-                shared[place] = jnp.where(
-                    lane == side * half + index, terms[line : line + rows], shared[place]
+                both = jnp.where(
+                    first_half, terms[line : line + rows], terms[line + rows : line + 2 * rows]
                 )
-    for place, out_ref in enumerate(out_refs):
-        out_ref[size, :, :LANES] = shared[place].astype(jnp.bfloat16)
+                lanes = (side * half + index) // 2 * LANES
+                out_ref[size, :, lanes : lanes + LANES] = both.astype(jnp.bfloat16)
 
 
 def score_parts(parts, clusters, norms):
@@ -325,13 +308,17 @@
     count, _, features = blocks_ref.shape
     tiles = features // LANES
     per_slab = 2 * count // SLABS
+    lane = lax.broadcasted_iota(jnp.int32, density_ref.shape, 1)
+    lane_slot = jnp.where(
+        lane % TERM_LANES < TERMS, lane % (LANES // 2) // TERM_LANES, -1
+    )
 
     def read(slot):
         base, last, rank = chunk_base(slot, per_slab, tiles)
         part = returned_ref[pl.ds(base, tiles)].astype(jnp.float32)
         terms = returned_ref[last].astype(jnp.float32)
-        terms = pltpu.roll(terms, lax.rem(LANES - rank * TERM_LANES, LANES), 1)
-        return part, terms[:, 0:1] + terms[:, 1:2] + terms[:, 2:3]
+        terms = jnp.where(lane_slot == rank, terms, 0.0)
+        return part, jnp.sum(terms, axis=1, keepdims=True)
 
     def body(block, densities):
         first_slot, second_slot = slots_ref[2 * block], slots_ref[2 * block + 1]
@@ -358,7 +345,6 @@
                 send_ref[second_slot, :, lanes] = mixed[tile]
         return jnp.where(lane == block, density, densities)
 
-    lane = lax.broadcasted_iota(jnp.int32, density_ref.shape, 1)
     density_ref[...] = lax.fori_loop(
         0, blocks_ref.shape[0], body, jnp.zeros(density_ref.shape, jnp.float32), unroll=4
     )
@@ -404,9 +390,6 @@
     cluster_index = lax.axis_index("cluster").astype(jnp.int32)
     depth, core = cluster_index // CORES, cluster_index % CORES
     own = corpus[0]
-    other = swap_cores(own)
-    clusters = (own, other)
-    norms = (half_norms_of(own), half_norms_of(other))
     log_count = math.log(2.0 * own.shape[0])
     current = queries
     outgoing, slots = fill(current, block_pairs.T, owner_table)
@@ -415,6 +398,10 @@
     for step in range(STEPS):
         arrived = exchange_slabs(outgoing)
         if step == 0:
+            arrived, own = lax.optimization_barrier((arrived, own))
+            other = swap_cores(own)
+            clusters = (own, other)
+            norms = (half_norms_of(own), half_norms_of(other))
             origin = sorted_origins(arrived, slots.shape[0], depth, core)
         parts = sort_by_depth(arrived, origin, features)
         parts = [parts[0]] + [shift_depth(p, k) for p, k in zip(parts[1:], SHIFTS[1:])]
@@ -425,8 +412,8 @@
             current, returned, slots, log_count, step < STEPS - 1
         )
         outgoing = outgoing[0] if outgoing else None
-        densities.append(density[:, : queries.shape[0]].T.reshape(-1))
-    return (current, jnp.stack(densities))
+        densities.append(density[:, : queries.shape[0]])
+    return (current, jnp.stack(densities).transpose(0, 2, 1).reshape(STEPS, -1))
 
 
 def solution(mesh):

time: 170 us -> 161 us (0.947)
  blocking collectives: 37.8 us -> 59 us
  waiting for transfers between devices: 65.9 us -> 51.4 us
  Pallas kernels: 27.2 us -> 20 us
  starting transfers between devices: 30.6 us -> 23.9 us
    all_to_all x2 -> x3, blocking collectives: 37.8 us -> 59 us  [exchange_slabs(): lax.all_to_all(array, AXES, split_axis=0, concat_axis=0, tiled=True, axis...]
    all_to_all x2 -> x1, waiting for transfers between devices: 29 us -> 12.3 us  [exchange_slabs(): lax.all_to_all(array, AXES, split_axis=0, concat_axis=0, tiled=True, axis...]
    all_to_all x2 -> x1, starting transfers between devices: 12.3 us -> 5.13 us  [exchange_slabs(): lax.all_to_all(array, AXES, split_axis=0, concat_axis=0, tiled=True, axis...]
    pallas_call x1, Pallas kernels: 5.28 us -> 2.63 us  [fill(): pl.pallas_call(fill_kernel, out_shape=[jax.ShapeDtypeStruct((SLABS * chun...]
    pallas_call x2, Pallas kernels: 6.75 us -> 4.2 us  [combine(): pl.pallas_call(functools.partial(combine_kernel, log_count), out_shape=ou...]
    ppermute x12, waiting for transfers between devices: 36.8 us -> 39 us  [shift_depth(): return lax.ppermute(array, AXES, pairs)]
    pallas_call x2, Pallas kernels: 4.69 us -> 2.72 us  [unsort(): pl.pallas_call(unsort_kernel, out_shape=jax.ShapeDtypeStruct((SLABS * chu...]
    unnamed x12 -> x10, local copies, waits for them, and re-layouts: 3.49 us -> 1.98 us
  transfers between devices with their start and end apart: 15 -> 14, of which waited for: 11 -> 10; matrix products, arithmetic and copies ran while one was open for 2% -> 2% of each run, Pallas kernels for 4% -> 1%
where the time goes in v5:
time: 161 us
  blocking collectives  59 us (37%)
  waiting for transfers between devices  51.4 us (32%)
  starting transfers between devices  23.9 us (15%)
  Pallas kernels  20 us (12%)
  other arithmetic  2.88 us (2%)
  local copies, waits for them, and re-layouts  2.84 us (2%)
    all_to_all x3, blocking collectives, exchange_slabs(): lax.all_to_all(array, AXES, split_axis=0, concat_axis=0, tiled=True, axis...  59 us
    ppermute x12, waiting for transfers between devices, shift_depth(): return lax.ppermute(array, AXES, pairs)  39 us
    ppermute x12, starting transfers between devices, shift_depth(): return lax.ppermute(array, AXES, pairs)  18.7 us
    all_to_all x1, waiting for transfers between devices, exchange_slabs(): lax.all_to_all(array, AXES, split_axis=0, concat_axis=0, tiled=True, axis...  12.3 us
    pallas_call x2, Pallas kernels, score_parts(): pl.pallas_call(score_kernel, out_shape=[out] * DEPTH, in_specs=[VMEM] * (...  8.88 us
    all_to_all x1, starting transfers between devices, exchange_slabs(): lax.all_to_all(array, AXES, split_axis=0, concat_axis=0, tiled=True, axis...  5.13 us
    pallas_call x2, Pallas kernels, combine(): pl.pallas_call(functools.partial(combine_kernel, log_count), out_shape=ou...  4.2 us
  transfers between devices with their start and end apart: 14, of which 10 were waited for; matrix products, arithmetic and copies ran while one was open for 2% of the time, Pallas kernels for 1%

profile of v5, /device:TPU:0, one launch (start us, length us, event | category | flops | bytes accessed | tf_op | source)
XLA Modules:
  0.0 160.8 jit_solution(2651228320723444256)
XLA Ops:
  0.6 0.0 copy-start.1
  0.7 1.2 copy-done.1
  1.8 2.6 %shard_map.59 = (bf16[528,8,128]{2,1,0:T(8,128)(2,1)S(1)}, s32[64]{0:T(128)S(1)}) custom-call(s32[2,32]{1,0:T(2,128)} %bitcast.24, s32[128]{0:T(128)} %table_hbm.1, bf16[32,8,1024]{2,1,0:T(8,128)(2,1)S(1)} %copy-done.1), custom_call_target="tpu_custom_call" | custom-call | tf_op jit(solution)/shard_map/pallas_call | solution.py:140
  4.5 24.6 %all_to_all.20.arrived_ref = bf16[528,8,128]{2,1,0:T(8,128)(2,1)S(1)} all-to-all(bf16[528,8,128]{2,1,0:T(8,128)(2,1)S(1)} %get-tuple-element.28), channel_id=1, replica_groups={{0,5,10,15,1,6,11,12,2,7,8,13,3,4,9,14},{16,21,26,31,20,25,30,19,24,29,..., dimensions={0} | all-to-all | bytes 2162688 | tf_op jit(solution)/shard_map/all_to_all | solution.py:39
  29.1 0.1 reshape.94
  29.1 0.2 convert_reduce_fusion
  29.4 0.1 select_reduce_fusion.origin_ref
  29.5 0.9 shard_map.60
  30.4 2.0 %collective-permute-start = (bf16[16,8,1024]{2,1,0:T(8,128)(2,1)S(1)}, bf16[16,8,1024]{2,1,0:T(8,128)(2,1)S(1)}, u32[]{:S(2)}, u32[]{:S(2)}) collective-permute-start(bf16[16,8,1024]{2,1,0:T(8,128)(2,1)S(1)} %get-tuple-element.31), channel_id=1, source_target_pairs={{0,32},{1,33},{2,34},{3,35},{4,36},{5,37},{6,38},{7,39},{8,40},{9,... | collective-permute-start | bytes 786440 | tf_op jit(solution)/shard_map/ppermute | solution.py:52
  32.4 2.2 %collective-permute-start.1 = (bf16[16,8,1024]{2,1,0:T(8,128)(2,1)S(1)}, bf16[16,8,1024]{2,1,0:T(8,128)(2,1)S(1)}, u32[]{:S(2)}, u32[]{:S(2)}) collective-permute-start(bf16[16,8,1024]{2,1,0:T(8,128)(2,1)S(1)} %get-tuple-element.32), channel_id=1, source_target_pairs={{0,96},{1,97},{2,98},{3,99},{4,100},{5,101},{6,102},{7,103},{8,104... | collective-permute-start | bytes 786440 | tf_op jit(solution)/shard_map/ppermute | solution.py:52
  34.6 1.8 %collective-permute-start.2 = (bf16[16,8,1024]{2,1,0:T(8,128)(2,1)S(1)}, bf16[16,8,1024]{2,1,0:T(8,128)(2,1)S(1)}, u32[]{:S(2)}, u32[]{:S(2)}) collective-permute-start(bf16[16,8,1024]{2,1,0:T(8,128)(2,1)S(1)} %get-tuple-element.33), channel_id=1, source_target_pairs={{0,64},{1,65},{2,66},{3,67},{4,68},{5,69},{6,70},{7,71},{8,72},{9,... | collective-permute-start | bytes 786440 | tf_op jit(solution)/shard_map/ppermute | solution.py:52
  36.3 0.5 multiply_reduce_fusion.1
  36.8 0.0 collective-permute-done.3.refs_5_
  36.8 2.1 %multiply_reduce_fusion = f32[1024]{0:T(1024)S(1)} fusion(bf16[1024,1024]{1,0:T(8,128)(2,1)} %collective-permute-done.3.refs_5_), kind=kLoop, calls=%fused_computation | loop fusion | flops 3144704 | bytes 2101248 | tf_op jit(solution)/shard_map/reduce_sum | solution.py:371
  38.9 2.5 %collective-permute-done.refs_1_ = bf16[16,8,1024]{2,1,0:T(8,128)(2,1)S(1)} collective-permute-done((bf16[16,8,1024]{2,1,0:T(8,128)(2,1)S(1)}, bf16[16,8,1024]{2,1,0:T(8,128)(2,1)S(1)}, u32[]{:S(2)}, u32[]{:S(2)}) %collective-permute-start) | collective-permute-done | bytes 262176 | tf_op jit(solution)/shard_map/ppermute | solution.py:52
  41.5 5.0 %collective-permute-done.1.refs_2_ = bf16[16,8,1024]{2,1,0:T(8,128)(2,1)S(1)} collective-permute-done((bf16[16,8,1024]{2,1,0:T(8,128)(2,1)S(1)}, bf16[16,8,1024]{2,1,0:T(8,128)(2,1)S(1)}, u32[]{:S(2)}, u32[]{:S(2)}) %collective-permute-start.1) | collective-permute-done | bytes 262176 | tf_op jit(solution)/shard_map/ppermute | solution.py:52
  46.5 1.8 %collective-permute-done.2.refs_3_ = bf16[16,8,1024]{2,1,0:T(8,128)(2,1)S(1)} collective-permute-done((bf16[16,8,1024]{2,1,0:T(8,128)(2,1)S(1)}, bf16[16,8,1024]{2,1,0:T(8,128)(2,1)S(1)}, u32[]{:S(2)}, u32[]{:S(2)}) %collective-permute-start.2) | collective-permute-done | bytes 262176 | tf_op jit(solution)/shard_map/ppermute | solution.py:52
  48.3 4.4 %shard_map.61 = (bf16[17,8,1024]{2,1,0:T(8,128)(2,1)S(1)}, bf16[17,8,1024]{2,1,0:T(8,128)(2,1)S(1)}, bf16[17,8,1024]{2,1,0:T(8,128)(2,1)S(1)}, bf16[17,8,1024]{2,1,0:T(8,128)(2,1)S(1)}) custom-call(bf16[16,8,1024]{2,1,0:T(8,128)(2,1)S(1)} %get-tuple-element.30.refs_0_, bf16[16,8,1024]{2,1,0:T(8,128)(2,1)S(1)} %collective-permute-done.refs_1_, ...), custom_call_target="tpu_custom_call" | custom-call | flops 2147483648 | bytes 6291456 | tf_op jit(solution)/shard_map/pallas_call | solution.py:293
  52.7 1.9 %collective-permute-start.4 = (bf16[17,8,1024]{2,1,0:T(8,128)(2,1)S(1)}, bf16[17,8,1024]{2,1,0:T(8,128)(2,1)S(1)}, u32[]{:S(2)}, u32[]{:S(2)}) collective-permute-start(bf16[17,8,1024]{2,1,0:T(8,128)(2,1)S(1)} %get-tuple-element.36), channel_id=1, source_target_pairs={{0,96},{1,97},{2,98},{3,99},{4,100},{5,101},{6,102},{7,103},{8,104... | collective-permute-start | bytes 835592 | tf_op jit(solution)/shard_map/ppermute | solution.py:52
  54.6 0.2 collective-permute-start.5
  54.8 1.4 collective-permute-start.6
  56.2 10.3 %collective-permute-done.4.refs_1_ = bf16[17,8,1024]{2,1,0:T(8,128)(2,1)S(1)} collective-permute-done((bf16[17,8,1024]{2,1,0:T(8,128)(2,1)S(1)}, bf16[17,8,1024]{2,1,0:T(8,128)(2,1)S(1)}, u32[]{:S(2)}, u32[]{:S(2)}) %collective-permute-start.4) | collective-permute-done | bytes 278560 | tf_op jit(solution)/shard_map/ppermute | solution.py:52
  66.4 3.4 %collective-permute-done.5.refs_2_ = bf16[17,8,1024]{2,1,0:T(8,128)(2,1)S(1)} collective-permute-done((bf16[17,8,1024]{2,1,0:T(8,128)(2,1)S(1)}, bf16[17,8,1024]{2,1,0:T(8,128)(2,1)S(1)}, u32[]{:S(2)}, u32[]{:S(2)}) %collective-permute-start.5) | collective-permute-done | bytes 278560 | tf_op jit(solution)/shard_map/ppermute | solution.py:52
  69.8 0.9 shard_map.62
  70.7 18.4 %all_to_all.21.returned_ref = bf16[528,8,128]{2,1,0:T(8,128)(2,1)S(1)} all-to-all(bf16[528,8,128]{2,1,0:T(8,128)(2,1)S(1)} %shard_map.62), channel_id=1, replica_groups={{0,5,10,15,1,6,11,12,2,7,8,13,3,4,9,14},{16,21,26,31,20,25,30,19,24,29,..., dimensions={0} | all-to-all | bytes 2162688 | tf_op jit(solution)/shard_map/all_to_all | solution.py:39
  89.0 1.7 %shard_map.63 = (bf16[32,8,1024]{2,1,0:T(8,128)(2,1)S(1)}, f32[8,128]{1,0:T(8,128)S(1)}, bf16[64,8,1024]{2,1,0:T(8,128)(2,1)S(1)}) custom-call(s32[64]{0:T(128)S(1)} %get-tuple-element.27.slots_ref, bf16[32,8,1024]{2,1,0:T(8,128)(2,1)S(1)} %copy-done.2, bf16[528,8,128]{2,1,0:T(8,128)(2,1)S(1)} %all_to_all.21.returned_ref), custom_call_target="tpu_custom_call" | custom-call | tf_op jit(solution)/shard_map/pallas_call | solution.py:361
  90.8 0.0 copy-start.3
  90.8 0.8 copy-done.3
  91.6 16.1 %all_to_all.22.arrived_ref = bf16[64,8,1024]{2,1,0:T(8,128)(2,1)S(1)} all-to-all(bf16[64,8,1024]{2,1,0:T(8,128)(2,1)S(1)} %get-tuple-element.40), channel_id=1, replica_groups={{0,5,10,15,1,6,11,12,2,7,8,13,3,4,9,14},{16,21,26,31,20,25,30,19,24,29,..., dimensions={0} | all-to-all | bytes 2097152 | tf_op jit(solution)/shard_map/all_to_all | solution.py:39
  107.7 0.7 shard_map.64
  108.4 1.5 collective-permute-start.7
  109.8 1.9 %collective-permute-start.8 = (bf16[16,8,1024]{2,1,0:T(8,128)(2,1)S(1)}, bf16[16,8,1024]{2,1,0:T(8,128)(2,1)S(1)}, u32[]{:S(2)}, u32[]{:S(2)}) collective-permute-start(bf16[16,8,1024]{2,1,0:T(8,128)(2,1)S(1)} %get-tuple-element.43), channel_id=1, source_target_pairs={{0,96},{1,97},{2,98},{3,99},{4,100},{5,101},{6,102},{7,103},{8,104... | collective-permute-start | bytes 786440 | tf_op jit(solution)/shard_map/ppermute | solution.py:52
  111.7 1.9 %collective-permute-start.9 = (bf16[16,8,1024]{2,1,0:T(8,128)(2,1)S(1)}, bf16[16,8,1024]{2,1,0:T(8,128)(2,1)S(1)}, u32[]{:S(2)}, u32[]{:S(2)}) collective-permute-start(bf16[16,8,1024]{2,1,0:T(8,128)(2,1)S(1)} %get-tuple-element.44), channel_id=1, source_target_pairs={{0,64},{1,65},{2,66},{3,67},{4,68},{5,69},{6,70},{7,71},{8,72},{9,... | collective-permute-start | bytes 786440 | tf_op jit(solution)/shard_map/ppermute | solution.py:52
  113.6 4.0 %collective-permute-done.7.refs_1_ = bf16[16,8,1024]{2,1,0:T(8,128)(2,1)S(1)} collective-permute-done((bf16[16,8,1024]{2,1,0:T(8,128)(2,1)S(1)}, bf16[16,8,1024]{2,1,0:T(8,128)(2,1)S(1)}, u32[]{:S(2)}, u32[]{:S(2)}) %collective-permute-start.7) | collective-permute-done | bytes 262176 | tf_op jit(solution)/shard_map/ppermute | solution.py:52
  117.6 0.0 collective-permute-done.8.refs_2_
  117.6 2.8 %collective-permute-done.9.refs_3_ = bf16[16,8,1024]{2,1,0:T(8,128)(2,1)S(1)} collective-permute-done((bf16[16,8,1024]{2,1,0:T(8,128)(2,1)S(1)}, bf16[16,8,1024]{2,1,0:T(8,128)(2,1)S(1)}, u32[]{:S(2)}, u32[]{:S(2)}) %collective-permute-start.9) | collective-permute-done | bytes 262176 | tf_op jit(solution)/shard_map/ppermute | solution.py:52
  120.4 4.5 %shard_map.65 = (bf16[17,8,1024]{2,1,0:T(8,128)(2,1)S(1)}, bf16[17,8,1024]{2,1,0:T(8,128)(2,1)S(1)}, bf16[17,8,1024]{2,1,0:T(8,128)(2,1)S(1)}, bf16[17,8,1024]{2,1,0:T(8,128)(2,1)S(1)}) custom-call(bf16[16,8,1024]{2,1,0:T(8,128)(2,1)S(1)} %get-tuple-element.41.refs_0_, bf16[16,8,1024]{2,1,0:T(8,128)(2,1)S(1)} %collective-permute-done.7.refs_1_, ...), custom_call_target="tpu_custom_call" | custom-call | flops 2147483648 | bytes 6291456 | tf_op jit(solution)/shard_map/pallas_call | solution.py:293
  124.9 2.5 %collective-permute-start.10 = (bf16[17,8,1024]{2,1,0:T(8,128)(2,1)S(1)}, bf16[17,8,1024]{2,1,0:T(8,128)(2,1)S(1)}, u32[]{:S(2)}, u32[]{:S(2)}) collective-permute-start(bf16[17,8,1024]{2,1,0:T(8,128)(2,1)S(1)} %get-tuple-element.46), channel_id=1, source_target_pairs={{0,96},{1,97},{2,98},{3,99},{4,100},{5,101},{6,102},{7,103},{8,104... | collective-permute-start | bytes 835592 | tf_op jit(solution)/shard_map/ppermute | solution.py:52
  127.4 0.0 collective-permute-start.11
  127.4 1.5 collective-permute-start.12
  129.0 3.6 %collective-permute-done.10.refs_1_ = bf16[17,8,1024]{2,1,0:T(8,128)(2,1)S(1)} collective-permute-done((bf16[17,8,1024]{2,1,0:T(8,128)(2,1)S(1)}, bf16[17,8,1024]{2,1,0:T(8,128)(2,1)S(1)}, u32[]{:S(2)}, u32[]{:S(2)}) %collective-permute-start.10) | collective-permute-done | bytes 278560 | tf_op jit(solution)/shard_map/ppermute | solution.py:52
  132.5 5.6 %collective-permute-done.11.refs_2_ = bf16[17,8,1024]{2,1,0:T(8,128)(2,1)S(1)} collective-permute-done((bf16[17,8,1024]{2,1,0:T(8,128)(2,1)S(1)}, bf16[17,8,1024]{2,1,0:T(8,128)(2,1)S(1)}, u32[]{:S(2)}, u32[]{:S(2)}) %collective-permute-start.11) | collective-permute-done | bytes 278560 | tf_op jit(solution)/shard_map/ppermute | solution.py:52
  138.2 1.9 %shard_map.66 = bf16[528,8,128]{2,1,0:T(8,128)(2,1)} custom-call(s32[64]{0:T(128)S(1)} %select_reduce_fusion.origin_ref, bf16[17,8,1024]{2,1,0:T(8,128)(2,1)S(1)} %get-tuple-element.45.refs_0_, bf16[17,8,1024]{2,1,0:T(8,128)(2,1)S(1)} %collective-permute-done.10.refs_1_, bf16[17,8,1024]{2,1,0:T(8,128)(2,1)S(1)} %collective-permute-done.11.refs_2_, ...), custom_call_target="tpu_custom_call" | custom-call | tf_op jit(solution)/shard_map/pallas_call | solution.py:231
  140.0 5.1 %all-to-all-start.3 = ((bf16[528,8,128]{2,1,0:T(8,128)(2,1)}), bf16[528,8,128]{2,1,0:T(8,128)(2,1)S(1)}, u32[]{:S(2)}, u32[]{:S(2)}) async-start(bf16[528,8,128]{2,1,0:T(8,128)(2,1)} %shard_map.66), calls=%async_computation.3 | async-start | bytes 2162688 | tf_op jit(solution)/shard_map/all_to_all | solution.py:39
  145.2 12.3 %all-to-all-done.3.returned_ref = bf16[528,8,128]{2,1,0:T(8,128)(2,1)S(1)} async-done(((bf16[528,8,128]{2,1,0:T(8,128)(2,1)}), bf16[528,8,128]{2,1,0:T(8,128)(2,1)S(1)}, u32[]{:S(2)}, u32[]{:S(2)}) %all-to-all-start.3) | async-done | bytes 1081376 | tf_op jit(solution)/shard_map/all_to_all | solution.py:39
  157.5 2.5 %shard_map.67 = (bf16[32,8,1024]{2,1,0:T(8,128)(2,1)}, f32[8,128]{1,0:T(8,128)S(1)}) custom-call(s32[64]{0:T(128)S(1)} %get-tuple-element.27.slots_ref, bf16[32,8,1024]{2,1,0:T(8,128)(2,1)S(1)} %copy-done.4, bf16[528,8,128]{2,1,0:T(8,128)(2,1)S(1)} %all-to-all-done.3.returned_ref), custom_call_target="tpu_custom_call" | custom-call | tf_op jit(solution)/shard_map/pallas_call | solution.py:361
  160.0 0.1 copy.10
  160.1 0.7 reshape.93
  (17 shorter events, 0.1 us)
Async XLA Ops:
  0.6 28.4 %copy-start = (bf16[1,1024,1024]{2,1,0:T(8,128)(2,1)S(1)}, bf16[1,1024,1024]{2,1,0:T(8,128)(2,1)}, u32[]{:S(2)}) copy-start(bf16[1,1024,1024]{2,1,0:T(8,128)(2,1)} %param.5) | copy-start | bytes 6291460
  0.6 1.2 copy-start.1
  29.0 7.8 %collective-permute-start.3 = (bf16[1024,1024]{1,0:T(8,128)(2,1)S(1)}, bf16[1024,1024]{1,0:T(8,128)(2,1)}, u32[]{:S(2)}, u32[]{:S(2)}) collective-permute-start(bf16[1024,1024]{1,0:T(8,128)(2,1)S(1)} %bitcast.16), channel_id=1, source_target_pairs={{0,16},{1,17},{2,18},{3,19},{4,20},{5,21},{6,22},{7,23},{8,24},{9,... | collective-permute-start | bytes 6291464 | tf_op jit(solution)/shard_map/ppermute | solution.py:60
  30.4 11.1 %collective-permute-start = (bf16[16,8,1024]{2,1,0:T(8,128)(2,1)S(1)}, bf16[16,8,1024]{2,1,0:T(8,128)(2,1)S(1)}, u32[]{:S(2)}, u32[]{:S(2)}) collective-permute-start(bf16[16,8,1024]{2,1,0:T(8,128)(2,1)S(1)} %get-tuple-element.31), channel_id=1, source_target_pairs={{0,32},{1,33},{2,34},{3,35},{4,36},{5,37},{6,38},{7,39},{8,40},{9,... | collective-permute-start | bytes 786440 | tf_op jit(solution)/shard_map/ppermute | solution.py:52
  32.4 14.1 %collective-permute-start.1 = (bf16[16,8,1024]{2,1,0:T(8,128)(2,1)S(1)}, bf16[16,8,1024]{2,1,0:T(8,128)(2,1)S(1)}, u32[]{:S(2)}, u32[]{:S(2)}) collective-permute-start(bf16[16,8,1024]{2,1,0:T(8,128)(2,1)S(1)} %get-tuple-element.32), channel_id=1, source_target_pairs={{0,96},{1,97},{2,98},{3,99},{4,100},{5,101},{6,102},{7,103},{8,104... | collective-permute-start | bytes 786440 | tf_op jit(solution)/shard_map/ppermute | solution.py:52
  34.6 13.7 %collective-permute-start.2 = (bf16[16,8,1024]{2,1,0:T(8,128)(2,1)S(1)}, bf16[16,8,1024]{2,1,0:T(8,128)(2,1)S(1)}, u32[]{:S(2)}, u32[]{:S(2)}) collective-permute-start(bf16[16,8,1024]{2,1,0:T(8,128)(2,1)S(1)} %get-tuple-element.33), channel_id=1, source_target_pairs={{0,64},{1,65},{2,66},{3,67},{4,68},{5,69},{6,70},{7,71},{8,72},{9,... | collective-permute-start | bytes 786440 | tf_op jit(solution)/shard_map/ppermute | solution.py:52
  52.7 13.7 %collective-permute-start.4 = (bf16[17,8,1024]{2,1,0:T(8,128)(2,1)S(1)}, bf16[17,8,1024]{2,1,0:T(8,128)(2,1)S(1)}, u32[]{:S(2)}, u32[]{:S(2)}) collective-permute-start(bf16[17,8,1024]{2,1,0:T(8,128)(2,1)S(1)} %get-tuple-element.36), channel_id=1, source_target_pairs={{0,96},{1,97},{2,98},{3,99},{4,100},{5,101},{6,102},{7,103},{8,104... | collective-permute-start | bytes 835592 | tf_op jit(solution)/shard_map/ppermute | solution.py:52
  54.6 15.2 %collective-permute-start.5 = (bf16[17,8,1024]{2,1,0:T(8,128)(2,1)S(1)}, bf16[17,8,1024]{2,1,0:T(8,128)(2,1)S(1)}, u32[]{:S(2)}, u32[]{:S(2)}) collective-permute-start(bf16[17,8,1024]{2,1,0:T(8,128)(2,1)S(1)} %get-tuple-element.37), channel_id=1, source_target_pairs={{0,32},{1,33},{2,34},{3,35},{4,36},{5,37},{6,38},{7,39},{8,40},{9,... | collective-permute-start | bytes 835592 | tf_op jit(solution)/shard_map/ppermute | solution.py:52
  54.8 15.0 %collective-permute-start.6 = (bf16[17,8,1024]{2,1,0:T(8,128)(2,1)S(1)}, bf16[17,8,1024]{2,1,0:T(8,128)(2,1)S(1)}, u32[]{:S(2)}, u32[]{:S(2)}) collective-permute-start(bf16[17,8,1024]{2,1,0:T(8,128)(2,1)S(1)} %get-tuple-element.38), channel_id=1, source_target_pairs={{0,64},{1,65},{2,66},{3,67},{4,68},{5,69},{6,70},{7,71},{8,72},{9,... | collective-permute-start | bytes 835592 | tf_op jit(solution)/shard_map/ppermute | solution.py:52
  69.8 19.2 %copy-start.2 = (bf16[32,8,1024]{2,1,0:T(8,128)(2,1)S(1)}, bf16[32,8,1024]{2,1,0:T(8,128)(2,1)}, u32[]{:S(2)}) copy-start(bf16[32,8,1024]{2,1,0:T(8,128)(2,1)} %blocks_ref.3) | copy-start | bytes 1572868
  90.8 0.8 copy-start.3
  108.4 9.3 %collective-permute-start.7 = (bf16[16,8,1024]{2,1,0:T(8,128)(2,1)S(1)}, bf16[16,8,1024]{2,1,0:T(8,128)(2,1)S(1)}, u32[]{:S(2)}, u32[]{:S(2)}) collective-permute-start(bf16[16,8,1024]{2,1,0:T(8,128)(2,1)S(1)} %get-tuple-element.42), channel_id=1, source_target_pairs={{0,32},{1,33},{2,34},{3,35},{4,36},{5,37},{6,38},{7,39},{8,40},{9,... | collective-permute-start | bytes 786440 | tf_op jit(solution)/shard_map/ppermute | solution.py:52
  109.8 7.8 %collective-permute-start.8 = (bf16[16,8,1024]{2,1,0:T(8,128)(2,1)S(1)}, bf16[16,8,1024]{2,1,0:T(8,128)(2,1)S(1)}, u32[]{:S(2)}, u32[]{:S(2)}) collective-permute-start(bf16[16,8,1024]{2,1,0:T(8,128)(2,1)S(1)} %get-tuple-element.43), channel_id=1, source_target_pairs={{0,96},{1,97},{2,98},{3,99},{4,100},{5,101},{6,102},{7,103},{8,104... | collective-permute-start | bytes 786440 | tf_op jit(solution)/shard_map/ppermute | solution.py:52
  111.7 8.8 %collective-permute-start.9 = (bf16[16,8,1024]{2,1,0:T(8,128)(2,1)S(1)}, bf16[16,8,1024]{2,1,0:T(8,128)(2,1)S(1)}, u32[]{:S(2)}, u32[]{:S(2)}) collective-permute-start(bf16[16,8,1024]{2,1,0:T(8,128)(2,1)S(1)} %get-tuple-element.44), channel_id=1, source_target_pairs={{0,64},{1,65},{2,66},{3,67},{4,68},{5,69},{6,70},{7,71},{8,72},{9,... | collective-permute-start | bytes 786440 | tf_op jit(solution)/shard_map/ppermute | solution.py:52
  124.9 7.6 %collective-permute-start.10 = (bf16[17,8,1024]{2,1,0:T(8,128)(2,1)S(1)}, bf16[17,8,1024]{2,1,0:T(8,128)(2,1)S(1)}, u32[]{:S(2)}, u32[]{:S(2)}) collective-permute-start(bf16[17,8,1024]{2,1,0:T(8,128)(2,1)S(1)} %get-tuple-element.46), channel_id=1, source_target_pairs={{0,96},{1,97},{2,98},{3,99},{4,100},{5,101},{6,102},{7,103},{8,104... | collective-permute-start | bytes 835592 | tf_op jit(solution)/shard_map/ppermute | solution.py:52
  127.4 10.7 %collective-permute-start.11 = (bf16[17,8,1024]{2,1,0:T(8,128)(2,1)S(1)}, bf16[17,8,1024]{2,1,0:T(8,128)(2,1)S(1)}, u32[]{:S(2)}, u32[]{:S(2)}) collective-permute-start(bf16[17,8,1024]{2,1,0:T(8,128)(2,1)S(1)} %get-tuple-element.47), channel_id=1, source_target_pairs={{0,32},{1,33},{2,34},{3,35},{4,36},{5,37},{6,38},{7,39},{8,40},{9,... | collective-permute-start | bytes 835592 | tf_op jit(solution)/shard_map/ppermute | solution.py:52
  127.4 10.7 %collective-permute-start.12 = (bf16[17,8,1024]{2,1,0:T(8,128)(2,1)S(1)}, bf16[17,8,1024]{2,1,0:T(8,128)(2,1)S(1)}, u32[]{:S(2)}, u32[]{:S(2)}) collective-permute-start(bf16[17,8,1024]{2,1,0:T(8,128)(2,1)S(1)} %get-tuple-element.48), channel_id=1, source_target_pairs={{0,64},{1,65},{2,66},{3,67},{4,68},{5,69},{6,70},{7,71},{8,72},{9,... | collective-permute-start | bytes 835592 | tf_op jit(solution)/shard_map/ppermute | solution.py:52
  138.2 19.4 %copy-start.4 = (bf16[32,8,1024]{2,1,0:T(8,128)(2,1)S(1)}, bf16[32,8,1024]{2,1,0:T(8,128)(2,1)}, u32[]{:S(2)}) copy-start(bf16[32,8,1024]{2,1,0:T(8,128)(2,1)} %copy-done.3) | copy-start | bytes 1572868
  140.0 17.5 %all-to-all-start.3 = ((bf16[528,8,128]{2,1,0:T(8,128)(2,1)}), bf16[528,8,128]{2,1,0:T(8,128)(2,1)S(1)}, u32[]{:S(2)}, u32[]{:S(2)}) async-start(bf16[528,8,128]{2,1,0:T(8,128)(2,1)} %shard_map.66), calls=%async_computation.3 | async-start | bytes 2162688 | tf_op jit(solution)/shard_map/all_to_all | solution.py:39

commit v6 on v5

v6 whole, which is shorter than its diff:
```python
import functools
import math

import jax
import jax.numpy as jnp
from jax import lax
from jax.experimental import pallas as pl
from jax.experimental.pallas import tpu as pltpu
from jax.sharding import PartitionSpec as P

STEPS = 2
INV_WIDTH = 1.0 / 16.0
LANES = 128
VMEM_LIMIT = 48 * 1024 * 1024
AXES = ("cluster", "slab")
SIDE = 4
CORES = 2
DEPTH = 4
SLABS = SIDE * SIDE
CLUSTER_DEVICES = DEPTH * CORES
OWN, OTHER, AHEAD, OTHER_AHEAD = range(4)
GROUPS = ((OWN, OTHER), (AHEAD, OTHER_AHEAD), (AHEAD, OTHER), (OWN, OTHER_AHEAD))
STAY = 2
HALVES = ((0, 2, 4, 6), (1, 5, 7, 3))
TERM_LANES = 8
TERMS = 3


def slab_order(core):
    order = [(a, (a + b) % SIDE) for b in range(SIDE) for a in range(SIDE)]
    return [x * SIDE + y if core == 0 else y * SIDE + x for x, y in order]


def slab_groups():
    return [
        [cluster * SLABS + slab for slab in slab_order(cluster % CORES)]
        for cluster in range(CLUSTER_DEVICES)
    ]


def exchange_slabs(array):
    return lax.all_to_all(
        array, AXES, split_axis=0, concat_axis=0, tiled=True, axis_index_groups=slab_groups()
    )


def send_ahead(array, steps):
    pairs = []
    for z in range(DEPTH):
        for core in range(CORES):
            target_z = (z + (steps if core == 0 else -steps)) % DEPTH
            for slab in range(SLABS):
                source = (z * CORES + core) * SLABS + slab
                target = (target_z * CORES + core) * SLABS + slab
                pairs.append((source, target))
    return lax.ppermute(array, AXES, pairs)


def swap_cores(array):
    pairs = []
    for cluster in range(CLUSTER_DEVICES):
        for slab in range(SLABS):
            pairs.append((cluster * SLABS + slab, (cluster ^ 1) * SLABS + slab))
    return lax.ppermute(array, AXES, pairs)


def whole(space):
    return pl.BlockSpec(memory_space=space)


SMEM, VMEM = whole(pltpu.SMEM), whole(pltpu.VMEM)


def params():
    return pltpu.CompilerParams(vmem_limit_bytes=VMEM_LIMIT)


def slab_place(slab, core):
    x, y = lax.div(slab, SIDE), lax.rem(slab, SIDE)
    first, second = jnp.where(core == 0, x, y), jnp.where(core == 0, y, x)
    return lax.rem(second - first + SIDE, SIDE) * SIDE + first


def fill_kernel(
    pairs_hbm, table_hbm, blocks_hbm, out_ref, slots_ref, squares_ref,
    pairs_ref, table_ref, blocks_ref, counts_ref, targets_ref, input_sems,
):
    count, rows, features = blocks_ref.shape
    tiles = features // LANES
    per_slab = 2 * count // SLABS
    core = lax.rem(lax.axis_index("cluster").astype(jnp.int32), CORES)
    inputs = [
        pltpu.make_async_copy(pairs_hbm, pairs_ref, input_sems.at[0]),
        pltpu.make_async_copy(table_hbm, table_ref, input_sems.at[1]),
        pltpu.make_async_copy(blocks_hbm, blocks_ref, input_sems.at[2]),
    ]
    for copy in inputs:
        copy.start()
    for place in range(SLABS):
        counts_ref[place] = 0
    for copy in inputs[:2]:
        copy.wait()

    def assign(block, carry):
        for side in range(2):
            entry = table_ref[pairs_ref[side, block]]
            place = slab_place(lax.rem(entry, SLABS), core)
            rank = counts_ref[place]
            counts_ref[place] = rank + 1
            slot = place * per_slab + rank
            slots_ref[2 * block + side] = slot
            targets_ref[slot] = lax.div(entry, SLABS)
        return carry

    lax.fori_loop(0, count, assign, 0, unroll=4)
    inputs[2].wait()
    lane = lax.broadcasted_iota(jnp.int32, (rows, LANES), 1)

    def put(block, squares):
        bases = [chunk_base(slots_ref[2 * block + side], per_slab, tiles)[0] for side in range(2)]
        total = jnp.zeros((rows, LANES), jnp.float32)
        for tile in range(tiles):
            values = blocks_ref[block, :, tile * LANES : (tile + 1) * LANES]
            for base in bases:
                out_ref[base + tile] = values
            total += jnp.square(values.astype(jnp.float32))
        return jnp.where(lane == block, jnp.sum(total, axis=1, keepdims=True), squares)

    squares_ref[...] = lax.fori_loop(
        0, count, put, jnp.zeros((rows, LANES), jnp.float32), unroll=4
    )

    def note(place, carry):
        tile = jnp.zeros((rows, LANES), jnp.int32)
        for rank in range(per_slab):
            tile = jnp.where(lane == rank, targets_ref[place * per_slab + rank], tile)
        tile = tile.astype(jnp.float32).astype(jnp.bfloat16)
        out_ref[place * (per_slab * tiles + 1) + per_slab * tiles] = tile
        return carry

    lax.fori_loop(0, SLABS, note, 0, unroll=4)


def fill(blocks, pairs, table):
    count, rows, features = blocks.shape
    chunk = 2 * count // SLABS * (features // LANES) + 1
    pairs = pltpu.with_memory_space_constraint(pairs, pltpu.HBM)
    table = pltpu.with_memory_space_constraint(table, pltpu.HBM)
    blocks = pltpu.with_memory_space_constraint(blocks, pltpu.HBM)
    hbm = whole(pltpu.HBM)
    return pl.pallas_call(
        fill_kernel,
        out_shape=[
            jax.ShapeDtypeStruct((SLABS * chunk, rows, LANES), jnp.bfloat16),
            jax.ShapeDtypeStruct((2 * count,), jnp.int32),
            jax.ShapeDtypeStruct((rows, LANES), jnp.float32),
        ],
        in_specs=[hbm, hbm, hbm],
        out_specs=[VMEM, SMEM, VMEM],
        scratch_shapes=[
            pltpu.SMEM(pairs.shape, jnp.int32),
            pltpu.SMEM(table.shape, jnp.int32),
            pltpu.VMEM(blocks.shape, jnp.bfloat16),
            pltpu.SMEM((SLABS,), jnp.int32),
            pltpu.SMEM((2 * count,), jnp.int32),
            pltpu.SemaphoreType.DMA((3,)),
        ],
        compiler_params=params(),
    )(pairs, table, blocks)


def chunk_base(message, per_slab, tiles):
    place, rank = lax.div(message, per_slab), lax.rem(message, per_slab)
    first = place * (per_slab * tiles + 1)
    return first + rank * tiles, first + per_slab * tiles, rank


def sort_kernel(origin_ref, arrived_ref, *out_refs):
    size, _, features = out_refs[0].shape
    tiles = features // LANES
    per_slab = len(GROUPS) * size // SLABS
    chunked = arrived_ref.shape[2] != features
    for place, out_ref in enumerate(out_refs):

        def body(index, carry, place=place, out_ref=out_ref):
            origin = origin_ref[place * size + index]
            if not chunked:
                out_ref[index] = arrived_ref[origin]
                return carry
            base, _, _ = chunk_base(origin, per_slab, tiles)
            for tile in range(tiles):
                out_ref[index, :, tile * LANES : (tile + 1) * LANES] = arrived_ref[base + tile]
            return carry

        lax.fori_loop(0, size, body, 0, unroll=4)


def sort_by_depth(arrived, origin, features):
    total, rows = origin.shape[0], arrived.shape[1]
    part = jax.ShapeDtypeStruct((total // len(GROUPS), rows, features), jnp.bfloat16)
    return pl.pallas_call(
        sort_kernel,
        out_shape=[part] * len(GROUPS),
        in_specs=[SMEM, VMEM],
        out_specs=[VMEM] * len(GROUPS),
        compiler_params=params(),
    )(origin, arrived)


def unsort_kernel(origin_ref, *refs):
    part_refs, out_ref, logs_ref = refs[:-2], refs[-2], refs[-1]
    size, rows, features = part_refs[0].shape
    size -= 1
    tiles = features // LANES
    total = len(GROUPS) * size
    per_slab = total // SLABS
    lane = lax.broadcasted_iota(jnp.int32, (rows, LANES), 1)
    halves = [lane < LANES // 2, lane >= LANES // 2]
    for place, part_ref in enumerate(part_refs):
        for index in range(size):
            origin = origin_ref[place * size + index]
            base, _, _ = chunk_base(origin, per_slab, tiles)
            for tile in range(tiles):
                out_ref[base + tile] = part_ref[index, :, tile * LANES : (tile + 1) * LANES]
            first = index // 2 * LANES
            terms = part_ref[size, :, first : first + LANES].astype(jnp.float32)
            logs_ref[origin] = jnp.where(halves[index % 2], terms, 0.0)
    slot = lane % (LANES // 2) // TERM_LANES

    def pack(place, carry):
        tile = logs_ref[place * per_slab]
        for rank in range(1, per_slab):
            tile = jnp.where(slot == rank, logs_ref[place * per_slab + rank], tile)
        out_ref[place * (per_slab * tiles + 1) + per_slab * tiles] = tile.astype(jnp.bfloat16)
        return carry

    lax.fori_loop(0, SLABS, pack, 0, unroll=4)


def unsort(parts, origin):
    size, rows, features = parts[0].shape
    total = origin.shape[0]
    chunk = total // SLABS * (features // LANES) + 1
    return pl.pallas_call(
        unsort_kernel,
        out_shape=jax.ShapeDtypeStruct((SLABS * chunk, rows, LANES), jnp.bfloat16),
        in_specs=[SMEM] + [VMEM] * len(GROUPS),
        out_specs=VMEM,
        scratch_shapes=[pltpu.VMEM((total, rows, LANES), jnp.float32)],
        compiler_params=params(),
    )(origin, *parts)


def products_of(flat, cluster):
    return lax.dot_general(
        flat, cluster, (((1,), (1,)), ((), ())), preferred_element_type=jnp.float32
    )


def weigh(products, norms):
    scores = (products - norms) * INV_WIDTH
    row_top = jnp.max(scores, axis=1, keepdims=True)
    weights = jnp.exp(scores - row_top)
    totals = jnp.sum(weights, axis=1, keepdims=True)
    log_weight = row_top + jnp.log(totals)
    first = log_weight.astype(jnp.bfloat16).astype(jnp.float32)
    rest = log_weight - first
    second = rest.astype(jnp.bfloat16).astype(jnp.float32)
    third = rest - second
    lane = lax.broadcasted_iota(jnp.int32, (products.shape[0], LANES), 1) % TERM_LANES
    terms = jnp.where(lane == 0, first, jnp.where(lane == 1, second, third))
    return weights.astype(jnp.bfloat16), totals, terms


def score_kernel(*refs):
    count = len(GROUPS)
    part_refs, refs = refs[:count], refs[count:]
    cluster_anys, refs = refs[:count], refs[count:]
    norm_refs, refs = refs[:count], refs[count:]
    out_refs, (clusters_ref, cluster_sems) = refs[:count], refs[count:]
    copies = [
        pltpu.make_async_copy(cluster_any, clusters_ref.at[index], cluster_sems.at[index])
        for index, cluster_any in enumerate(cluster_anys)
    ]
    for copy in copies:
        copy.start()
    size, rows, features = part_refs[0].shape
    half = size // 2
    lines = half * rows
    first_half = lax.broadcasted_iota(jnp.int32, (rows, LANES), 1) < LANES // 2
    members = [
        [(group, side) for group, pair in enumerate(GROUPS) for side in range(2) if pair[side] == cluster]
        for cluster in range(count)
    ]
    products = []
    for cluster in range(count):
        flat = jnp.concatenate(
            [
                part_refs[group][side * half : (side + 1) * half]
                .astype(jnp.float32)
                .reshape(lines, features)
                for group, side in members[cluster]
            ]
        ).astype(jnp.bfloat16)
        copies[cluster].wait()
        products.append(products_of(flat, clusters_ref[cluster]))
    for cluster in range(count):
        weights, totals, terms = weigh(products[cluster], norm_refs[cluster][...])
        summed = jnp.dot(weights, clusters_ref[cluster], preferred_element_type=jnp.float32)
        part = summed * (1.0 / totals)
        for place, (group, side) in enumerate(members[cluster]):
            first, out_ref = place * lines, out_refs[group]
            out_ref[side * half : (side + 1) * half] = (
                part[first : first + lines].reshape(half, rows, features).astype(jnp.bfloat16)
            )
            for index in range(0, half, 2):
                line = first + index * rows
                both = jnp.where(
                    first_half, terms[line : line + rows], terms[line + rows : line + 2 * rows]
                )
                lanes = (side * half + index) // 2 * LANES
                out_ref[size, :, lanes : lanes + LANES] = both.astype(jnp.bfloat16)


def score_parts(parts, clusters, norms):
    count = len(GROUPS)
    size, rows, features = parts[0].shape
    references = clusters[0].shape[0]
    total = count * size * rows
    out = jax.ShapeDtypeStruct((size + 1, rows, features), jnp.bfloat16)
    return pl.pallas_call(
        score_kernel,
        out_shape=[out] * count,
        in_specs=[VMEM] * count + [whole(pl.ANY)] * count + [VMEM] * count,
        out_specs=[VMEM] * count,
        scratch_shapes=[
            pltpu.VMEM((count, references, features), jnp.bfloat16),
            pltpu.SemaphoreType.DMA((count,)),
        ],
        compiler_params=params(),
        cost_estimate=pl.CostEstimate(
            flops=4 * total * references * features,
            bytes_accessed=2 * (2 * total * features + count * references * features),
            transcendentals=total * references,
        ),
    )(*parts, *clusters, *norms)


def combine_kernel(log_count, step, slots_ref, squares_ref, returned_ref, earlier_ref, *out_refs):
    density_ref, *out_refs = out_refs
    rows = squares_ref.shape[0]
    count = slots_ref.shape[0] // 2
    per_slab = 2 * count // SLABS
    tiles = (returned_ref.shape[0] // SLABS - 1) // per_slab
    row = lax.broadcasted_iota(jnp.int32, (rows, LANES), 0)
    lane = lax.broadcasted_iota(jnp.int32, (rows, LANES), 1)
    lane_slot = jnp.where(
        lane % TERM_LANES < TERMS, lane % (LANES // 2) // TERM_LANES, -1
    )
    last = len(out_refs) == 1
    squares = squares_ref[...]

    def read(slot):
        base, shared, rank = chunk_base(slot, per_slab, tiles)
        part = returned_ref[pl.ds(base, tiles)].astype(jnp.float32)
        terms = returned_ref[shared].astype(jnp.float32)
        terms = jnp.where(lane_slot == rank, terms, 0.0)
        return part, jnp.sum(terms, axis=1, keepdims=True)

    def body(block, carry):
        densities, next_squares = carry
        first_slot, second_slot = slots_ref[2 * block], slots_ref[2 * block + 1]
        first_part, first_log = read(first_slot)
        second_part, second_log = read(second_slot)
        both_top = jnp.maximum(first_log, second_log)
        first_share = jnp.exp(first_log - both_top)
        second_share = jnp.exp(second_log - both_top)
        pair_total = first_share + second_share
        inverse = 1.0 / pair_total
        mixed = (
            (first_share * inverse)[None] * first_part
            + (second_share * inverse)[None] * second_part
        ).astype(jnp.bfloat16)
        density = both_top + jnp.log(pair_total)
        densities = jnp.where(lane == block, density, densities)
        if last:
            for tile in range(tiles):
                out_refs[0][block, :, tile * LANES : (tile + 1) * LANES] = mixed[tile]
            return densities, next_squares
        for tile in range(tiles):
            lanes = slice(tile * LANES, (tile + 1) * LANES)
            out_refs[0][first_slot, :, lanes] = mixed[tile]
            out_refs[0][second_slot, :, lanes] = mixed[tile]
        total = jnp.sum(jnp.square(mixed.astype(jnp.float32)), axis=0)
        total = jnp.sum(total, axis=1, keepdims=True)
        return densities, jnp.where(lane == block, total, next_squares)

    zeros = jnp.zeros((rows, LANES), jnp.float32)
    densities, next_squares = lax.fori_loop(0, count, body, (zeros, zeros), unroll=4)
    if not last:
        out_refs[1][...] = next_squares
    densities = densities - 0.5 * INV_WIDTH * squares - log_count
    blocks_wide = LANES // rows
    for wide in range(count // blocks_wide):
        spread = zeros
        for index in range(blocks_wide):
            block = wide * blocks_wide + index
            column = densities[:, block : block + 1]
            spread = jnp.where(lane == index * rows + row, column, spread)
        line = jnp.sum(
            jnp.where(lane % rows == row, spread, 0.0), axis=0, keepdims=True
        )
        lanes = slice(wide * LANES, (wide + 1) * LANES)
        for other in range(density_ref.shape[0]):
            if other == step:
                density_ref[other : other + 1, lanes] = line
            else:
                density_ref[other : other + 1, lanes] = earlier_ref[other : other + 1, lanes]


def combine(squares, returned, slots, earlier, log_count, step, features):
    rows = squares.shape[0]
    total = slots.shape[0]
    outs = [jax.ShapeDtypeStruct(earlier.shape, jnp.float32)]
    if step == STEPS - 1:
        outs.append(jax.ShapeDtypeStruct((total // 2, rows, features), jnp.bfloat16))
    else:
        outs.append(jax.ShapeDtypeStruct((total, rows, features), jnp.bfloat16))
        outs.append(jax.ShapeDtypeStruct(squares.shape, jnp.float32))
    return pl.pallas_call(
        functools.partial(combine_kernel, log_count, step),
        out_shape=outs,
        in_specs=[SMEM, VMEM, VMEM, VMEM],
        out_specs=[VMEM] * len(outs),
        compiler_params=params(),
    )(slots, squares, returned, earlier)


def half_norms_of(cluster_rows):
    return 0.5 * jnp.sum(jnp.square(cluster_rows.astype(jnp.float32)), axis=1)[None, :]


def sorted_origins(arrived, total, depth, core):
    chunks = arrived.reshape(SLABS, -1, *arrived.shape[1:])
    targets = chunks[:, -1, 0, : total // SLABS].reshape(-1).astype(jnp.int32)
    order = jnp.arange(total, dtype=jnp.int32)
    earlier = (targets[:, None] == targets[None, :]) & (order[None, :] < order[:, None])
    rank = jnp.sum(earlier.astype(jnp.int32), axis=1)
    side = (targets % CORES) ^ core
    ahead = targets // CORES - depth
    ahead = jnp.where(core == 0, ahead, -ahead) % DEPTH
    half = sum(
        jnp.where((side == at) & (ahead == steps), HALVES[at][steps], 0)
        for at in range(CORES)
        for steps in range(DEPTH)
    )
    slot = half * (total // CLUSTER_DEVICES) + rank
    return jnp.sum(jnp.where(slot[None, :] == order[:, None], order[None, :], 0), axis=1)


def local(queries, corpus, block_pairs, owner_table):
    features = queries.shape[2]
    cluster_index = lax.axis_index("cluster").astype(jnp.int32)
    depth, core = cluster_index // CORES, cluster_index % CORES
    own = corpus[0]
    ahead = send_ahead(own, -1)
    other = swap_cores(own)
    log_count = math.log(2.0 * own.shape[0])
    outgoing, slots, squares = fill(queries, block_pairs.T, owner_table)
    densities = jnp.zeros((STEPS, queries.shape[0] * queries.shape[1]), jnp.float32)
    for step in range(STEPS):
        arrived = exchange_slabs(outgoing)
        if step == 0:
            ahead, arrived = lax.optimization_barrier((ahead, arrived))
            clusters = (own, other, ahead, swap_cores(ahead))
            norms = [half_norms_of(cluster) for cluster in clusters]
            origin = sorted_origins(arrived, slots.shape[0], depth, core)
        parts = list(sort_by_depth(arrived, origin, features))
        parts[STAY:] = [send_ahead(parts[STAY], 1), send_ahead(parts[STAY + 1], -1)]
        answers = list(score_parts(parts, clusters, norms))
        answers[STAY:] = [send_ahead(answers[STAY], -1), send_ahead(answers[STAY + 1], 1)]
        returned = exchange_slabs(unsort(answers, origin))
        densities, outgoing, *squares_next = combine(
            squares, returned, slots, densities, log_count, step, features
        )
        squares = squares_next[0] if squares_next else None
    return (outgoing, densities)


def solution(mesh):
    return jax.shard_map(
        local,
        mesh=mesh,
        in_specs=(
            P(("cluster", "slab"), None, None),
            P(("cluster", "slab"), None, None),
            P(("cluster", "slab"), None),
            P(),
        ),
        out_specs=(P(("cluster", "slab"), None, None), P(None, ("cluster", "slab"))),
        check_vma=False,
    )
```

time: 161 us -> 151 us (0.938)
  waiting for transfers between devices: 51.4 us -> 36.7 us
  other arithmetic: 2.88 us -> 7.02 us
  Pallas kernels: 20 us -> 22.7 us
  local copies, waits for them, and re-layouts: 2.84 us -> 1.07 us
    ppermute x12 -> x9, waiting for transfers between devices: 39 us -> 21.6 us  [send_ahead(): return lax.ppermute(array, AXES, pairs)]
    reduce_sum x2 -> x4, other arithmetic: 2.54 us -> 6.68 us  [half_norms_of(): jnp.sum(jnp.square(cluster_rows.astype(jnp.float32)), axis=1)[None, :]]
    pallas_call x6, Pallas kernels: 14.7 us -> 18.1 us  [the longest x2 11.5 us: score_parts(): pl.pallas_call(score_kernel, out_shape=[out] * count, in_specs=[VMEM] * c...]
    all_to_all x1, waiting for transfers between devices: 12.3 us -> 15 us  [exchange_slabs(): lax.all_to_all(array, AXES, split_axis=0, concat_axis=0, tiled=True, axis...]
    ppermute x12 -> x9, starting transfers between devices: 18.7 us -> 16.7 us  [send_ahead(): return lax.ppermute(array, AXES, pairs)]
    all_to_all x1, starting transfers between devices: 5.13 us -> 7.03 us  [exchange_slabs(): lax.all_to_all(array, AXES, split_axis=0, concat_axis=0, tiled=True, axis...]
  transfers between devices with their start and end apart: 14 -> 12, of which waited for: 10 -> 6; matrix products, arithmetic and copies ran while one was open for 2% -> 5% of each run, Pallas kernels for 1% -> 3%
where the time goes in v6:
time: 151 us; the launch traced here: 150 us
  blocking collectives  58.3 us (39%)
  waiting for transfers between devices  36.7 us (24%)
  starting transfers between devices  23.8 us (16%)
  Pallas kernels  22.7 us (15%)
  other arithmetic  7.02 us (5%)
    all_to_all x3, blocking collectives, exchange_slabs(): lax.all_to_all(array, AXES, split_axis=0, concat_axis=0, tiled=True, axis...  58.3 us
    ppermute x9, waiting for transfers between devices, send_ahead(): return lax.ppermute(array, AXES, pairs)  21.6 us
    ppermute x9, starting transfers between devices, send_ahead(): return lax.ppermute(array, AXES, pairs)  16.7 us
    all_to_all x1, waiting for transfers between devices, exchange_slabs(): lax.all_to_all(array, AXES, split_axis=0, concat_axis=0, tiled=True, axis...  15 us
    pallas_call x2, Pallas kernels, score_parts(): pl.pallas_call(score_kernel, out_shape=[out] * count, in_specs=[VMEM] * c...  11.5 us
    all_to_all x1, starting transfers between devices, exchange_slabs(): lax.all_to_all(array, AXES, split_axis=0, concat_axis=0, tiled=True, axis...  7.03 us
    reduce_sum x4, other arithmetic, half_norms_of(): jnp.sum(jnp.square(cluster_rows.astype(jnp.float32)), axis=1)[None, :]  6.68 us
    pallas_call x2, Pallas kernels, combine(): pl.pallas_call(functools.partial(combine_kernel, log_count, step), out_sh...  4.93 us
  transfers between devices with their start and end apart: 12, of which 6 were waited for; matrix products, arithmetic and copies ran while one was open for 5% of the time, Pallas kernels for 3%

profile of v6, /device:TPU:0, one launch (start us, length us, event | category | flops | bytes accessed | tf_op | source)
XLA Modules:
  0.0 150.4 jit_solution(15364531569918743571)
XLA Ops:
  0.6 0.0 copy-start
  0.6 4.2 %collective-permute-start = (bf16[1024,1024]{1,0:T(8,128)(2,1)}, bf16[1024,1024]{1,0:T(8,128)(2,1)}, u32[]{:S(2)}, u32[]{:S(2)}) collective-permute-start(bf16[1024,1024]{1,0:T(8,128)(2,1)} %bitcast.12), channel_id=1, source_target_pairs={{0,96},{1,97},{2,98},{3,99},{4,100},{5,101},{6,102},{7,103},{8,104... | collective-permute-start | bytes 6291464 | tf_op jit(solution)/shard_map/ppermute | solution.py:56
  4.8 3.0 %shard_map.59 = (bf16[528,8,128]{2,1,0:T(8,128)(2,1)S(1)}, s32[64]{0:T(128)S(1)}, f32[8,128]{1,0:T(8,128)S(1)}) custom-call(s32[2,32]{1,0:T(2,128)} %bitcast.25, s32[128]{0:T(128)} %table_hbm.1, bf16[32,8,1024]{2,1,0:T(8,128)(2,1)} %blocks_hbm.1), custom_call_target="tpu_custom_call" | custom-call | tf_op jit(solution)/shard_map/pallas_call | solution.py:151
  7.8 0.0 copy-start.1
  7.8 1.0 copy-done.1
  8.8 7.0 %all-to-all-start = ((bf16[528,8,128]{2,1,0:T(8,128)(2,1)}), bf16[528,8,128]{2,1,0:T(8,128)(2,1)S(1)}, u32[]{:S(2)}, u32[]{:S(2)}) async-start(bf16[528,8,128]{2,1,0:T(8,128)(2,1)} %copy-done.1), calls=%async_computation | async-start | bytes 2162688 | tf_op jit(solution)/shard_map/all_to_all | solution.py:42
  15.8 0.0 copy-done
  15.8 0.1 collective-permute-start.3
  15.9 15.0 %all-to-all-done.arrived_ref = bf16[528,8,128]{2,1,0:T(8,128)(2,1)S(1)} async-done(((bf16[528,8,128]{2,1,0:T(8,128)(2,1)}), bf16[528,8,128]{2,1,0:T(8,128)(2,1)S(1)}, u32[]{:S(2)}, u32[]{:S(2)}) %all-to-all-start) | async-done | bytes 1081376 | tf_op jit(solution)/shard_map/all_to_all | solution.py:42
  30.9 0.0 collective-permute-done.refs_6_
  30.9 0.0 collective-permute-start.4
  30.9 0.5 multiply_reduce_fusion.3
  31.5 0.1 reshape.134
  31.5 0.2 convert_reduce_fusion
  31.8 0.1 select_reduce_fusion.origin_ref
  31.9 0.9 shard_map.60
  32.8 1.3 collective-permute-start.1
  34.1 2.0 %collective-permute-start.2 = (bf16[16,8,1024]{2,1,0:T(8,128)(2,1)S(1)}, bf16[16,8,1024]{2,1,0:T(8,128)(2,1)S(1)}, u32[]{:S(2)}, u32[]{:S(2)}) collective-permute-start(bf16[16,8,1024]{2,1,0:T(8,128)(2,1)S(1)} %get-tuple-element.35), channel_id=1, source_target_pairs={{0,96},{1,97},{2,98},{3,99},{4,100},{5,101},{6,102},{7,103},{8,104... | collective-permute-start | bytes 786440 | tf_op jit(solution)/shard_map/ppermute | solution.py:56
  36.1 0.0 collective-permute-done.3.refs_5_
  36.1 2.1 %multiply_reduce_fusion.2 = f32[1024]{0:T(1024)S(1)} fusion(bf16[1024,1024]{1,0:T(8,128)(2,1)} %collective-permute-done.3.refs_5_), kind=kLoop, calls=%fused_computation.2 | loop fusion | flops 3144704 | bytes 2101248 | tf_op jit(solution)/shard_map/reduce_sum | solution.py:440
  38.2 2.1 %multiply_reduce_fusion.1 = f32[1024]{0:T(1024)S(1)} fusion(bf16[1024,1024]{1,0:T(8,128)(2,1)} %collective-permute-done.refs_6_), kind=kLoop, calls=%fused_computation.1 | loop fusion | flops 3144704 | bytes 2101248 | tf_op jit(solution)/shard_map/reduce_sum | solution.py:440
  40.3 0.0 collective-permute-done.4.refs_7_
  40.3 2.1 %multiply_reduce_fusion = f32[1024]{0:T(1024)S(1)} fusion(bf16[1024,1024]{1,0:T(8,128)(2,1)} %collective-permute-done.4.refs_7_), kind=kLoop, calls=%fused_computation | loop fusion | flops 3144704 | bytes 2101248 | tf_op jit(solution)/shard_map/reduce_sum | solution.py:440
  42.4 0.0 collective-permute-done.1.refs_2_
  42.4 0.0 collective-permute-done.2.refs_3_
  42.4 5.8 %shard_map.61 = (bf16[17,8,1024]{2,1,0:T(8,128)(2,1)S(1)}, bf16[17,8,1024]{2,1,0:T(8,128)(2,1)S(1)}, bf16[17,8,1024]{2,1,0:T(8,128)(2,1)S(1)}, bf16[17,8,1024]{2,1,0:T(8,128)(2,1)S(1)}) custom-call(bf16[16,8,1024]{2,1,0:T(8,128)(2,1)S(1)} %get-tuple-element.32.refs_0_, bf16[16,8,1024]{2,1,0:T(8,128)(2,1)S(1)} %get-tuple-element.33.refs_1_, ...), custom_call_target="tpu_custom_call" | custom-call | flops 2147483648 | bytes 10485760 | tf_op jit(solution)/shard_map/pallas_call | solution.py:331
  48.2 2.2 %collective-permute-start.5 = (bf16[17,8,1024]{2,1,0:T(8,128)(2,1)S(1)}, bf16[17,8,1024]{2,1,0:T(8,128)(2,1)S(1)}, u32[]{:S(2)}, u32[]{:S(2)}) collective-permute-start(bf16[17,8,1024]{2,1,0:T(8,128)(2,1)S(1)} %get-tuple-element.39), channel_id=1, source_target_pairs={{0,96},{1,97},{2,98},{3,99},{4,100},{5,101},{6,102},{7,103},{8,104... | collective-permute-start | bytes 835592 | tf_op jit(solution)/shard_map/ppermute | solution.py:56
  50.3 0.0 collective-permute-start.6
  50.3 7.2 %collective-permute-done.5.refs_2_ = bf16[17,8,1024]{2,1,0:T(8,128)(2,1)S(1)} collective-permute-done((bf16[17,8,1024]{2,1,0:T(8,128)(2,1)S(1)}, bf16[17,8,1024]{2,1,0:T(8,128)(2,1)S(1)}, u32[]{:S(2)}, u32[]{:S(2)}) %collective-permute-start.5) | collective-permute-done | bytes 278560 | tf_op jit(solution)/shard_map/ppermute | solution.py:56
  57.6 1.1 collective-permute-done.6.refs_3_
  58.7 0.9 shard_map.62
  59.5 21.6 %all_to_all.20.returned_ref = bf16[528,8,128]{2,1,0:T(8,128)(2,1)S(1)} all-to-all(bf16[528,8,128]{2,1,0:T(8,128)(2,1)S(1)} %shard_map.62), channel_id=1, replica_groups={{0,5,10,15,1,6,11,12,2,7,8,13,3,4,9,14},{16,21,26,31,20,25,30,19,24,29,..., dimensions={0} | all-to-all | bytes 2162688 | tf_op jit(solution)/shard_map/all_to_all | solution.py:42
  81.1 2.5 %shard_map.63 = (f32[2,256]{1,0:T(2,128)S(1)}, bf16[64,8,1024]{2,1,0:T(8,128)(2,1)S(1)}, f32[8,128]{1,0:T(8,128)S(1)}) custom-call(s32[64]{0:T(128)S(1)} %get-tuple-element.28.slots_ref, f32[8,128]{1,0:T(8,128)S(1)} %get-tuple-element.29.squares_ref, bf16[528,8,128]{2,1,0:T(8,128)(2,1)S(1)} %all_to_all.20.returned_ref, f32[2,256]{1,0:T(2,128)S(1)} %broadcast_in_dim.52.earlier_ref), custom_call_target="tpu_custom_call" | custom-call | tf_op jit(solution)/shard_map/pallas_call | solution.py:430
  83.6 16.4 %all_to_all.21.arrived_ref = bf16[64,8,1024]{2,1,0:T(8,128)(2,1)S(1)} all-to-all(bf16[64,8,1024]{2,1,0:T(8,128)(2,1)S(1)} %get-tuple-element.42), channel_id=1, replica_groups={{0,5,10,15,1,6,11,12,2,7,8,13,3,4,9,14},{16,21,26,31,20,25,30,19,24,29,..., dimensions={0} | all-to-all | bytes 2097152 | tf_op jit(solution)/shard_map/all_to_all | solution.py:42
  100.0 0.7 shard_map.64
  100.7 2.5 %collective-permute-start.7 = (bf16[16,8,1024]{2,1,0:T(8,128)(2,1)S(1)}, bf16[16,8,1024]{2,1,0:T(8,128)(2,1)S(1)}, u32[]{:S(2)}, u32[]{:S(2)}) collective-permute-start(bf16[16,8,1024]{2,1,0:T(8,128)(2,1)S(1)} %get-tuple-element.45), channel_id=1, source_target_pairs={{0,32},{1,33},{2,34},{3,35},{4,36},{5,37},{6,38},{7,39},{8,40},{9,... | collective-permute-start | bytes 786440 | tf_op jit(solution)/shard_map/ppermute | solution.py:56
  103.2 2.4 %collective-permute-start.8 = (bf16[16,8,1024]{2,1,0:T(8,128)(2,1)S(1)}, bf16[16,8,1024]{2,1,0:T(8,128)(2,1)S(1)}, u32[]{:S(2)}, u32[]{:S(2)}) collective-permute-start(bf16[16,8,1024]{2,1,0:T(8,128)(2,1)S(1)} %get-tuple-element.46), channel_id=1, source_target_pairs={{0,96},{1,97},{2,98},{3,99},{4,100},{5,101},{6,102},{7,103},{8,104... | collective-permute-start | bytes 786440 | tf_op jit(solution)/shard_map/ppermute | solution.py:56
  105.6 5.5 %collective-permute-done.7.refs_2_ = bf16[16,8,1024]{2,1,0:T(8,128)(2,1)S(1)} collective-permute-done((bf16[16,8,1024]{2,1,0:T(8,128)(2,1)S(1)}, bf16[16,8,1024]{2,1,0:T(8,128)(2,1)S(1)}, u32[]{:S(2)}, u32[]{:S(2)}) %collective-permute-start.7) | collective-permute-done | bytes 262176 | tf_op jit(solution)/shard_map/ppermute | solution.py:56
  111.2 0.0 collective-permute-done.8.refs_3_
  111.2 5.8 %shard_map.65 = (bf16[17,8,1024]{2,1,0:T(8,128)(2,1)S(1)}, bf16[17,8,1024]{2,1,0:T(8,128)(2,1)S(1)}, bf16[17,8,1024]{2,1,0:T(8,128)(2,1)S(1)}, bf16[17,8,1024]{2,1,0:T(8,128)(2,1)S(1)}) custom-call(bf16[16,8,1024]{2,1,0:T(8,128)(2,1)S(1)} %get-tuple-element.43.refs_0_, bf16[16,8,1024]{2,1,0:T(8,128)(2,1)S(1)} %get-tuple-element.44.refs_1_, ...), custom_call_target="tpu_custom_call" | custom-call | flops 2147483648 | bytes 10485760 | tf_op jit(solution)/shard_map/pallas_call | solution.py:331
  117.0 2.1 %collective-permute-start.9 = (bf16[17,8,1024]{2,1,0:T(8,128)(2,1)S(1)}, bf16[17,8,1024]{2,1,0:T(8,128)(2,1)S(1)}, u32[]{:S(2)}, u32[]{:S(2)}) collective-permute-start(bf16[17,8,1024]{2,1,0:T(8,128)(2,1)S(1)} %get-tuple-element.49), channel_id=1, source_target_pairs={{0,96},{1,97},{2,98},{3,99},{4,100},{5,101},{6,102},{7,103},{8,104... | collective-permute-start | bytes 835592 | tf_op jit(solution)/shard_map/ppermute | solution.py:56
  119.1 0.0 collective-permute-start.10
  119.1 5.7 %collective-permute-done.9.refs_2_ = bf16[17,8,1024]{2,1,0:T(8,128)(2,1)S(1)} collective-permute-done((bf16[17,8,1024]{2,1,0:T(8,128)(2,1)S(1)}, bf16[17,8,1024]{2,1,0:T(8,128)(2,1)S(1)}, u32[]{:S(2)}, u32[]{:S(2)}) %collective-permute-start.9) | collective-permute-done | bytes 278560 | tf_op jit(solution)/shard_map/ppermute | solution.py:56
  124.8 2.1 %collective-permute-done.10.refs_3_ = bf16[17,8,1024]{2,1,0:T(8,128)(2,1)S(1)} collective-permute-done((bf16[17,8,1024]{2,1,0:T(8,128)(2,1)S(1)}, bf16[17,8,1024]{2,1,0:T(8,128)(2,1)S(1)}, u32[]{:S(2)}, u32[]{:S(2)}) %collective-permute-start.10) | collective-permute-done | bytes 278560 | tf_op jit(solution)/shard_map/ppermute | solution.py:56
  126.8 0.9 shard_map.66
  127.7 20.3 %all_to_all.22.returned_ref = bf16[528,8,128]{2,1,0:T(8,128)(2,1)S(1)} all-to-all(bf16[528,8,128]{2,1,0:T(8,128)(2,1)S(1)} %shard_map.66), channel_id=1, replica_groups={{0,5,10,15,1,6,11,12,2,7,8,13,3,4,9,14},{16,21,26,31,20,25,30,19,24,29,..., dimensions={0} | all-to-all | bytes 2162688 | tf_op jit(solution)/shard_map/all_to_all | solution.py:42
  148.0 2.4 %shard_map.67 = (f32[2,256]{1,0:T(2,128)}, bf16[32,8,1024]{2,1,0:T(8,128)(2,1)}) custom-call(s32[64]{0:T(128)S(1)} %get-tuple-element.28.slots_ref, f32[8,128]{1,0:T(8,128)S(1)} %get-tuple-element.41.squares_ref, bf16[528,8,128]{2,1,0:T(8,128)(2,1)S(1)} %all_to_all.22.returned_ref, f32[2,256]{1,0:T(2,128)S(1)} %get-tuple-element.51.earlier_ref), custom_call_target="tpu_custom_call" | custom-call | tf_op jit(solution)/shard_map/pallas_call | solution.py:430
  (8 shorter events, 0.1 us)
Async XLA Ops:
  0.6 15.2 %copy-start = (bf16[1,1024,1024]{2,1,0:T(8,128)(2,1)S(1)}, bf16[1,1024,1024]{2,1,0:T(8,128)(2,1)}, u32[]{:S(2)}) copy-start(bf16[1,1024,1024]{2,1,0:T(8,128)(2,1)} %param.5) | copy-start | bytes 6291460
  0.6 30.3 %collective-permute-start = (bf16[1024,1024]{1,0:T(8,128)(2,1)}, bf16[1024,1024]{1,0:T(8,128)(2,1)}, u32[]{:S(2)}, u32[]{:S(2)}) collective-permute-start(bf16[1024,1024]{1,0:T(8,128)(2,1)} %bitcast.12), channel_id=1, source_target_pairs={{0,96},{1,97},{2,98},{3,99},{4,100},{5,101},{6,102},{7,103},{8,104... | collective-permute-start | bytes 6291464 | tf_op jit(solution)/shard_map/ppermute | solution.py:56
  7.8 1.0 copy-start.1
  8.8 22.2 %all-to-all-start = ((bf16[528,8,128]{2,1,0:T(8,128)(2,1)}), bf16[528,8,128]{2,1,0:T(8,128)(2,1)S(1)}, u32[]{:S(2)}, u32[]{:S(2)}) async-start(bf16[528,8,128]{2,1,0:T(8,128)(2,1)} %copy-done.1), calls=%async_computation | async-start | bytes 2162688 | tf_op jit(solution)/shard_map/all_to_all | solution.py:42
  15.8 20.3 %collective-permute-start.3 = (bf16[1024,1024]{1,0:T(8,128)(2,1)S(1)}, bf16[1024,1024]{1,0:T(8,128)(2,1)}, u32[]{:S(2)}, u32[]{:S(2)}) collective-permute-start(bf16[1024,1024]{1,0:T(8,128)(2,1)S(1)} %bitcast.13), channel_id=1, source_target_pairs={{0,16},{1,17},{2,18},{3,19},{4,20},{5,21},{6,22},{7,23},{8,24},{9,... | collective-permute-start | bytes 6291464 | tf_op jit(solution)/shard_map/ppermute | solution.py:64
  30.9 9.3 %collective-permute-start.4 = (bf16[1024,1024]{1,0:T(8,128)(2,1)}, bf16[1024,1024]{1,0:T(8,128)(2,1)}, u32[]{:S(2)}, u32[]{:S(2)}) collective-permute-start(bf16[1024,1024]{1,0:T(8,128)(2,1)} %collective-permute-done.refs_6_), channel_id=1, source_target_pairs={{0,16},{1,17},{2,18},{3,19},{4,20},{5,21},{6,22},{7,23},{8,24},{9,... | collective-permute-start | bytes 6291464 | tf_op jit(solution)/shard_map/ppermute | solution.py:64
  32.8 9.6 %collective-permute-start.1 = (bf16[16,8,1024]{2,1,0:T(8,128)(2,1)S(1)}, bf16[16,8,1024]{2,1,0:T(8,128)(2,1)S(1)}, u32[]{:S(2)}, u32[]{:S(2)}) collective-permute-start(bf16[16,8,1024]{2,1,0:T(8,128)(2,1)S(1)} %get-tuple-element.34), channel_id=1, source_target_pairs={{0,32},{1,33},{2,34},{3,35},{4,36},{5,37},{6,38},{7,39},{8,40},{9,... | collective-permute-start | bytes 786440 | tf_op jit(solution)/shard_map/ppermute | solution.py:56
  34.1 8.3 %collective-permute-start.2 = (bf16[16,8,1024]{2,1,0:T(8,128)(2,1)S(1)}, bf16[16,8,1024]{2,1,0:T(8,128)(2,1)S(1)}, u32[]{:S(2)}, u32[]{:S(2)}) collective-permute-start(bf16[16,8,1024]{2,1,0:T(8,128)(2,1)S(1)} %get-tuple-element.35), channel_id=1, source_target_pairs={{0,96},{1,97},{2,98},{3,99},{4,100},{5,101},{6,102},{7,103},{8,104... | collective-permute-start | bytes 786440 | tf_op jit(solution)/shard_map/ppermute | solution.py:56
  48.2 9.4 %collective-permute-start.5 = (bf16[17,8,1024]{2,1,0:T(8,128)(2,1)S(1)}, bf16[17,8,1024]{2,1,0:T(8,128)(2,1)S(1)}, u32[]{:S(2)}, u32[]{:S(2)}) collective-permute-start(bf16[17,8,1024]{2,1,0:T(8,128)(2,1)S(1)} %get-tuple-element.39), channel_id=1, source_target_pairs={{0,96},{1,97},{2,98},{3,99},{4,100},{5,101},{6,102},{7,103},{8,104... | collective-permute-start | bytes 835592 | tf_op jit(solution)/shard_map/ppermute | solution.py:56
  50.3 8.3 %collective-permute-start.6 = (bf16[17,8,1024]{2,1,0:T(8,128)(2,1)S(1)}, bf16[17,8,1024]{2,1,0:T(8,128)(2,1)S(1)}, u32[]{:S(2)}, u32[]{:S(2)}) collective-permute-start(bf16[17,8,1024]{2,1,0:T(8,128)(2,1)S(1)} %get-tuple-element.40), channel_id=1, source_target_pairs={{0,32},{1,33},{2,34},{3,35},{4,36},{5,37},{6,38},{7,39},{8,40},{9,... | collective-permute-start | bytes 835592 | tf_op jit(solution)/shard_map/ppermute | solution.py:56
  100.7 10.4 %collective-permute-start.7 = (bf16[16,8,1024]{2,1,0:T(8,128)(2,1)S(1)}, bf16[16,8,1024]{2,1,0:T(8,128)(2,1)S(1)}, u32[]{:S(2)}, u32[]{:S(2)}) collective-permute-start(bf16[16,8,1024]{2,1,0:T(8,128)(2,1)S(1)} %get-tuple-element.45), channel_id=1, source_target_pairs={{0,32},{1,33},{2,34},{3,35},{4,36},{5,37},{6,38},{7,39},{8,40},{9,... | collective-permute-start | bytes 786440 | tf_op jit(solution)/shard_map/ppermute | solution.py:56
  103.2 8.0 %collective-permute-start.8 = (bf16[16,8,1024]{2,1,0:T(8,128)(2,1)S(1)}, bf16[16,8,1024]{2,1,0:T(8,128)(2,1)S(1)}, u32[]{:S(2)}, u32[]{:S(2)}) collective-permute-start(bf16[16,8,1024]{2,1,0:T(8,128)(2,1)S(1)} %get-tuple-element.46), channel_id=1, source_target_pairs={{0,96},{1,97},{2,98},{3,99},{4,100},{5,101},{6,102},{7,103},{8,104... | collective-permute-start | bytes 786440 | tf_op jit(solution)/shard_map/ppermute | solution.py:56
  117.0 7.8 %collective-permute-start.9 = (bf16[17,8,1024]{2,1,0:T(8,128)(2,1)S(1)}, bf16[17,8,1024]{2,1,0:T(8,128)(2,1)S(1)}, u32[]{:S(2)}, u32[]{:S(2)}) collective-permute-start(bf16[17,8,1024]{2,1,0:T(8,128)(2,1)S(1)} %get-tuple-element.49), channel_id=1, source_target_pairs={{0,96},{1,97},{2,98},{3,99},{4,100},{5,101},{6,102},{7,103},{8,104... | collective-permute-start | bytes 835592 | tf_op jit(solution)/shard_map/ppermute | solution.py:56
  119.1 7.8 %collective-permute-start.10 = (bf16[17,8,1024]{2,1,0:T(8,128)(2,1)S(1)}, bf16[17,8,1024]{2,1,0:T(8,128)(2,1)S(1)}, u32[]{:S(2)}, u32[]{:S(2)}) collective-permute-start(bf16[17,8,1024]{2,1,0:T(8,128)(2,1)S(1)} %get-tuple-element.50), channel_id=1, source_target_pairs={{0,32},{1,33},{2,34},{3,35},{4,36},{5,37},{6,38},{7,39},{8,40},{9,... | collective-permute-start | bytes 835592 | tf_op jit(solution)/shard_map/ppermute | solution.py:56

commit v7 on v6

--- a/solution.py
+++ b/solution.py
@@ -112,7 +112,7 @@
             targets_ref[slot] = lax.div(entry, SLABS)
         return carry
 
-    lax.fori_loop(0, count, assign, 0, unroll=4)
+    lax.fori_loop(0, count, assign, 0, unroll=8)
     inputs[2].wait()
     lane = lax.broadcasted_iota(jnp.int32, (rows, LANES), 1)
 
@@ -127,7 +127,7 @@
         return jnp.where(lane == block, jnp.sum(total, axis=1, keepdims=True), squares)
 
     squares_ref[...] = lax.fori_loop(
-        0, count, put, jnp.zeros((rows, LANES), jnp.float32), unroll=4
+        0, count, put, jnp.zeros((rows, LANES), jnp.float32), unroll=8
     )
 
     def note(place, carry):
@@ -138,7 +138,7 @@
         out_ref[place * (per_slab * tiles + 1) + per_slab * tiles] = tile
         return carry
 
-    lax.fori_loop(0, SLABS, note, 0, unroll=4)
+    lax.fori_loop(0, SLABS, note, 0, unroll=16)
 
 
 def fill(blocks, pairs, table):
@@ -192,7 +192,7 @@
                 out_ref[index, :, tile * LANES : (tile + 1) * LANES] = arrived_ref[base + tile]
             return carry
 
-        lax.fori_loop(0, size, body, 0, unroll=4)
+        lax.fori_loop(0, size, body, 0, unroll=16)
 
 
 def sort_by_depth(arrived, origin, features):
@@ -234,7 +234,7 @@
         out_ref[place * (per_slab * tiles + 1) + per_slab * tiles] = tile.astype(jnp.bfloat16)
         return carry
 
-    lax.fori_loop(0, SLABS, pack, 0, unroll=4)
+    lax.fori_loop(0, SLABS, pack, 0, unroll=16)
 
 
 def unsort(parts, origin):
@@ -396,7 +396,7 @@
         return densities, jnp.where(lane == block, total, next_squares)
 
     zeros = jnp.zeros((rows, LANES), jnp.float32)
-    densities, next_squares = lax.fori_loop(0, count, body, (zeros, zeros), unroll=4)
+    densities, next_squares = lax.fori_loop(0, count, body, (zeros, zeros), unroll=16)
     if not last:
         out_refs[1][...] = next_squares
     densities = densities - 0.5 * INV_WIDTH * squares - log_count

time: 151 us -> 149 us (0.987)
  Pallas kernels: 22.7 us -> 20.5 us
    pallas_call x2, Pallas kernels: 4.93 us -> 3.34 us  [combine(): pl.pallas_call(functools.partial(combine_kernel, log_count, step), out_sh...]
  transfers between devices with their start and end apart: 12 -> 12, of which waited for: 6 -> 6; matrix products, arithmetic and copies ran while one was open for 5% -> 5% of each run, Pallas kernels for 3% -> 2%
where the time goes in v7:
time: 149 us
  blocking collectives  58.7 us (39%)
  waiting for transfers between devices  36.5 us (24%)
  starting transfers between devices  24 us (16%)
  Pallas kernels  20.5 us (14%)
  other arithmetic  7.02 us (5%)
    all_to_all x3, blocking collectives, exchange_slabs(): lax.all_to_all(array, AXES, split_axis=0, concat_axis=0, tiled=True, axis...  58.7 us
    ppermute x9, waiting for transfers between devices, send_ahead(): return lax.ppermute(array, AXES, pairs)  21.5 us
    ppermute x9, starting transfers between devices, send_ahead(): return lax.ppermute(array, AXES, pairs)  16.9 us
    all_to_all x1, waiting for transfers between devices, exchange_slabs(): lax.all_to_all(array, AXES, split_axis=0, concat_axis=0, tiled=True, axis...  15 us
    pallas_call x2, Pallas kernels, score_parts(): pl.pallas_call(score_kernel, out_shape=[out] * count, in_specs=[VMEM] * c...  11.5 us
    all_to_all x1, starting transfers between devices, exchange_slabs(): lax.all_to_all(array, AXES, split_axis=0, concat_axis=0, tiled=True, axis...  7.03 us
    reduce_sum x4, other arithmetic, half_norms_of(): jnp.sum(jnp.square(cluster_rows.astype(jnp.float32)), axis=1)[None, :]  6.68 us
    pallas_call x2, Pallas kernels, combine(): pl.pallas_call(functools.partial(combine_kernel, log_count, step), out_sh...  3.34 us
  transfers between devices with their start and end apart: 12, of which 6 were waited for; matrix products, arithmetic and copies ran while one was open for 5% of the time, Pallas kernels for 2%

profile of v7, /device:TPU:0, one launch (start us, length us, event | category | flops | bytes accessed | tf_op | source)
XLA Modules:
  0.0 148.6 jit_solution(4314773111051370707)
XLA Ops:
  0.6 0.0 copy-start
  0.6 4.2 %collective-permute-start = (bf16[1024,1024]{1,0:T(8,128)(2,1)}, bf16[1024,1024]{1,0:T(8,128)(2,1)}, u32[]{:S(2)}, u32[]{:S(2)}) collective-permute-start(bf16[1024,1024]{1,0:T(8,128)(2,1)} %bitcast.12), channel_id=1, source_target_pairs={{0,96},{1,97},{2,98},{3,99},{4,100},{5,101},{6,102},{7,103},{8,104... | collective-permute-start | bytes 6291464 | tf_op jit(solution)/shard_map/ppermute | solution.py:56
  4.8 2.5 %shard_map.59 = (bf16[528,8,128]{2,1,0:T(8,128)(2,1)S(1)}, s32[64]{0:T(128)S(1)}, f32[8,128]{1,0:T(8,128)S(1)}) custom-call(s32[2,32]{1,0:T(2,128)} %bitcast.25, s32[128]{0:T(128)} %table_hbm.1, bf16[32,8,1024]{2,1,0:T(8,128)(2,1)} %blocks_hbm.1), custom_call_target="tpu_custom_call" | custom-call | tf_op jit(solution)/shard_map/pallas_call | solution.py:151
  7.4 0.0 copy-start.1
  7.4 1.0 copy-done.1
  8.3 7.0 %all-to-all-start = ((bf16[528,8,128]{2,1,0:T(8,128)(2,1)}), bf16[528,8,128]{2,1,0:T(8,128)(2,1)S(1)}, u32[]{:S(2)}, u32[]{:S(2)}) async-start(bf16[528,8,128]{2,1,0:T(8,128)(2,1)} %copy-done.1), calls=%async_computation | async-start | bytes 2162688 | tf_op jit(solution)/shard_map/all_to_all | solution.py:42
  15.4 0.0 copy-done
  15.4 0.1 collective-permute-start.3
  15.5 15.0 %all-to-all-done.arrived_ref = bf16[528,8,128]{2,1,0:T(8,128)(2,1)S(1)} async-done(((bf16[528,8,128]{2,1,0:T(8,128)(2,1)}), bf16[528,8,128]{2,1,0:T(8,128)(2,1)S(1)}, u32[]{:S(2)}, u32[]{:S(2)}) %all-to-all-start) | async-done | bytes 1081376 | tf_op jit(solution)/shard_map/all_to_all | solution.py:42
  30.5 0.0 collective-permute-done.refs_6_
  30.5 0.0 collective-permute-start.4
  30.5 0.5 multiply_reduce_fusion.3
  31.0 0.1 reshape.134
  31.1 0.2 convert_reduce_fusion
  31.3 0.1 select_reduce_fusion.origin_ref
  31.4 0.8 shard_map.60
  32.3 1.3 collective-permute-start.1
  33.5 2.0 %collective-permute-start.2 = (bf16[16,8,1024]{2,1,0:T(8,128)(2,1)S(1)}, bf16[16,8,1024]{2,1,0:T(8,128)(2,1)S(1)}, u32[]{:S(2)}, u32[]{:S(2)}) collective-permute-start(bf16[16,8,1024]{2,1,0:T(8,128)(2,1)S(1)} %get-tuple-element.35), channel_id=1, source_target_pairs={{0,96},{1,97},{2,98},{3,99},{4,100},{5,101},{6,102},{7,103},{8,104... | collective-permute-start | bytes 786440 | tf_op jit(solution)/shard_map/ppermute | solution.py:56
  35.6 0.0 collective-permute-done.3.refs_5_
  35.6 2.1 %multiply_reduce_fusion.2 = f32[1024]{0:T(1024)S(1)} fusion(bf16[1024,1024]{1,0:T(8,128)(2,1)} %collective-permute-done.3.refs_5_), kind=kLoop, calls=%fused_computation.2 | loop fusion | flops 3144704 | bytes 2101248 | tf_op jit(solution)/shard_map/reduce_sum | solution.py:440
  37.7 2.1 %multiply_reduce_fusion.1 = f32[1024]{0:T(1024)S(1)} fusion(bf16[1024,1024]{1,0:T(8,128)(2,1)} %collective-permute-done.refs_6_), kind=kLoop, calls=%fused_computation.1 | loop fusion | flops 3144704 | bytes 2101248 | tf_op jit(solution)/shard_map/reduce_sum | solution.py:440
  39.7 0.0 collective-permute-done.4.refs_7_
  39.7 2.1 %multiply_reduce_fusion = f32[1024]{0:T(1024)S(1)} fusion(bf16[1024,1024]{1,0:T(8,128)(2,1)} %collective-permute-done.4.refs_7_), kind=kLoop, calls=%fused_computation | loop fusion | flops 3144704 | bytes 2101248 | tf_op jit(solution)/shard_map/reduce_sum | solution.py:440
  41.8 0.0 collective-permute-done.1.refs_2_
  41.8 0.0 collective-permute-done.2.refs_3_
  41.9 5.8 %shard_map.61 = (bf16[17,8,1024]{2,1,0:T(8,128)(2,1)S(1)}, bf16[17,8,1024]{2,1,0:T(8,128)(2,1)S(1)}, bf16[17,8,1024]{2,1,0:T(8,128)(2,1)S(1)}, bf16[17,8,1024]{2,1,0:T(8,128)(2,1)S(1)}) custom-call(bf16[16,8,1024]{2,1,0:T(8,128)(2,1)S(1)} %get-tuple-element.32.refs_0_, bf16[16,8,1024]{2,1,0:T(8,128)(2,1)S(1)} %get-tuple-element.33.refs_1_, ...), custom_call_target="tpu_custom_call" | custom-call | flops 2147483648 | bytes 10485760 | tf_op jit(solution)/shard_map/pallas_call | solution.py:331
  47.6 2.4 %collective-permute-start.5 = (bf16[17,8,1024]{2,1,0:T(8,128)(2,1)S(1)}, bf16[17,8,1024]{2,1,0:T(8,128)(2,1)S(1)}, u32[]{:S(2)}, u32[]{:S(2)}) collective-permute-start(bf16[17,8,1024]{2,1,0:T(8,128)(2,1)S(1)} %get-tuple-element.39), channel_id=1, source_target_pairs={{0,96},{1,97},{2,98},{3,99},{4,100},{5,101},{6,102},{7,103},{8,104... | collective-permute-start | bytes 835592 | tf_op jit(solution)/shard_map/ppermute | solution.py:56
  50.0 0.0 collective-permute-start.6
  50.0 7.0 %collective-permute-done.5.refs_2_ = bf16[17,8,1024]{2,1,0:T(8,128)(2,1)S(1)} collective-permute-done((bf16[17,8,1024]{2,1,0:T(8,128)(2,1)S(1)}, bf16[17,8,1024]{2,1,0:T(8,128)(2,1)S(1)}, u32[]{:S(2)}, u32[]{:S(2)}) %collective-permute-start.5) | collective-permute-done | bytes 278560 | tf_op jit(solution)/shard_map/ppermute | solution.py:56
  57.0 1.1 collective-permute-done.6.refs_3_
  58.2 0.8 shard_map.62
  59.0 22.0 %all_to_all.20.returned_ref = bf16[528,8,128]{2,1,0:T(8,128)(2,1)S(1)} all-to-all(bf16[528,8,128]{2,1,0:T(8,128)(2,1)S(1)} %shard_map.62), channel_id=1, replica_groups={{0,5,10,15,1,6,11,12,2,7,8,13,3,4,9,14},{16,21,26,31,20,25,30,19,24,29,..., dimensions={0} | all-to-all | bytes 2162688 | tf_op jit(solution)/shard_map/all_to_all | solution.py:42
  81.0 1.5 shard_map.63
  82.5 16.4 %all_to_all.21.arrived_ref = bf16[64,8,1024]{2,1,0:T(8,128)(2,1)S(1)} all-to-all(bf16[64,8,1024]{2,1,0:T(8,128)(2,1)S(1)} %get-tuple-element.42), channel_id=1, replica_groups={{0,5,10,15,1,6,11,12,2,7,8,13,3,4,9,14},{16,21,26,31,20,25,30,19,24,29,..., dimensions={0} | all-to-all | bytes 2097152 | tf_op jit(solution)/shard_map/all_to_all | solution.py:42
  98.9 0.6 shard_map.64
  99.5 2.3 %collective-permute-start.7 = (bf16[16,8,1024]{2,1,0:T(8,128)(2,1)S(1)}, bf16[16,8,1024]{2,1,0:T(8,128)(2,1)S(1)}, u32[]{:S(2)}, u32[]{:S(2)}) collective-permute-start(bf16[16,8,1024]{2,1,0:T(8,128)(2,1)S(1)} %get-tuple-element.45), channel_id=1, source_target_pairs={{0,32},{1,33},{2,34},{3,35},{4,36},{5,37},{6,38},{7,39},{8,40},{9,... | collective-permute-start | bytes 786440 | tf_op jit(solution)/shard_map/ppermute | solution.py:56
  101.8 2.6 %collective-permute-start.8 = (bf16[16,8,1024]{2,1,0:T(8,128)(2,1)S(1)}, bf16[16,8,1024]{2,1,0:T(8,128)(2,1)S(1)}, u32[]{:S(2)}, u32[]{:S(2)}) collective-permute-start(bf16[16,8,1024]{2,1,0:T(8,128)(2,1)S(1)} %get-tuple-element.46), channel_id=1, source_target_pairs={{0,96},{1,97},{2,98},{3,99},{4,100},{5,101},{6,102},{7,103},{8,104... | collective-permute-start | bytes 786440 | tf_op jit(solution)/shard_map/ppermute | solution.py:56
  104.4 5.5 %collective-permute-done.7.refs_2_ = bf16[16,8,1024]{2,1,0:T(8,128)(2,1)S(1)} collective-permute-done((bf16[16,8,1024]{2,1,0:T(8,128)(2,1)S(1)}, bf16[16,8,1024]{2,1,0:T(8,128)(2,1)S(1)}, u32[]{:S(2)}, u32[]{:S(2)}) %collective-permute-start.7) | collective-permute-done | bytes 262176 | tf_op jit(solution)/shard_map/ppermute | solution.py:56
  110.0 0.0 collective-permute-done.8.refs_3_
  110.0 5.8 %shard_map.65 = (bf16[17,8,1024]{2,1,0:T(8,128)(2,1)S(1)}, bf16[17,8,1024]{2,1,0:T(8,128)(2,1)S(1)}, bf16[17,8,1024]{2,1,0:T(8,128)(2,1)S(1)}, bf16[17,8,1024]{2,1,0:T(8,128)(2,1)S(1)}) custom-call(bf16[16,8,1024]{2,1,0:T(8,128)(2,1)S(1)} %get-tuple-element.43.refs_0_, bf16[16,8,1024]{2,1,0:T(8,128)(2,1)S(1)} %get-tuple-element.44.refs_1_, ...), custom_call_target="tpu_custom_call" | custom-call | flops 2147483648 | bytes 10485760 | tf_op jit(solution)/shard_map/pallas_call | solution.py:331
  115.8 2.1 %collective-permute-start.9 = (bf16[17,8,1024]{2,1,0:T(8,128)(2,1)S(1)}, bf16[17,8,1024]{2,1,0:T(8,128)(2,1)S(1)}, u32[]{:S(2)}, u32[]{:S(2)}) collective-permute-start(bf16[17,8,1024]{2,1,0:T(8,128)(2,1)S(1)} %get-tuple-element.49), channel_id=1, source_target_pairs={{0,96},{1,97},{2,98},{3,99},{4,100},{5,101},{6,102},{7,103},{8,104... | collective-permute-start | bytes 835592 | tf_op jit(solution)/shard_map/ppermute | solution.py:56
  117.9 0.0 collective-permute-start.10
  117.9 5.7 %collective-permute-done.9.refs_2_ = bf16[17,8,1024]{2,1,0:T(8,128)(2,1)S(1)} collective-permute-done((bf16[17,8,1024]{2,1,0:T(8,128)(2,1)S(1)}, bf16[17,8,1024]{2,1,0:T(8,128)(2,1)S(1)}, u32[]{:S(2)}, u32[]{:S(2)}) %collective-permute-start.9) | collective-permute-done | bytes 278560 | tf_op jit(solution)/shard_map/ppermute | solution.py:56
  123.6 2.1 %collective-permute-done.10.refs_3_ = bf16[17,8,1024]{2,1,0:T(8,128)(2,1)S(1)} collective-permute-done((bf16[17,8,1024]{2,1,0:T(8,128)(2,1)S(1)}, bf16[17,8,1024]{2,1,0:T(8,128)(2,1)S(1)}, u32[]{:S(2)}, u32[]{:S(2)}) %collective-permute-start.10) | collective-permute-done | bytes 278560 | tf_op jit(solution)/shard_map/ppermute | solution.py:56
  125.6 0.8 shard_map.66
  126.5 20.3 %all_to_all.22.returned_ref = bf16[528,8,128]{2,1,0:T(8,128)(2,1)S(1)} all-to-all(bf16[528,8,128]{2,1,0:T(8,128)(2,1)S(1)} %shard_map.66), channel_id=1, replica_groups={{0,5,10,15,1,6,11,12,2,7,8,13,3,4,9,14},{16,21,26,31,20,25,30,19,24,29,..., dimensions={0} | all-to-all | bytes 2162688 | tf_op jit(solution)/shard_map/all_to_all | solution.py:42
  146.8 1.9 %shard_map.67 = (f32[2,256]{1,0:T(2,128)}, bf16[32,8,1024]{2,1,0:T(8,128)(2,1)}) custom-call(s32[64]{0:T(128)S(1)} %get-tuple-element.28.slots_ref, f32[8,128]{1,0:T(8,128)S(1)} %get-tuple-element.41.squares_ref, bf16[528,8,128]{2,1,0:T(8,128)(2,1)S(1)} %all_to_all.22.returned_ref, f32[2,256]{1,0:T(2,128)S(1)} %get-tuple-element.51.earlier_ref), custom_call_target="tpu_custom_call" | custom-call | tf_op jit(solution)/shard_map/pallas_call | solution.py:430
  (8 shorter events, 0.1 us)
Async XLA Ops:
  0.6 14.8 %copy-start = (bf16[1,1024,1024]{2,1,0:T(8,128)(2,1)S(1)}, bf16[1,1024,1024]{2,1,0:T(8,128)(2,1)}, u32[]{:S(2)}) copy-start(bf16[1,1024,1024]{2,1,0:T(8,128)(2,1)} %param.5) | copy-start | bytes 6291460
  0.6 29.9 %collective-permute-start = (bf16[1024,1024]{1,0:T(8,128)(2,1)}, bf16[1024,1024]{1,0:T(8,128)(2,1)}, u32[]{:S(2)}, u32[]{:S(2)}) collective-permute-start(bf16[1024,1024]{1,0:T(8,128)(2,1)} %bitcast.12), channel_id=1, source_target_pairs={{0,96},{1,97},{2,98},{3,99},{4,100},{5,101},{6,102},{7,103},{8,104... | collective-permute-start | bytes 6291464 | tf_op jit(solution)/shard_map/ppermute | solution.py:56
  7.4 1.0 copy-start.1
  8.3 22.2 %all-to-all-start = ((bf16[528,8,128]{2,1,0:T(8,128)(2,1)}), bf16[528,8,128]{2,1,0:T(8,128)(2,1)S(1)}, u32[]{:S(2)}, u32[]{:S(2)}) async-start(bf16[528,8,128]{2,1,0:T(8,128)(2,1)} %copy-done.1), calls=%async_computation | async-start | bytes 2162688 | tf_op jit(solution)/shard_map/all_to_all | solution.py:42
  15.4 20.2 %collective-permute-start.3 = (bf16[1024,1024]{1,0:T(8,128)(2,1)S(1)}, bf16[1024,1024]{1,0:T(8,128)(2,1)}, u32[]{:S(2)}, u32[]{:S(2)}) collective-permute-start(bf16[1024,1024]{1,0:T(8,128)(2,1)S(1)} %bitcast.13), channel_id=1, source_target_pairs={{0,16},{1,17},{2,18},{3,19},{4,20},{5,21},{6,22},{7,23},{8,24},{9,... | collective-permute-start | bytes 6291464 | tf_op jit(solution)/shard_map/ppermute | solution.py:64
  30.5 9.2 %collective-permute-start.4 = (bf16[1024,1024]{1,0:T(8,128)(2,1)}, bf16[1024,1024]{1,0:T(8,128)(2,1)}, u32[]{:S(2)}, u32[]{:S(2)}) collective-permute-start(bf16[1024,1024]{1,0:T(8,128)(2,1)} %collective-permute-done.refs_6_), channel_id=1, source_target_pairs={{0,16},{1,17},{2,18},{3,19},{4,20},{5,21},{6,22},{7,23},{8,24},{9,... | collective-permute-start | bytes 6291464 | tf_op jit(solution)/shard_map/ppermute | solution.py:64
  32.3 9.6 %collective-permute-start.1 = (bf16[16,8,1024]{2,1,0:T(8,128)(2,1)S(1)}, bf16[16,8,1024]{2,1,0:T(8,128)(2,1)S(1)}, u32[]{:S(2)}, u32[]{:S(2)}) collective-permute-start(bf16[16,8,1024]{2,1,0:T(8,128)(2,1)S(1)} %get-tuple-element.34), channel_id=1, source_target_pairs={{0,32},{1,33},{2,34},{3,35},{4,36},{5,37},{6,38},{7,39},{8,40},{9,... | collective-permute-start | bytes 786440 | tf_op jit(solution)/shard_map/ppermute | solution.py:56
  33.5 8.3 %collective-permute-start.2 = (bf16[16,8,1024]{2,1,0:T(8,128)(2,1)S(1)}, bf16[16,8,1024]{2,1,0:T(8,128)(2,1)S(1)}, u32[]{:S(2)}, u32[]{:S(2)}) collective-permute-start(bf16[16,8,1024]{2,1,0:T(8,128)(2,1)S(1)} %get-tuple-element.35), channel_id=1, source_target_pairs={{0,96},{1,97},{2,98},{3,99},{4,100},{5,101},{6,102},{7,103},{8,104... | collective-permute-start | bytes 786440 | tf_op jit(solution)/shard_map/ppermute | solution.py:56
  47.6 9.4 %collective-permute-start.5 = (bf16[17,8,1024]{2,1,0:T(8,128)(2,1)S(1)}, bf16[17,8,1024]{2,1,0:T(8,128)(2,1)S(1)}, u32[]{:S(2)}, u32[]{:S(2)}) collective-permute-start(bf16[17,8,1024]{2,1,0:T(8,128)(2,1)S(1)} %get-tuple-element.39), channel_id=1, source_target_pairs={{0,96},{1,97},{2,98},{3,99},{4,100},{5,101},{6,102},{7,103},{8,104... | collective-permute-start | bytes 835592 | tf_op jit(solution)/shard_map/ppermute | solution.py:56
  50.0 8.2 %collective-permute-start.6 = (bf16[17,8,1024]{2,1,0:T(8,128)(2,1)S(1)}, bf16[17,8,1024]{2,1,0:T(8,128)(2,1)S(1)}, u32[]{:S(2)}, u32[]{:S(2)}) collective-permute-start(bf16[17,8,1024]{2,1,0:T(8,128)(2,1)S(1)} %get-tuple-element.40), channel_id=1, source_target_pairs={{0,32},{1,33},{2,34},{3,35},{4,36},{5,37},{6,38},{7,39},{8,40},{9,... | collective-permute-start | bytes 835592 | tf_op jit(solution)/shard_map/ppermute | solution.py:56
  99.5 10.4 %collective-permute-start.7 = (bf16[16,8,1024]{2,1,0:T(8,128)(2,1)S(1)}, bf16[16,8,1024]{2,1,0:T(8,128)(2,1)S(1)}, u32[]{:S(2)}, u32[]{:S(2)}) collective-permute-start(bf16[16,8,1024]{2,1,0:T(8,128)(2,1)S(1)} %get-tuple-element.45), channel_id=1, source_target_pairs={{0,32},{1,33},{2,34},{3,35},{4,36},{5,37},{6,38},{7,39},{8,40},{9,... | collective-permute-start | bytes 786440 | tf_op jit(solution)/shard_map/ppermute | solution.py:56
  101.8 8.2 %collective-permute-start.8 = (bf16[16,8,1024]{2,1,0:T(8,128)(2,1)S(1)}, bf16[16,8,1024]{2,1,0:T(8,128)(2,1)S(1)}, u32[]{:S(2)}, u32[]{:S(2)}) collective-permute-start(bf16[16,8,1024]{2,1,0:T(8,128)(2,1)S(1)} %get-tuple-element.46), channel_id=1, source_target_pairs={{0,96},{1,97},{2,98},{3,99},{4,100},{5,101},{6,102},{7,103},{8,104... | collective-permute-start | bytes 786440 | tf_op jit(solution)/shard_map/ppermute | solution.py:56
  115.8 7.8 %collective-permute-start.9 = (bf16[17,8,1024]{2,1,0:T(8,128)(2,1)S(1)}, bf16[17,8,1024]{2,1,0:T(8,128)(2,1)S(1)}, u32[]{:S(2)}, u32[]{:S(2)}) collective-permute-start(bf16[17,8,1024]{2,1,0:T(8,128)(2,1)S(1)} %get-tuple-element.49), channel_id=1, source_target_pairs={{0,96},{1,97},{2,98},{3,99},{4,100},{5,101},{6,102},{7,103},{8,104... | collective-permute-start | bytes 835592 | tf_op jit(solution)/shard_map/ppermute | solution.py:56
  117.9 7.8 %collective-permute-start.10 = (bf16[17,8,1024]{2,1,0:T(8,128)(2,1)S(1)}, bf16[17,8,1024]{2,1,0:T(8,128)(2,1)S(1)}, u32[]{:S(2)}, u32[]{:S(2)}) collective-permute-start(bf16[17,8,1024]{2,1,0:T(8,128)(2,1)S(1)} %get-tuple-element.50), channel_id=1, source_target_pairs={{0,32},{1,33},{2,34},{3,35},{4,36},{5,37},{6,38},{7,39},{8,40},{9,... | collective-permute-start | bytes 835592 | tf_op jit(solution)/shard_map/ppermute | solution.py:56

commit v8 on v7

--- a/solution.py
+++ b/solution.py
@@ -471,11 +471,12 @@
     for step in range(STEPS):
         arrived = exchange_slabs(outgoing)
         if step == 0:
-            ahead, arrived = lax.optimization_barrier((ahead, arrived))
+            origin = sorted_origins(arrived, slots.shape[0], depth, core)
+        parts = list(sort_by_depth(arrived, origin, features))
+        if step == 0:
+            ahead, parts[0] = lax.optimization_barrier((ahead, parts[0]))
             clusters = (own, other, ahead, swap_cores(ahead))
             norms = [half_norms_of(cluster) for cluster in clusters]
-            origin = sorted_origins(arrived, slots.shape[0], depth, core)
-        parts = list(sort_by_depth(arrived, origin, features))
         parts[STAY:] = [send_ahead(parts[STAY], 1), send_ahead(parts[STAY + 1], -1)]
         answers = list(score_parts(parts, clusters, norms))
         answers[STAY:] = [send_ahead(answers[STAY], -1), send_ahead(answers[STAY + 1], 1)]

time: 149 us -> 148 us (level)
  waiting for transfers between devices: 36.5 us -> 38.2 us
  other arithmetic: 7.02 us -> 5.43 us
    ppermute x9, waiting for transfers between devices: 21.5 us -> 23.2 us  [send_ahead(): return lax.ppermute(array, AXES, pairs)]
    reduce_sum x4, other arithmetic: 6.68 us -> 5.09 us  [half_norms_of(): jnp.sum(jnp.square(cluster_rows.astype(jnp.float32)), axis=1)[None, :]]
  transfers between devices with their start and end apart: 12 -> 12, of which waited for: 6 -> 7; matrix products, arithmetic and copies ran while one was open for 5% -> 4% of each run, Pallas kernels for 2% -> 2%
where the time goes in v8:
time: 148 us
  blocking collectives  58 us (39%)
  waiting for transfers between devices  38.2 us (26%)
  starting transfers between devices  23.7 us (16%)
  Pallas kernels  20.5 us (14%)
  other arithmetic  5.43 us (4%)
    all_to_all x3, blocking collectives, exchange_slabs(): lax.all_to_all(array, AXES, split_axis=0, concat_axis=0, tiled=True, axis...  58 us
    ppermute x9, waiting for transfers between devices, send_ahead(): return lax.ppermute(array, AXES, pairs)  23.2 us
    ppermute x9, starting transfers between devices, send_ahead(): return lax.ppermute(array, AXES, pairs)  16.5 us
    all_to_all x1, waiting for transfers between devices, exchange_slabs(): lax.all_to_all(array, AXES, split_axis=0, concat_axis=0, tiled=True, axis...  15 us
    pallas_call x2, Pallas kernels, score_parts(): pl.pallas_call(score_kernel, out_shape=[out] * count, in_specs=[VMEM] * c...  11.5 us
    all_to_all x1, starting transfers between devices, exchange_slabs(): lax.all_to_all(array, AXES, split_axis=0, concat_axis=0, tiled=True, axis...  7.03 us
    reduce_sum x4, other arithmetic, half_norms_of(): jnp.sum(jnp.square(cluster_rows.astype(jnp.float32)), axis=1)[None, :]  5.09 us
    pallas_call x2, Pallas kernels, combine(): pl.pallas_call(functools.partial(combine_kernel, log_count, step), out_sh...  3.34 us
  transfers between devices with their start and end apart: 12, of which 7 were waited for; matrix products, arithmetic and copies ran while one was open for 4% of the time, Pallas kernels for 2%

profile of v8, /device:TPU:0, one launch (start us, length us, event | category | flops | bytes accessed | tf_op | source)
XLA Modules:
  0.0 147.8 jit_solution(16865192431676623122)
XLA Ops:
  0.6 0.0 copy-start
  0.6 4.2 %collective-permute-start = (bf16[1024,1024]{1,0:T(8,128)(2,1)}, bf16[1024,1024]{1,0:T(8,128)(2,1)}, u32[]{:S(2)}, u32[]{:S(2)}) collective-permute-start(bf16[1024,1024]{1,0:T(8,128)(2,1)} %bitcast.12), channel_id=1, source_target_pairs={{0,96},{1,97},{2,98},{3,99},{4,100},{5,101},{6,102},{7,103},{8,104... | collective-permute-start | bytes 6291464 | tf_op jit(solution)/shard_map/ppermute | solution.py:56
  4.8 2.5 %shard_map.59 = (bf16[528,8,128]{2,1,0:T(8,128)(2,1)S(1)}, s32[64]{0:T(128)S(1)}, f32[8,128]{1,0:T(8,128)S(1)}) custom-call(s32[2,32]{1,0:T(2,128)} %bitcast.25, s32[128]{0:T(128)} %table_hbm.1, bf16[32,8,1024]{2,1,0:T(8,128)(2,1)} %blocks_hbm.1), custom_call_target="tpu_custom_call" | custom-call | tf_op jit(solution)/shard_map/pallas_call | solution.py:151
  7.4 0.0 copy-start.1
  7.4 1.0 copy-done.1
  8.3 7.0 %all-to-all-start = ((bf16[528,8,128]{2,1,0:T(8,128)(2,1)}), bf16[528,8,128]{2,1,0:T(8,128)(2,1)S(1)}, u32[]{:S(2)}, u32[]{:S(2)}) async-start(bf16[528,8,128]{2,1,0:T(8,128)(2,1)} %copy-done.1), calls=%async_computation | async-start | bytes 2162688 | tf_op jit(solution)/shard_map/all_to_all | solution.py:42
  15.4 0.0 copy-done
  15.4 0.1 collective-permute-start.3
  15.5 15.0 %all-to-all-done.arrived_ref = bf16[528,8,128]{2,1,0:T(8,128)(2,1)S(1)} async-done(((bf16[528,8,128]{2,1,0:T(8,128)(2,1)}), bf16[528,8,128]{2,1,0:T(8,128)(2,1)S(1)}, u32[]{:S(2)}, u32[]{:S(2)}) %all-to-all-start) | async-done | bytes 1081376 | tf_op jit(solution)/shard_map/all_to_all | solution.py:42
  30.5 0.1 reshape.134
  30.6 0.2 convert_reduce_fusion
  30.8 0.1 select_reduce_fusion.origin_ref
  30.9 0.8 shard_map.60
  31.8 0.0 collective-permute-done.refs_6_
  31.8 0.1 collective-permute-start.4
  31.9 0.5 multiply_reduce_fusion.3
  32.3 1.3 collective-permute-start.1
  33.6 2.0 %collective-permute-start.2 = (bf16[16,8,1024]{2,1,0:T(8,128)(2,1)S(1)}, bf16[16,8,1024]{2,1,0:T(8,128)(2,1)S(1)}, u32[]{:S(2)}, u32[]{:S(2)}) collective-permute-start(bf16[16,8,1024]{2,1,0:T(8,128)(2,1)S(1)} %get-tuple-element.35), channel_id=1, source_target_pairs={{0,96},{1,97},{2,98},{3,99},{4,100},{5,101},{6,102},{7,103},{8,104... | collective-permute-start | bytes 786440 | tf_op jit(solution)/shard_map/ppermute | solution.py:56
  35.7 0.0 collective-permute-done.3.refs_5_
  35.7 2.1 %multiply_reduce_fusion.2 = f32[1024]{0:T(1024)S(1)} fusion(bf16[1024,1024]{1,0:T(8,128)(2,1)} %collective-permute-done.3.refs_5_), kind=kLoop, calls=%fused_computation.2 | loop fusion | flops 3144704 | bytes 2101248 | tf_op jit(solution)/shard_map/reduce_sum | solution.py:440
  37.7 2.1 %multiply_reduce_fusion.1 = f32[1024]{0:T(1024)S(1)} fusion(bf16[1024,1024]{1,0:T(8,128)(2,1)} %collective-permute-done.refs_6_), kind=kLoop, calls=%fused_computation.1 | loop fusion | flops 3144704 | bytes 2101248 | tf_op jit(solution)/shard_map/reduce_sum | solution.py:440
  39.8 0.0 collective-permute-done.4.refs_7_
  39.8 0.0 copy-start.2
  39.8 0.5 multiply_reduce_fusion
  40.3 1.5 %collective-permute-done.1.refs_2_ = bf16[16,8,1024]{2,1,0:T(8,128)(2,1)S(1)} collective-permute-done((bf16[16,8,1024]{2,1,0:T(8,128)(2,1)S(1)}, bf16[16,8,1024]{2,1,0:T(8,128)(2,1)S(1)}, u32[]{:S(2)}, u32[]{:S(2)}) %collective-permute-start.1) | collective-permute-done | bytes 262176 | tf_op jit(solution)/shard_map/ppermute | solution.py:56
  41.9 0.0 collective-permute-done.2.refs_3_
  41.9 5.8 %shard_map.61 = (bf16[17,8,1024]{2,1,0:T(8,128)(2,1)S(1)}, bf16[17,8,1024]{2,1,0:T(8,128)(2,1)S(1)}, bf16[17,8,1024]{2,1,0:T(8,128)(2,1)S(1)}, bf16[17,8,1024]{2,1,0:T(8,128)(2,1)S(1)}) custom-call(bf16[16,8,1024]{2,1,0:T(8,128)(2,1)S(1)} %get-tuple-element.32.refs_0_, bf16[16,8,1024]{2,1,0:T(8,128)(2,1)S(1)} %get-tuple-element.33.refs_1_, ...), custom_call_target="tpu_custom_call" | custom-call | flops 2147483648 | bytes 10485760 | tf_op jit(solution)/shard_map/pallas_call | solution.py:331
  47.6 2.3 %collective-permute-start.5 = (bf16[17,8,1024]{2,1,0:T(8,128)(2,1)S(1)}, bf16[17,8,1024]{2,1,0:T(8,128)(2,1)S(1)}, u32[]{:S(2)}, u32[]{:S(2)}) collective-permute-start(bf16[17,8,1024]{2,1,0:T(8,128)(2,1)S(1)} %get-tuple-element.39), channel_id=1, source_target_pairs={{0,96},{1,97},{2,98},{3,99},{4,100},{5,101},{6,102},{7,103},{8,104... | collective-permute-start | bytes 835592 | tf_op jit(solution)/shard_map/ppermute | solution.py:56
  49.9 0.0 collective-permute-start.6
  49.9 7.2 %collective-permute-done.5.refs_2_ = bf16[17,8,1024]{2,1,0:T(8,128)(2,1)S(1)} collective-permute-done((bf16[17,8,1024]{2,1,0:T(8,128)(2,1)S(1)}, bf16[17,8,1024]{2,1,0:T(8,128)(2,1)S(1)}, u32[]{:S(2)}, u32[]{:S(2)}) %collective-permute-start.5) | collective-permute-done | bytes 278560 | tf_op jit(solution)/shard_map/ppermute | solution.py:56
  57.1 1.1 collective-permute-done.6.refs_3_
  58.2 0.8 shard_map.62
  59.1 20.9 %all_to_all.20.returned_ref = bf16[528,8,128]{2,1,0:T(8,128)(2,1)S(1)} all-to-all(bf16[528,8,128]{2,1,0:T(8,128)(2,1)S(1)} %shard_map.62), channel_id=1, replica_groups={{0,5,10,15,1,6,11,12,2,7,8,13,3,4,9,14},{16,21,26,31,20,25,30,19,24,29,..., dimensions={0} | all-to-all | bytes 2162688 | tf_op jit(solution)/shard_map/all_to_all | solution.py:42
  80.0 1.5 shard_map.63
  81.5 16.8 %all_to_all.21.arrived_ref = bf16[64,8,1024]{2,1,0:T(8,128)(2,1)S(1)} all-to-all(bf16[64,8,1024]{2,1,0:T(8,128)(2,1)S(1)} %get-tuple-element.42), channel_id=1, replica_groups={{0,5,10,15,1,6,11,12,2,7,8,13,3,4,9,14},{16,21,26,31,20,25,30,19,24,29,..., dimensions={0} | all-to-all | bytes 2097152 | tf_op jit(solution)/shard_map/all_to_all | solution.py:42
  98.3 0.6 shard_map.64
  99.0 3.0 %collective-permute-start.7 = (bf16[16,8,1024]{2,1,0:T(8,128)(2,1)S(1)}, bf16[16,8,1024]{2,1,0:T(8,128)(2,1)S(1)}, u32[]{:S(2)}, u32[]{:S(2)}) collective-permute-start(bf16[16,8,1024]{2,1,0:T(8,128)(2,1)S(1)} %get-tuple-element.45), channel_id=1, source_target_pairs={{0,32},{1,33},{2,34},{3,35},{4,36},{5,37},{6,38},{7,39},{8,40},{9,... | collective-permute-start | bytes 786440 | tf_op jit(solution)/shard_map/ppermute | solution.py:56
  102.0 1.6 %collective-permute-start.8 = (bf16[16,8,1024]{2,1,0:T(8,128)(2,1)S(1)}, bf16[16,8,1024]{2,1,0:T(8,128)(2,1)S(1)}, u32[]{:S(2)}, u32[]{:S(2)}) collective-permute-start(bf16[16,8,1024]{2,1,0:T(8,128)(2,1)S(1)} %get-tuple-element.46), channel_id=1, source_target_pairs={{0,96},{1,97},{2,98},{3,99},{4,100},{5,101},{6,102},{7,103},{8,104... | collective-permute-start | bytes 786440 | tf_op jit(solution)/shard_map/ppermute | solution.py:56
  103.6 5.7 %collective-permute-done.7.refs_2_ = bf16[16,8,1024]{2,1,0:T(8,128)(2,1)S(1)} collective-permute-done((bf16[16,8,1024]{2,1,0:T(8,128)(2,1)S(1)}, bf16[16,8,1024]{2,1,0:T(8,128)(2,1)S(1)}, u32[]{:S(2)}, u32[]{:S(2)}) %collective-permute-start.7) | collective-permute-done | bytes 262176 | tf_op jit(solution)/shard_map/ppermute | solution.py:56
  109.2 0.0 collective-permute-done.8.refs_3_
  109.2 5.8 %shard_map.65 = (bf16[17,8,1024]{2,1,0:T(8,128)(2,1)S(1)}, bf16[17,8,1024]{2,1,0:T(8,128)(2,1)S(1)}, bf16[17,8,1024]{2,1,0:T(8,128)(2,1)S(1)}, bf16[17,8,1024]{2,1,0:T(8,128)(2,1)S(1)}) custom-call(bf16[16,8,1024]{2,1,0:T(8,128)(2,1)S(1)} %get-tuple-element.43.refs_0_, bf16[16,8,1024]{2,1,0:T(8,128)(2,1)S(1)} %get-tuple-element.44.refs_1_, ...), custom_call_target="tpu_custom_call" | custom-call | flops 2147483648 | bytes 10485760 | tf_op jit(solution)/shard_map/pallas_call | solution.py:331
  115.0 2.0 %collective-permute-start.9 = (bf16[17,8,1024]{2,1,0:T(8,128)(2,1)S(1)}, bf16[17,8,1024]{2,1,0:T(8,128)(2,1)S(1)}, u32[]{:S(2)}, u32[]{:S(2)}) collective-permute-start(bf16[17,8,1024]{2,1,0:T(8,128)(2,1)S(1)} %get-tuple-element.49), channel_id=1, source_target_pairs={{0,96},{1,97},{2,98},{3,99},{4,100},{5,101},{6,102},{7,103},{8,104... | collective-permute-start | bytes 835592 | tf_op jit(solution)/shard_map/ppermute | solution.py:56
  117.0 0.1 collective-permute-start.10
  117.1 5.9 %collective-permute-done.9.refs_2_ = bf16[17,8,1024]{2,1,0:T(8,128)(2,1)S(1)} collective-permute-done((bf16[17,8,1024]{2,1,0:T(8,128)(2,1)S(1)}, bf16[17,8,1024]{2,1,0:T(8,128)(2,1)S(1)}, u32[]{:S(2)}, u32[]{:S(2)}) %collective-permute-start.9) | collective-permute-done | bytes 278560 | tf_op jit(solution)/shard_map/ppermute | solution.py:56
  123.0 1.8 %collective-permute-done.10.refs_3_ = bf16[17,8,1024]{2,1,0:T(8,128)(2,1)S(1)} collective-permute-done((bf16[17,8,1024]{2,1,0:T(8,128)(2,1)S(1)}, bf16[17,8,1024]{2,1,0:T(8,128)(2,1)S(1)}, u32[]{:S(2)}, u32[]{:S(2)}) %collective-permute-start.10) | collective-permute-done | bytes 278560 | tf_op jit(solution)/shard_map/ppermute | solution.py:56
  124.7 0.8 shard_map.66
  125.6 20.3 %all_to_all.22.returned_ref = bf16[528,8,128]{2,1,0:T(8,128)(2,1)S(1)} all-to-all(bf16[528,8,128]{2,1,0:T(8,128)(2,1)S(1)} %shard_map.66), channel_id=1, replica_groups={{0,5,10,15,1,6,11,12,2,7,8,13,3,4,9,14},{16,21,26,31,20,25,30,19,24,29,..., dimensions={0} | all-to-all | bytes 2162688 | tf_op jit(solution)/shard_map/all_to_all | solution.py:42
  145.9 1.9 %shard_map.67 = (f32[2,256]{1,0:T(2,128)}, bf16[32,8,1024]{2,1,0:T(8,128)(2,1)}) custom-call(s32[64]{0:T(128)S(1)} %get-tuple-element.28.slots_ref, f32[8,128]{1,0:T(8,128)S(1)} %get-tuple-element.41.squares_ref, bf16[528,8,128]{2,1,0:T(8,128)(2,1)S(1)} %all_to_all.22.returned_ref, f32[2,256]{1,0:T(2,128)S(1)} %get-tuple-element.51.earlier_ref), custom_call_target="tpu_custom_call" | custom-call | tf_op jit(solution)/shard_map/pallas_call | solution.py:430
  (9 shorter events, 0.1 us)
Async XLA Ops:
  0.6 14.8 %copy-start = (bf16[1,1024,1024]{2,1,0:T(8,128)(2,1)S(1)}, bf16[1,1024,1024]{2,1,0:T(8,128)(2,1)}, u32[]{:S(2)}) copy-start(bf16[1,1024,1024]{2,1,0:T(8,128)(2,1)} %param.5) | copy-start | bytes 6291460
  0.6 31.1 %collective-permute-start = (bf16[1024,1024]{1,0:T(8,128)(2,1)}, bf16[1024,1024]{1,0:T(8,128)(2,1)}, u32[]{:S(2)}, u32[]{:S(2)}) collective-permute-start(bf16[1024,1024]{1,0:T(8,128)(2,1)} %bitcast.12), channel_id=1, source_target_pairs={{0,96},{1,97},{2,98},{3,99},{4,100},{5,101},{6,102},{7,103},{8,104... | collective-permute-start | bytes 6291464 | tf_op jit(solution)/shard_map/ppermute | solution.py:56
  7.4 1.0 copy-start.1
  8.3 22.2 %all-to-all-start = ((bf16[528,8,128]{2,1,0:T(8,128)(2,1)}), bf16[528,8,128]{2,1,0:T(8,128)(2,1)S(1)}, u32[]{:S(2)}, u32[]{:S(2)}) async-start(bf16[528,8,128]{2,1,0:T(8,128)(2,1)} %copy-done.1), calls=%async_computation | async-start | bytes 2162688 | tf_op jit(solution)/shard_map/all_to_all | solution.py:42
  15.4 20.3 %collective-permute-start.3 = (bf16[1024,1024]{1,0:T(8,128)(2,1)S(1)}, bf16[1024,1024]{1,0:T(8,128)(2,1)}, u32[]{:S(2)}, u32[]{:S(2)}) collective-permute-start(bf16[1024,1024]{1,0:T(8,128)(2,1)S(1)} %bitcast.13), channel_id=1, source_target_pairs={{0,16},{1,17},{2,18},{3,19},{4,20},{5,21},{6,22},{7,23},{8,24},{9,... | collective-permute-start | bytes 6291464 | tf_op jit(solution)/shard_map/ppermute | solution.py:64
  31.8 8.1 %collective-permute-start.4 = (bf16[1024,1024]{1,0:T(8,128)(2,1)}, bf16[1024,1024]{1,0:T(8,128)(2,1)S(1)}, u32[]{:S(2)}, u32[]{:S(2)}) collective-permute-start(bf16[1024,1024]{1,0:T(8,128)(2,1)} %collective-permute-done.refs_6_), channel_id=1, source_target_pairs={{0,16},{1,17},{2,18},{3,19},{4,20},{5,21},{6,22},{7,23},{8,24},{9,... | collective-permute-start | bytes 6291464 | tf_op jit(solution)/shard_map/ppermute | solution.py:64
  32.3 9.5 %collective-permute-start.1 = (bf16[16,8,1024]{2,1,0:T(8,128)(2,1)S(1)}, bf16[16,8,1024]{2,1,0:T(8,128)(2,1)S(1)}, u32[]{:S(2)}, u32[]{:S(2)}) collective-permute-start(bf16[16,8,1024]{2,1,0:T(8,128)(2,1)S(1)} %get-tuple-element.34), channel_id=1, source_target_pairs={{0,32},{1,33},{2,34},{3,35},{4,36},{5,37},{6,38},{7,39},{8,40},{9,... | collective-permute-start | bytes 786440 | tf_op jit(solution)/shard_map/ppermute | solution.py:56
  33.6 8.2 %collective-permute-start.2 = (bf16[16,8,1024]{2,1,0:T(8,128)(2,1)S(1)}, bf16[16,8,1024]{2,1,0:T(8,128)(2,1)S(1)}, u32[]{:S(2)}, u32[]{:S(2)}) collective-permute-start(bf16[16,8,1024]{2,1,0:T(8,128)(2,1)S(1)} %get-tuple-element.35), channel_id=1, source_target_pairs={{0,96},{1,97},{2,98},{3,99},{4,100},{5,101},{6,102},{7,103},{8,104... | collective-permute-start | bytes 786440 | tf_op jit(solution)/shard_map/ppermute | solution.py:56
  39.8 2.0 %copy-start.2 = (bf16[1024,1024]{1,0:T(8,128)(2,1)}, bf16[1024,1024]{1,0:T(8,128)(2,1)S(1)}, u32[]{:S(2)}) copy-start(bf16[1024,1024]{1,0:T(8,128)(2,1)S(1)} %collective-permute-done.4.refs_7_) | copy-start | bytes 6291460
  47.6 9.5 %collective-permute-start.5 = (bf16[17,8,1024]{2,1,0:T(8,128)(2,1)S(1)}, bf16[17,8,1024]{2,1,0:T(8,128)(2,1)S(1)}, u32[]{:S(2)}, u32[]{:S(2)}) collective-permute-start(bf16[17,8,1024]{2,1,0:T(8,128)(2,1)S(1)} %get-tuple-element.39), channel_id=1, source_target_pairs={{0,96},{1,97},{2,98},{3,99},{4,100},{5,101},{6,102},{7,103},{8,104... | collective-permute-start | bytes 835592 | tf_op jit(solution)/shard_map/ppermute | solution.py:56
  49.9 8.4 %collective-permute-start.6 = (bf16[17,8,1024]{2,1,0:T(8,128)(2,1)S(1)}, bf16[17,8,1024]{2,1,0:T(8,128)(2,1)S(1)}, u32[]{:S(2)}, u32[]{:S(2)}) collective-permute-start(bf16[17,8,1024]{2,1,0:T(8,128)(2,1)S(1)} %get-tuple-element.40), channel_id=1, source_target_pairs={{0,32},{1,33},{2,34},{3,35},{4,36},{5,37},{6,38},{7,39},{8,40},{9,... | collective-permute-start | bytes 835592 | tf_op jit(solution)/shard_map/ppermute | solution.py:56
  99.0 10.3 %collective-permute-start.7 = (bf16[16,8,1024]{2,1,0:T(8,128)(2,1)S(1)}, bf16[16,8,1024]{2,1,0:T(8,128)(2,1)S(1)}, u32[]{:S(2)}, u32[]{:S(2)}) collective-permute-start(bf16[16,8,1024]{2,1,0:T(8,128)(2,1)S(1)} %get-tuple-element.45), channel_id=1, source_target_pairs={{0,32},{1,33},{2,34},{3,35},{4,36},{5,37},{6,38},{7,39},{8,40},{9,... | collective-permute-start | bytes 786440 | tf_op jit(solution)/shard_map/ppermute | solution.py:56
  102.0 7.3 %collective-permute-start.8 = (bf16[16,8,1024]{2,1,0:T(8,128)(2,1)S(1)}, bf16[16,8,1024]{2,1,0:T(8,128)(2,1)S(1)}, u32[]{:S(2)}, u32[]{:S(2)}) collective-permute-start(bf16[16,8,1024]{2,1,0:T(8,128)(2,1)S(1)} %get-tuple-element.46), channel_id=1, source_target_pairs={{0,96},{1,97},{2,98},{3,99},{4,100},{5,101},{6,102},{7,103},{8,104... | collective-permute-start | bytes 786440 | tf_op jit(solution)/shard_map/ppermute | solution.py:56
  115.0 8.0 %collective-permute-start.9 = (bf16[17,8,1024]{2,1,0:T(8,128)(2,1)S(1)}, bf16[17,8,1024]{2,1,0:T(8,128)(2,1)S(1)}, u32[]{:S(2)}, u32[]{:S(2)}) collective-permute-start(bf16[17,8,1024]{2,1,0:T(8,128)(2,1)S(1)} %get-tuple-element.49), channel_id=1, source_target_pairs={{0,96},{1,97},{2,98},{3,99},{4,100},{5,101},{6,102},{7,103},{8,104... | collective-permute-start | bytes 835592 | tf_op jit(solution)/shard_map/ppermute | solution.py:56
  117.0 7.8 %collective-permute-start.10 = (bf16[17,8,1024]{2,1,0:T(8,128)(2,1)S(1)}, bf16[17,8,1024]{2,1,0:T(8,128)(2,1)S(1)}, u32[]{:S(2)}, u32[]{:S(2)}) collective-permute-start(bf16[17,8,1024]{2,1,0:T(8,128)(2,1)S(1)} %get-tuple-element.50), channel_id=1, source_target_pairs={{0,32},{1,33},{2,34},{3,35},{4,36},{5,37},{6,38},{7,39},{8,40},{9,... | collective-permute-start | bytes 835592 | tf_op jit(solution)/shard_map/ppermute | solution.py:56

commit v9 on v8

--- a/solution.py
+++ b/solution.py
@@ -27,8 +27,7 @@
 
 
 def slab_order(core):
-    order = [(a, (a + b) % SIDE) for b in range(SIDE) for a in range(SIDE)]
-    return [x * SIDE + y if core == 0 else y * SIDE + x for x, y in order]
+    return [2, 10, 0, 14, 6, 5, 3, 8, 7, 11, 15, 1, 12, 13, 9, 4] if core == 0 else [2, 3, 11, 10, 8, 1, 5, 4, 7, 15, 9, 12, 6, 13, 14, 0]
 
 
 def slab_groups():
@@ -75,15 +74,14 @@
     return pltpu.CompilerParams(vmem_limit_bytes=VMEM_LIMIT)
 
 
-def slab_place(slab, core):
-    x, y = lax.div(slab, SIDE), lax.rem(slab, SIDE)
-    first, second = jnp.where(core == 0, x, y), jnp.where(core == 0, y, x)
-    return lax.rem(second - first + SIDE, SIDE) * SIDE + first
+def slab_places(core):
+    order = slab_order(core)
+    return [order.index(slab) for slab in range(SLABS)]
 
 
 def fill_kernel(
     pairs_hbm, table_hbm, blocks_hbm, out_ref, slots_ref, squares_ref,
-    pairs_ref, table_ref, blocks_ref, counts_ref, targets_ref, input_sems,
+    pairs_ref, table_ref, blocks_ref, places_ref, counts_ref, targets_ref, input_sems,
 ):
     count, rows, features = blocks_ref.shape
     tiles = features // LANES
@@ -96,15 +94,16 @@
     ]
     for copy in inputs:
         copy.start()
-    for place in range(SLABS):
-        counts_ref[place] = 0
+    for slab, (first, second) in enumerate(zip(slab_places(0), slab_places(1))):
+        places_ref[slab] = jnp.where(core == 0, first, second)
+        counts_ref[slab] = 0
     for copy in inputs[:2]:
         copy.wait()
 
     def assign(block, carry):
         for side in range(2):
             entry = table_ref[pairs_ref[side, block]]
-            place = slab_place(lax.rem(entry, SLABS), core)
+            place = places_ref[lax.rem(entry, SLABS)]
             rank = counts_ref[place]
             counts_ref[place] = rank + 1
             slot = place * per_slab + rank
@@ -112,7 +111,7 @@
             targets_ref[slot] = lax.div(entry, SLABS)
         return carry
 
-    lax.fori_loop(0, count, assign, 0, unroll=8)
+    lax.fori_loop(0, count, assign, 0, unroll=32)
     inputs[2].wait()
     lane = lax.broadcasted_iota(jnp.int32, (rows, LANES), 1)
 
@@ -127,7 +126,7 @@
         return jnp.where(lane == block, jnp.sum(total, axis=1, keepdims=True), squares)
 
     squares_ref[...] = lax.fori_loop(
-        0, count, put, jnp.zeros((rows, LANES), jnp.float32), unroll=8
+        0, count, put, jnp.zeros((rows, LANES), jnp.float32), unroll=32
     )
 
     def note(place, carry):
@@ -161,6 +160,7 @@
             pltpu.SMEM(pairs.shape, jnp.int32),
             pltpu.SMEM(table.shape, jnp.int32),
             pltpu.VMEM(blocks.shape, jnp.bfloat16),
+            pltpu.SMEM((SLABS,), jnp.int32),
             pltpu.SMEM((SLABS,), jnp.int32),
             pltpu.SMEM((2 * count,), jnp.int32),
             pltpu.SemaphoreType.DMA((3,)),
@@ -396,7 +396,7 @@
         return densities, jnp.where(lane == block, total, next_squares)
 
     zeros = jnp.zeros((rows, LANES), jnp.float32)
-    densities, next_squares = lax.fori_loop(0, count, body, (zeros, zeros), unroll=16)
+    densities, next_squares = lax.fori_loop(0, count, body, (zeros, zeros), unroll=32)
     if not last:
         out_refs[1][...] = next_squares
     densities = densities - 0.5 * INV_WIDTH * squares - log_count

time: 148 us -> 147 us (level)
  waiting for transfers between devices: 38.2 us -> 34.3 us
  starting transfers between devices: 23.7 us -> 26.9 us
    all_to_all x1, waiting for transfers between devices: 15 us -> 12 us  [exchange_slabs(): lax.all_to_all(array, AXES, split_axis=0, concat_axis=0, tiled=True, axis...]
    ppermute x9, starting transfers between devices: 16.5 us -> 18.5 us  [send_ahead(): return lax.ppermute(array, AXES, pairs)]
  transfers between devices with their start and end apart: 12 -> 12, of which waited for: 7 -> 8; matrix products, arithmetic and copies ran while one was open for 4% -> 4% of each run, Pallas kernels for 2% -> 2%
where the time goes in v9:
time: 147 us; the launch traced here: 146 us
  blocking collectives  58.1 us (40%)
  waiting for transfers between devices  34.3 us (23%)
  starting transfers between devices  26.9 us (18%)
  Pallas kernels  19.8 us (13%)
  other arithmetic  5.43 us (4%)
    all_to_all x3, blocking collectives, exchange_slabs(): lax.all_to_all(array, AXES, split_axis=0, concat_axis=0, tiled=True, axis...  58.1 us
    ppermute x9, waiting for transfers between devices, send_ahead(): return lax.ppermute(array, AXES, pairs)  22.3 us
    ppermute x9, starting transfers between devices, send_ahead(): return lax.ppermute(array, AXES, pairs)  18.5 us
    all_to_all x1, waiting for transfers between devices, exchange_slabs(): lax.all_to_all(array, AXES, split_axis=0, concat_axis=0, tiled=True, axis...  12 us
    pallas_call x2, Pallas kernels, score_parts(): pl.pallas_call(score_kernel, out_shape=[out] * count, in_specs=[VMEM] * c...  11.5 us
    all_to_all x1, starting transfers between devices, exchange_slabs(): lax.all_to_all(array, AXES, split_axis=0, concat_axis=0, tiled=True, axis...  8.23 us
    reduce_sum x4, other arithmetic, half_norms_of(): jnp.sum(jnp.square(cluster_rows.astype(jnp.float32)), axis=1)[None, :]  5.09 us
    pallas_call x2, Pallas kernels, combine(): pl.pallas_call(functools.partial(combine_kernel, log_count, step), out_sh...  3.24 us
  transfers between devices with their start and end apart: 12, of which 8 were waited for; matrix products, arithmetic and copies ran while one was open for 4% of the time, Pallas kernels for 2%

profile of v9, /device:TPU:0, one launch (start us, length us, event | category | flops | bytes accessed | tf_op | source)
XLA Modules:
  0.0 146.4 jit_solution(1867460626669273535)
XLA Ops:
  0.6 0.0 copy-start
  0.6 4.2 %collective-permute-start = (bf16[1024,1024]{1,0:T(8,128)(2,1)}, bf16[1024,1024]{1,0:T(8,128)(2,1)}, u32[]{:S(2)}, u32[]{:S(2)}) collective-permute-start(bf16[1024,1024]{1,0:T(8,128)(2,1)} %bitcast.12), channel_id=1, source_target_pairs={{0,96},{1,97},{2,98},{3,99},{4,100},{5,101},{6,102},{7,103},{8,104... | collective-permute-start | bytes 6291464 | tf_op jit(solution)/shard_map/ppermute | solution.py:55
  4.8 1.9 %shard_map.59 = (bf16[528,8,128]{2,1,0:T(8,128)(2,1)S(1)}, s32[64]{0:T(128)S(1)}, f32[8,128]{1,0:T(8,128)S(1)}) custom-call(s32[2,32]{1,0:T(2,128)} %bitcast.25, s32[128]{0:T(128)} %table_hbm.1, bf16[32,8,1024]{2,1,0:T(8,128)(2,1)} %blocks_hbm.1), custom_call_target="tpu_custom_call" | custom-call | tf_op jit(solution)/shard_map/pallas_call | solution.py:150
  6.8 0.0 copy-start.1
  6.8 1.0 copy-done.1
  7.8 8.2 %all-to-all-start = ((bf16[528,8,128]{2,1,0:T(8,128)(2,1)}), bf16[528,8,128]{2,1,0:T(8,128)(2,1)S(1)}, u32[]{:S(2)}, u32[]{:S(2)}) async-start(bf16[528,8,128]{2,1,0:T(8,128)(2,1)} %copy-done.1), calls=%async_computation | async-start | bytes 2162688 | tf_op jit(solution)/shard_map/all_to_all | solution.py:41
  16.0 0.0 copy-done
  16.0 0.1 collective-permute-start.3
  16.1 12.0 %all-to-all-done.arrived_ref = bf16[528,8,128]{2,1,0:T(8,128)(2,1)S(1)} async-done(((bf16[528,8,128]{2,1,0:T(8,128)(2,1)}), bf16[528,8,128]{2,1,0:T(8,128)(2,1)S(1)}, u32[]{:S(2)}, u32[]{:S(2)}) %all-to-all-start) | async-done | bytes 1081376 | tf_op jit(solution)/shard_map/all_to_all | solution.py:41
  28.1 0.1 reshape.134
  28.2 0.2 convert_reduce_fusion
  28.4 0.1 select_reduce_fusion.origin_ref
  28.6 0.8 shard_map.60
  29.4 0.0 collective-permute-done.refs_6_
  29.4 0.1 collective-permute-start.4
  29.5 0.5 multiply_reduce_fusion.3
  30.0 1.7 %collective-permute-start.1 = (bf16[16,8,1024]{2,1,0:T(8,128)(2,1)S(1)}, bf16[16,8,1024]{2,1,0:T(8,128)(2,1)S(1)}, u32[]{:S(2)}, u32[]{:S(2)}) collective-permute-start(bf16[16,8,1024]{2,1,0:T(8,128)(2,1)S(1)} %get-tuple-element.34), channel_id=1, source_target_pairs={{0,32},{1,33},{2,34},{3,35},{4,36},{5,37},{6,38},{7,39},{8,40},{9,... | collective-permute-start | bytes 786440 | tf_op jit(solution)/shard_map/ppermute | solution.py:55
  31.7 1.6 %collective-permute-start.2 = (bf16[16,8,1024]{2,1,0:T(8,128)(2,1)S(1)}, bf16[16,8,1024]{2,1,0:T(8,128)(2,1)S(1)}, u32[]{:S(2)}, u32[]{:S(2)}) collective-permute-start(bf16[16,8,1024]{2,1,0:T(8,128)(2,1)S(1)} %get-tuple-element.35), channel_id=1, source_target_pairs={{0,96},{1,97},{2,98},{3,99},{4,100},{5,101},{6,102},{7,103},{8,104... | collective-permute-start | bytes 786440 | tf_op jit(solution)/shard_map/ppermute | solution.py:55
  33.3 0.0 collective-permute-done.3.refs_5_
  33.3 2.1 %multiply_reduce_fusion.2 = f32[1024]{0:T(1024)S(1)} fusion(bf16[1024,1024]{1,0:T(8,128)(2,1)} %collective-permute-done.3.refs_5_), kind=kLoop, calls=%fused_computation.2 | loop fusion | flops 3144704 | bytes 2101248 | tf_op jit(solution)/shard_map/reduce_sum | solution.py:440
  35.4 2.1 %multiply_reduce_fusion.1 = f32[1024]{0:T(1024)S(1)} fusion(bf16[1024,1024]{1,0:T(8,128)(2,1)} %collective-permute-done.refs_6_), kind=kLoop, calls=%fused_computation.1 | loop fusion | flops 3144704 | bytes 2101248 | tf_op jit(solution)/shard_map/reduce_sum | solution.py:440
  37.4 0.0 collective-permute-done.4.refs_7_
  37.4 0.0 copy-start.2
  37.5 0.5 multiply_reduce_fusion
  38.0 0.2 collective-permute-done.1.refs_2_
  38.2 1.0 collective-permute-done.2.refs_3_
  39.2 5.8 %shard_map.61 = (bf16[17,8,1024]{2,1,0:T(8,128)(2,1)S(1)}, bf16[17,8,1024]{2,1,0:T(8,128)(2,1)S(1)}, bf16[17,8,1024]{2,1,0:T(8,128)(2,1)S(1)}, bf16[17,8,1024]{2,1,0:T(8,128)(2,1)S(1)}) custom-call(bf16[16,8,1024]{2,1,0:T(8,128)(2,1)S(1)} %get-tuple-element.32.refs_0_, bf16[16,8,1024]{2,1,0:T(8,128)(2,1)S(1)} %get-tuple-element.33.refs_1_, ...), custom_call_target="tpu_custom_call" | custom-call | flops 2147483648 | bytes 10485760 | tf_op jit(solution)/shard_map/pallas_call | solution.py:331
  45.0 3.8 %collective-permute-start.5 = (bf16[17,8,1024]{2,1,0:T(8,128)(2,1)S(1)}, bf16[17,8,1024]{2,1,0:T(8,128)(2,1)S(1)}, u32[]{:S(2)}, u32[]{:S(2)}) collective-permute-start(bf16[17,8,1024]{2,1,0:T(8,128)(2,1)S(1)} %get-tuple-element.39), channel_id=1, source_target_pairs={{0,96},{1,97},{2,98},{3,99},{4,100},{5,101},{6,102},{7,103},{8,104... | collective-permute-start | bytes 835592 | tf_op jit(solution)/shard_map/ppermute | solution.py:55
  48.7 0.0 collective-permute-start.6
  48.7 6.4 %collective-permute-done.5.refs_2_ = bf16[17,8,1024]{2,1,0:T(8,128)(2,1)S(1)} collective-permute-done((bf16[17,8,1024]{2,1,0:T(8,128)(2,1)S(1)}, bf16[17,8,1024]{2,1,0:T(8,128)(2,1)S(1)}, u32[]{:S(2)}, u32[]{:S(2)}) %collective-permute-start.5) | collective-permute-done | bytes 278560 | tf_op jit(solution)/shard_map/ppermute | solution.py:55
  55.1 1.4 collective-permute-done.6.refs_3_
  56.5 0.8 shard_map.62
  57.3 21.0 %all_to_all.20.returned_ref = bf16[528,8,128]{2,1,0:T(8,128)(2,1)S(1)} all-to-all(bf16[528,8,128]{2,1,0:T(8,128)(2,1)S(1)} %shard_map.62), channel_id=1, replica_groups={{2,10,0,14,6,5,3,8,7,11,15,1,12,13,9,4},{18,19,27,26,24,17,21,20,23,31,..., dimensions={0} | all-to-all | bytes 2162688 | tf_op jit(solution)/shard_map/all_to_all | solution.py:41
  78.3 1.4 shard_map.63
  79.7 16.9 %all_to_all.21.arrived_ref = bf16[64,8,1024]{2,1,0:T(8,128)(2,1)S(1)} all-to-all(bf16[64,8,1024]{2,1,0:T(8,128)(2,1)S(1)} %get-tuple-element.42), channel_id=1, replica_groups={{2,10,0,14,6,5,3,8,7,11,15,1,12,13,9,4},{18,19,27,26,24,17,21,20,23,31,..., dimensions={0} | all-to-all | bytes 2097152 | tf_op jit(solution)/shard_map/all_to_all | solution.py:41
  96.6 0.6 shard_map.64
  97.2 2.3 %collective-permute-start.7 = (bf16[16,8,1024]{2,1,0:T(8,128)(2,1)S(1)}, bf16[16,8,1024]{2,1,0:T(8,128)(2,1)S(1)}, u32[]{:S(2)}, u32[]{:S(2)}) collective-permute-start(bf16[16,8,1024]{2,1,0:T(8,128)(2,1)S(1)} %get-tuple-element.45), channel_id=1, source_target_pairs={{0,32},{1,33},{2,34},{3,35},{4,36},{5,37},{6,38},{7,39},{8,40},{9,... | collective-permute-start | bytes 786440 | tf_op jit(solution)/shard_map/ppermute | solution.py:55
  99.5 2.8 %collective-permute-start.8 = (bf16[16,8,1024]{2,1,0:T(8,128)(2,1)S(1)}, bf16[16,8,1024]{2,1,0:T(8,128)(2,1)S(1)}, u32[]{:S(2)}, u32[]{:S(2)}) collective-permute-start(bf16[16,8,1024]{2,1,0:T(8,128)(2,1)S(1)} %get-tuple-element.46), channel_id=1, source_target_pairs={{0,96},{1,97},{2,98},{3,99},{4,100},{5,101},{6,102},{7,103},{8,104... | collective-permute-start | bytes 786440 | tf_op jit(solution)/shard_map/ppermute | solution.py:55
  102.3 5.5 %collective-permute-done.7.refs_2_ = bf16[16,8,1024]{2,1,0:T(8,128)(2,1)S(1)} collective-permute-done((bf16[16,8,1024]{2,1,0:T(8,128)(2,1)S(1)}, bf16[16,8,1024]{2,1,0:T(8,128)(2,1)S(1)}, u32[]{:S(2)}, u32[]{:S(2)}) %collective-permute-start.7) | collective-permute-done | bytes 262176 | tf_op jit(solution)/shard_map/ppermute | solution.py:55
  107.8 0.0 collective-permute-done.8.refs_3_
  107.8 5.8 %shard_map.65 = (bf16[17,8,1024]{2,1,0:T(8,128)(2,1)S(1)}, bf16[17,8,1024]{2,1,0:T(8,128)(2,1)S(1)}, bf16[17,8,1024]{2,1,0:T(8,128)(2,1)S(1)}, bf16[17,8,1024]{2,1,0:T(8,128)(2,1)S(1)}) custom-call(bf16[16,8,1024]{2,1,0:T(8,128)(2,1)S(1)} %get-tuple-element.43.refs_0_, bf16[16,8,1024]{2,1,0:T(8,128)(2,1)S(1)} %get-tuple-element.44.refs_1_, ...), custom_call_target="tpu_custom_call" | custom-call | flops 2147483648 | bytes 10485760 | tf_op jit(solution)/shard_map/pallas_call | solution.py:331
  113.6 2.1 %collective-permute-start.9 = (bf16[17,8,1024]{2,1,0:T(8,128)(2,1)S(1)}, bf16[17,8,1024]{2,1,0:T(8,128)(2,1)S(1)}, u32[]{:S(2)}, u32[]{:S(2)}) collective-permute-start(bf16[17,8,1024]{2,1,0:T(8,128)(2,1)S(1)} %get-tuple-element.49), channel_id=1, source_target_pairs={{0,96},{1,97},{2,98},{3,99},{4,100},{5,101},{6,102},{7,103},{8,104... | collective-permute-start | bytes 835592 | tf_op jit(solution)/shard_map/ppermute | solution.py:55
  115.8 0.0 collective-permute-start.10
  115.8 5.6 %collective-permute-done.9.refs_2_ = bf16[17,8,1024]{2,1,0:T(8,128)(2,1)S(1)} collective-permute-done((bf16[17,8,1024]{2,1,0:T(8,128)(2,1)S(1)}, bf16[17,8,1024]{2,1,0:T(8,128)(2,1)S(1)}, u32[]{:S(2)}, u32[]{:S(2)}) %collective-permute-start.9) | collective-permute-done | bytes 278560 | tf_op jit(solution)/shard_map/ppermute | solution.py:55
  121.4 2.1 %collective-permute-done.10.refs_3_ = bf16[17,8,1024]{2,1,0:T(8,128)(2,1)S(1)} collective-permute-done((bf16[17,8,1024]{2,1,0:T(8,128)(2,1)S(1)}, bf16[17,8,1024]{2,1,0:T(8,128)(2,1)S(1)}, u32[]{:S(2)}, u32[]{:S(2)}) %collective-permute-start.10) | collective-permute-done | bytes 278560 | tf_op jit(solution)/shard_map/ppermute | solution.py:55
  123.5 0.8 shard_map.66
  124.4 20.2 %all_to_all.22.returned_ref = bf16[528,8,128]{2,1,0:T(8,128)(2,1)S(1)} all-to-all(bf16[528,8,128]{2,1,0:T(8,128)(2,1)S(1)} %shard_map.66), channel_id=1, replica_groups={{2,10,0,14,6,5,3,8,7,11,15,1,12,13,9,4},{18,19,27,26,24,17,21,20,23,31,..., dimensions={0} | all-to-all | bytes 2162688 | tf_op jit(solution)/shard_map/all_to_all | solution.py:41
  144.6 1.9 %shard_map.67 = (f32[2,256]{1,0:T(2,128)}, bf16[32,8,1024]{2,1,0:T(8,128)(2,1)}) custom-call(s32[64]{0:T(128)S(1)} %get-tuple-element.28.slots_ref, f32[8,128]{1,0:T(8,128)S(1)} %get-tuple-element.41.squares_ref, bf16[528,8,128]{2,1,0:T(8,128)(2,1)S(1)} %all_to_all.22.returned_ref, f32[2,256]{1,0:T(2,128)S(1)} %get-tuple-element.51.earlier_ref), custom_call_target="tpu_custom_call" | custom-call | tf_op jit(solution)/shard_map/pallas_call | solution.py:430
  (9 shorter events, 0.1 us)
Async XLA Ops:
  0.6 15.4 %copy-start = (bf16[1,1024,1024]{2,1,0:T(8,128)(2,1)S(1)}, bf16[1,1024,1024]{2,1,0:T(8,128)(2,1)}, u32[]{:S(2)}) copy-start(bf16[1,1024,1024]{2,1,0:T(8,128)(2,1)} %param.5) | copy-start | bytes 6291460
  0.6 28.7 %collective-permute-start = (bf16[1024,1024]{1,0:T(8,128)(2,1)}, bf16[1024,1024]{1,0:T(8,128)(2,1)}, u32[]{:S(2)}, u32[]{:S(2)}) collective-permute-start(bf16[1024,1024]{1,0:T(8,128)(2,1)} %bitcast.12), channel_id=1, source_target_pairs={{0,96},{1,97},{2,98},{3,99},{4,100},{5,101},{6,102},{7,103},{8,104... | collective-permute-start | bytes 6291464 | tf_op jit(solution)/shard_map/ppermute | solution.py:55
  6.8 1.0 copy-start.1
  7.8 20.3 %all-to-all-start = ((bf16[528,8,128]{2,1,0:T(8,128)(2,1)}), bf16[528,8,128]{2,1,0:T(8,128)(2,1)S(1)}, u32[]{:S(2)}, u32[]{:S(2)}) async-start(bf16[528,8,128]{2,1,0:T(8,128)(2,1)} %copy-done.1), calls=%async_computation | async-start | bytes 2162688 | tf_op jit(solution)/shard_map/all_to_all | solution.py:41
  16.0 17.3 %collective-permute-start.3 = (bf16[1024,1024]{1,0:T(8,128)(2,1)S(1)}, bf16[1024,1024]{1,0:T(8,128)(2,1)}, u32[]{:S(2)}, u32[]{:S(2)}) collective-permute-start(bf16[1024,1024]{1,0:T(8,128)(2,1)S(1)} %bitcast.13), channel_id=1, source_target_pairs={{0,16},{1,17},{2,18},{3,19},{4,20},{5,21},{6,22},{7,23},{8,24},{9,... | collective-permute-start | bytes 6291464 | tf_op jit(solution)/shard_map/ppermute | solution.py:63
  29.4 8.1 %collective-permute-start.4 = (bf16[1024,1024]{1,0:T(8,128)(2,1)}, bf16[1024,1024]{1,0:T(8,128)(2,1)S(1)}, u32[]{:S(2)}, u32[]{:S(2)}) collective-permute-start(bf16[1024,1024]{1,0:T(8,128)(2,1)} %collective-permute-done.refs_6_), channel_id=1, source_target_pairs={{0,16},{1,17},{2,18},{3,19},{4,20},{5,21},{6,22},{7,23},{8,24},{9,... | collective-permute-start | bytes 6291464 | tf_op jit(solution)/shard_map/ppermute | solution.py:63
  30.0 8.2 %collective-permute-start.1 = (bf16[16,8,1024]{2,1,0:T(8,128)(2,1)S(1)}, bf16[16,8,1024]{2,1,0:T(8,128)(2,1)S(1)}, u32[]{:S(2)}, u32[]{:S(2)}) collective-permute-start(bf16[16,8,1024]{2,1,0:T(8,128)(2,1)S(1)} %get-tuple-element.34), channel_id=1, source_target_pairs={{0,32},{1,33},{2,34},{3,35},{4,36},{5,37},{6,38},{7,39},{8,40},{9,... | collective-permute-start | bytes 786440 | tf_op jit(solution)/shard_map/ppermute | solution.py:55
  31.7 7.5 %collective-permute-start.2 = (bf16[16,8,1024]{2,1,0:T(8,128)(2,1)S(1)}, bf16[16,8,1024]{2,1,0:T(8,128)(2,1)S(1)}, u32[]{:S(2)}, u32[]{:S(2)}) collective-permute-start(bf16[16,8,1024]{2,1,0:T(8,128)(2,1)S(1)} %get-tuple-element.35), channel_id=1, source_target_pairs={{0,96},{1,97},{2,98},{3,99},{4,100},{5,101},{6,102},{7,103},{8,104... | collective-permute-start | bytes 786440 | tf_op jit(solution)/shard_map/ppermute | solution.py:55
  37.4 1.7 %copy-start.2 = (bf16[1024,1024]{1,0:T(8,128)(2,1)}, bf16[1024,1024]{1,0:T(8,128)(2,1)S(1)}, u32[]{:S(2)}) copy-start(bf16[1024,1024]{1,0:T(8,128)(2,1)S(1)} %collective-permute-done.4.refs_7_) | copy-start | bytes 6291460
  45.0 10.2 %collective-permute-start.5 = (bf16[17,8,1024]{2,1,0:T(8,128)(2,1)S(1)}, bf16[17,8,1024]{2,1,0:T(8,128)(2,1)S(1)}, u32[]{:S(2)}, u32[]{:S(2)}) collective-permute-start(bf16[17,8,1024]{2,1,0:T(8,128)(2,1)S(1)} %get-tuple-element.39), channel_id=1, source_target_pairs={{0,96},{1,97},{2,98},{3,99},{4,100},{5,101},{6,102},{7,103},{8,104... | collective-permute-start | bytes 835592 | tf_op jit(solution)/shard_map/ppermute | solution.py:55
  48.7 7.8 %collective-permute-start.6 = (bf16[17,8,1024]{2,1,0:T(8,128)(2,1)S(1)}, bf16[17,8,1024]{2,1,0:T(8,128)(2,1)S(1)}, u32[]{:S(2)}, u32[]{:S(2)}) collective-permute-start(bf16[17,8,1024]{2,1,0:T(8,128)(2,1)S(1)} %get-tuple-element.40), channel_id=1, source_target_pairs={{0,32},{1,33},{2,34},{3,35},{4,36},{5,37},{6,38},{7,39},{8,40},{9,... | collective-permute-start | bytes 835592 | tf_op jit(solution)/shard_map/ppermute | solution.py:55
  97.2 10.6 %collective-permute-start.7 = (bf16[16,8,1024]{2,1,0:T(8,128)(2,1)S(1)}, bf16[16,8,1024]{2,1,0:T(8,128)(2,1)S(1)}, u32[]{:S(2)}, u32[]{:S(2)}) collective-permute-start(bf16[16,8,1024]{2,1,0:T(8,128)(2,1)S(1)} %get-tuple-element.45), channel_id=1, source_target_pairs={{0,32},{1,33},{2,34},{3,35},{4,36},{5,37},{6,38},{7,39},{8,40},{9,... | collective-permute-start | bytes 786440 | tf_op jit(solution)/shard_map/ppermute | solution.py:55
  99.5 8.3 %collective-permute-start.8 = (bf16[16,8,1024]{2,1,0:T(8,128)(2,1)S(1)}, bf16[16,8,1024]{2,1,0:T(8,128)(2,1)S(1)}, u32[]{:S(2)}, u32[]{:S(2)}) collective-permute-start(bf16[16,8,1024]{2,1,0:T(8,128)(2,1)S(1)} %get-tuple-element.46), channel_id=1, source_target_pairs={{0,96},{1,97},{2,98},{3,99},{4,100},{5,101},{6,102},{7,103},{8,104... | collective-permute-start | bytes 786440 | tf_op jit(solution)/shard_map/ppermute | solution.py:55
  113.6 7.8 %collective-permute-start.9 = (bf16[17,8,1024]{2,1,0:T(8,128)(2,1)S(1)}, bf16[17,8,1024]{2,1,0:T(8,128)(2,1)S(1)}, u32[]{:S(2)}, u32[]{:S(2)}) collective-permute-start(bf16[17,8,1024]{2,1,0:T(8,128)(2,1)S(1)} %get-tuple-element.49), channel_id=1, source_target_pairs={{0,96},{1,97},{2,98},{3,99},{4,100},{5,101},{6,102},{7,103},{8,104... | collective-permute-start | bytes 835592 | tf_op jit(solution)/shard_map/ppermute | solution.py:55
  115.8 7.8 %collective-permute-start.10 = (bf16[17,8,1024]{2,1,0:T(8,128)(2,1)S(1)}, bf16[17,8,1024]{2,1,0:T(8,128)(2,1)S(1)}, u32[]{:S(2)}, u32[]{:S(2)}) collective-permute-start(bf16[17,8,1024]{2,1,0:T(8,128)(2,1)S(1)} %get-tuple-element.50), channel_id=1, source_target_pairs={{0,32},{1,33},{2,34},{3,35},{4,36},{5,37},{6,38},{7,39},{8,40},{9,... | collective-permute-start | bytes 835592 | tf_op jit(solution)/shard_map/ppermute | solution.py:55

commit v10 on v9

--- a/solution.py
+++ b/solution.py
@@ -275,7 +275,7 @@
 def score_kernel(*refs):
     count = len(GROUPS)
     part_refs, refs = refs[:count], refs[count:]
-    cluster_anys, refs = refs[:count], refs[count:]
+    (own_ref, *cluster_anys), refs = refs[:count], refs[count:]
     norm_refs, refs = refs[:count], refs[count:]
     out_refs, (clusters_ref, cluster_sems) = refs[:count], refs[count:]
     copies = [
@@ -286,6 +286,10 @@
         copy.start()
     size, rows, features = part_refs[0].shape
     half = size // 2
+
+    def cluster_rows(cluster):
+        return own_ref[...] if cluster == OWN else clusters_ref[cluster - 1]
+
     lines = half * rows
     first_half = lax.broadcasted_iota(jnp.int32, (rows, LANES), 1) < LANES // 2
     members = [
@@ -302,11 +306,12 @@
                 for group, side in members[cluster]
             ]
         ).astype(jnp.bfloat16)
-        copies[cluster].wait()
-        products.append(products_of(flat, clusters_ref[cluster]))
+        if cluster != OWN:
+            copies[cluster - 1].wait()
+        products.append(products_of(flat, cluster_rows(cluster)))
     for cluster in range(count):
         weights, totals, terms = weigh(products[cluster], norm_refs[cluster][...])
-        summed = jnp.dot(weights, clusters_ref[cluster], preferred_element_type=jnp.float32)
+        summed = jnp.dot(weights, cluster_rows(cluster), preferred_element_type=jnp.float32)
         part = summed * (1.0 / totals)
         for place, (group, side) in enumerate(members[cluster]):
             first, out_ref = place * lines, out_refs[group]
@@ -331,11 +336,11 @@
     return pl.pallas_call(
         score_kernel,
         out_shape=[out] * count,
-        in_specs=[VMEM] * count + [whole(pl.ANY)] * count + [VMEM] * count,
+        in_specs=[VMEM] * (count + 1) + [whole(pl.ANY)] * (count - 1) + [VMEM] * count,
         out_specs=[VMEM] * count,
         scratch_shapes=[
-            pltpu.VMEM((count, references, features), jnp.bfloat16),
-            pltpu.SemaphoreType.DMA((count,)),
+            pltpu.VMEM((count - 1, references, features), jnp.bfloat16),
+            pltpu.SemaphoreType.DMA((count - 1,)),
         ],
         compiler_params=params(),
         cost_estimate=pl.CostEstimate(

time: 147 us -> 147 us (level)
  no operation moved by 1% of the time
where the time goes in v10:
time: 147 us; the launch traced here: 146 us
  blocking collectives  58.1 us (40%)
  waiting for transfers between devices  34.3 us (23%)
  starting transfers between devices  26.9 us (18%)
  Pallas kernels  19.5 us (13%)
  other arithmetic  5.43 us (4%)
    all_to_all x3, blocking collectives, exchange_slabs(): lax.all_to_all(array, AXES, split_axis=0, concat_axis=0, tiled=True, axis...  58.1 us
    ppermute x9, waiting for transfers between devices, send_ahead(): return lax.ppermute(array, AXES, pairs)  22.3 us
    ppermute x9, starting transfers between devices, send_ahead(): return lax.ppermute(array, AXES, pairs)  18.5 us
    all_to_all x1, waiting for transfers between devices, exchange_slabs(): lax.all_to_all(array, AXES, split_axis=0, concat_axis=0, tiled=True, axis...  12 us
    pallas_call x2, Pallas kernels, score_parts(): pl.pallas_call(score_kernel, out_shape=[out] * count, in_specs=[VMEM] * (...  11.2 us
    all_to_all x1, starting transfers between devices, exchange_slabs(): lax.all_to_all(array, AXES, split_axis=0, concat_axis=0, tiled=True, axis...  8.23 us
    reduce_sum x4, other arithmetic, half_norms_of(): jnp.sum(jnp.square(cluster_rows.astype(jnp.float32)), axis=1)[None, :]  5.09 us
    pallas_call x2, Pallas kernels, combine(): pl.pallas_call(functools.partial(combine_kernel, log_count, step), out_sh...  3.23 us
  transfers between devices with their start and end apart: 12, of which 8 were waited for; matrix products, arithmetic and copies ran while one was open for 4% of the time, Pallas kernels for 2%

profile of v10, /device:TPU:0, one launch (start us, length us, event | category | flops | bytes accessed | tf_op | source)
XLA Modules:
  0.0 146.1 jit_solution(11253747246923569610)
XLA Ops:
  0.6 0.0 copy-start
  0.6 4.2 %collective-permute-start = (bf16[1024,1024]{1,0:T(8,128)(2,1)}, bf16[1024,1024]{1,0:T(8,128)(2,1)}, u32[]{:S(2)}, u32[]{:S(2)}) collective-permute-start(bf16[1024,1024]{1,0:T(8,128)(2,1)} %bitcast.12), channel_id=1, source_target_pairs={{0,96},{1,97},{2,98},{3,99},{4,100},{5,101},{6,102},{7,103},{8,104... | collective-permute-start | bytes 6291464 | tf_op jit(solution)/shard_map/ppermute | solution.py:55
  4.8 1.9 %shard_map.59 = (bf16[528,8,128]{2,1,0:T(8,128)(2,1)S(1)}, s32[64]{0:T(128)S(1)}, f32[8,128]{1,0:T(8,128)S(1)}) custom-call(s32[2,32]{1,0:T(2,128)} %bitcast.25, s32[128]{0:T(128)} %table_hbm.1, bf16[32,8,1024]{2,1,0:T(8,128)(2,1)} %blocks_hbm.1), custom_call_target="tpu_custom_call" | custom-call | tf_op jit(solution)/shard_map/pallas_call | solution.py:150
  6.8 0.0 copy-start.1
  6.8 1.0 copy-done.1
  7.8 8.2 %all-to-all-start = ((bf16[528,8,128]{2,1,0:T(8,128)(2,1)}), bf16[528,8,128]{2,1,0:T(8,128)(2,1)S(1)}, u32[]{:S(2)}, u32[]{:S(2)}) async-start(bf16[528,8,128]{2,1,0:T(8,128)(2,1)} %copy-done.1), calls=%async_computation | async-start | bytes 2162688 | tf_op jit(solution)/shard_map/all_to_all | solution.py:41
  16.0 0.0 copy-done
  16.0 0.1 collective-permute-start.3
  16.1 12.0 %all-to-all-done.arrived_ref = bf16[528,8,128]{2,1,0:T(8,128)(2,1)S(1)} async-done(((bf16[528,8,128]{2,1,0:T(8,128)(2,1)}), bf16[528,8,128]{2,1,0:T(8,128)(2,1)S(1)}, u32[]{:S(2)}, u32[]{:S(2)}) %all-to-all-start) | async-done | bytes 1081376 | tf_op jit(solution)/shard_map/all_to_all | solution.py:41
  28.1 0.1 reshape.134
  28.2 0.2 convert_reduce_fusion
  28.4 0.1 select_reduce_fusion.origin_ref
  28.6 0.8 shard_map.60
  29.4 0.0 collective-permute-done.refs_6_
  29.4 0.1 collective-permute-start.4
  29.5 0.5 multiply_reduce_fusion.3
  30.0 1.7 %collective-permute-start.1 = (bf16[16,8,1024]{2,1,0:T(8,128)(2,1)S(1)}, bf16[16,8,1024]{2,1,0:T(8,128)(2,1)S(1)}, u32[]{:S(2)}, u32[]{:S(2)}) collective-permute-start(bf16[16,8,1024]{2,1,0:T(8,128)(2,1)S(1)} %get-tuple-element.34), channel_id=1, source_target_pairs={{0,32},{1,33},{2,34},{3,35},{4,36},{5,37},{6,38},{7,39},{8,40},{9,... | collective-permute-start | bytes 786440 | tf_op jit(solution)/shard_map/ppermute | solution.py:55
  31.7 1.6 %collective-permute-start.2 = (bf16[16,8,1024]{2,1,0:T(8,128)(2,1)S(1)}, bf16[16,8,1024]{2,1,0:T(8,128)(2,1)S(1)}, u32[]{:S(2)}, u32[]{:S(2)}) collective-permute-start(bf16[16,8,1024]{2,1,0:T(8,128)(2,1)S(1)} %get-tuple-element.35), channel_id=1, source_target_pairs={{0,96},{1,97},{2,98},{3,99},{4,100},{5,101},{6,102},{7,103},{8,104... | collective-permute-start | bytes 786440 | tf_op jit(solution)/shard_map/ppermute | solution.py:55
  33.3 0.0 collective-permute-done.3.refs_5_
  33.3 2.1 %multiply_reduce_fusion.2 = f32[1024]{0:T(1024)S(1)} fusion(bf16[1024,1024]{1,0:T(8,128)(2,1)} %collective-permute-done.3.refs_5_), kind=kLoop, calls=%fused_computation.2 | loop fusion | flops 3144704 | bytes 2101248 | tf_op jit(solution)/shard_map/reduce_sum | solution.py:445
  35.4 2.1 %multiply_reduce_fusion.1 = f32[1024]{0:T(1024)S(1)} fusion(bf16[1024,1024]{1,0:T(8,128)(2,1)} %collective-permute-done.refs_6_), kind=kLoop, calls=%fused_computation.1 | loop fusion | flops 3144704 | bytes 2101248 | tf_op jit(solution)/shard_map/reduce_sum | solution.py:445
  37.4 0.0 collective-permute-done.4.refs_7_
  37.5 0.5 multiply_reduce_fusion
  38.0 0.2 collective-permute-done.1.refs_2_
  38.2 1.0 collective-permute-done.2.refs_3_
  39.2 0.0 copy-done.2
  39.2 5.6 %shard_map.61 = (bf16[17,8,1024]{2,1,0:T(8,128)(2,1)S(1)}, bf16[17,8,1024]{2,1,0:T(8,128)(2,1)S(1)}, bf16[17,8,1024]{2,1,0:T(8,128)(2,1)S(1)}, bf16[17,8,1024]{2,1,0:T(8,128)(2,1)S(1)}) custom-call(bf16[16,8,1024]{2,1,0:T(8,128)(2,1)S(1)} %get-tuple-element.32.refs_0_, bf16[16,8,1024]{2,1,0:T(8,128)(2,1)S(1)} %get-tuple-element.33.refs_1_, ...), custom_call_target="tpu_custom_call" | custom-call | flops 2147483648 | bytes 10485760 | tf_op jit(solution)/shard_map/pallas_call | solution.py:336
  44.8 3.8 %collective-permute-start.5 = (bf16[17,8,1024]{2,1,0:T(8,128)(2,1)S(1)}, bf16[17,8,1024]{2,1,0:T(8,128)(2,1)S(1)}, u32[]{:S(2)}, u32[]{:S(2)}) collective-permute-start(bf16[17,8,1024]{2,1,0:T(8,128)(2,1)S(1)} %get-tuple-element.39), channel_id=1, source_target_pairs={{0,96},{1,97},{2,98},{3,99},{4,100},{5,101},{6,102},{7,103},{8,104... | collective-permute-start | bytes 835592 | tf_op jit(solution)/shard_map/ppermute | solution.py:55
  48.6 0.0 collective-permute-start.6
  48.6 6.4 %collective-permute-done.5.refs_2_ = bf16[17,8,1024]{2,1,0:T(8,128)(2,1)S(1)} collective-permute-done((bf16[17,8,1024]{2,1,0:T(8,128)(2,1)S(1)}, bf16[17,8,1024]{2,1,0:T(8,128)(2,1)S(1)}, u32[]{:S(2)}, u32[]{:S(2)}) %collective-permute-start.5) | collective-permute-done | bytes 278560 | tf_op jit(solution)/shard_map/ppermute | solution.py:55
  55.0 1.4 collective-permute-done.6.refs_3_
  56.3 0.8 shard_map.62
  57.2 21.0 %all_to_all.20.returned_ref = bf16[528,8,128]{2,1,0:T(8,128)(2,1)S(1)} all-to-all(bf16[528,8,128]{2,1,0:T(8,128)(2,1)S(1)} %shard_map.62), channel_id=1, replica_groups={{2,10,0,14,6,5,3,8,7,11,15,1,12,13,9,4},{18,19,27,26,24,17,21,20,23,31,..., dimensions={0} | all-to-all | bytes 2162688 | tf_op jit(solution)/shard_map/all_to_all | solution.py:41
  78.2 1.4 shard_map.63
  79.5 16.9 %all_to_all.21.arrived_ref = bf16[64,8,1024]{2,1,0:T(8,128)(2,1)S(1)} all-to-all(bf16[64,8,1024]{2,1,0:T(8,128)(2,1)S(1)} %get-tuple-element.42), channel_id=1, replica_groups={{2,10,0,14,6,5,3,8,7,11,15,1,12,13,9,4},{18,19,27,26,24,17,21,20,23,31,..., dimensions={0} | all-to-all | bytes 2097152 | tf_op jit(solution)/shard_map/all_to_all | solution.py:41
  96.4 0.6 shard_map.64
  97.1 2.3 %collective-permute-start.7 = (bf16[16,8,1024]{2,1,0:T(8,128)(2,1)S(1)}, bf16[16,8,1024]{2,1,0:T(8,128)(2,1)S(1)}, u32[]{:S(2)}, u32[]{:S(2)}) collective-permute-start(bf16[16,8,1024]{2,1,0:T(8,128)(2,1)S(1)} %get-tuple-element.45), channel_id=1, source_target_pairs={{0,32},{1,33},{2,34},{3,35},{4,36},{5,37},{6,38},{7,39},{8,40},{9,... | collective-permute-start | bytes 786440 | tf_op jit(solution)/shard_map/ppermute | solution.py:55
  99.4 2.8 %collective-permute-start.8 = (bf16[16,8,1024]{2,1,0:T(8,128)(2,1)S(1)}, bf16[16,8,1024]{2,1,0:T(8,128)(2,1)S(1)}, u32[]{:S(2)}, u32[]{:S(2)}) collective-permute-start(bf16[16,8,1024]{2,1,0:T(8,128)(2,1)S(1)} %get-tuple-element.46), channel_id=1, source_target_pairs={{0,96},{1,97},{2,98},{3,99},{4,100},{5,101},{6,102},{7,103},{8,104... | collective-permute-start | bytes 786440 | tf_op jit(solution)/shard_map/ppermute | solution.py:55
  102.2 5.5 %collective-permute-done.7.refs_2_ = bf16[16,8,1024]{2,1,0:T(8,128)(2,1)S(1)} collective-permute-done((bf16[16,8,1024]{2,1,0:T(8,128)(2,1)S(1)}, bf16[16,8,1024]{2,1,0:T(8,128)(2,1)S(1)}, u32[]{:S(2)}, u32[]{:S(2)}) %collective-permute-start.7) | collective-permute-done | bytes 262176 | tf_op jit(solution)/shard_map/ppermute | solution.py:55
  107.7 0.0 collective-permute-done.8.refs_3_
  107.7 5.6 %shard_map.65 = (bf16[17,8,1024]{2,1,0:T(8,128)(2,1)S(1)}, bf16[17,8,1024]{2,1,0:T(8,128)(2,1)S(1)}, bf16[17,8,1024]{2,1,0:T(8,128)(2,1)S(1)}, bf16[17,8,1024]{2,1,0:T(8,128)(2,1)S(1)}) custom-call(bf16[16,8,1024]{2,1,0:T(8,128)(2,1)S(1)} %get-tuple-element.43.refs_0_, bf16[16,8,1024]{2,1,0:T(8,128)(2,1)S(1)} %get-tuple-element.44.refs_1_, ...), custom_call_target="tpu_custom_call" | custom-call | flops 2147483648 | bytes 10485760 | tf_op jit(solution)/shard_map/pallas_call | solution.py:336
  113.3 2.1 %collective-permute-start.9 = (bf16[17,8,1024]{2,1,0:T(8,128)(2,1)S(1)}, bf16[17,8,1024]{2,1,0:T(8,128)(2,1)S(1)}, u32[]{:S(2)}, u32[]{:S(2)}) collective-permute-start(bf16[17,8,1024]{2,1,0:T(8,128)(2,1)S(1)} %get-tuple-element.49), channel_id=1, source_target_pairs={{0,96},{1,97},{2,98},{3,99},{4,100},{5,101},{6,102},{7,103},{8,104... | collective-permute-start | bytes 835592 | tf_op jit(solution)/shard_map/ppermute | solution.py:55
  115.5 0.0 collective-permute-start.10
  115.5 5.6 %collective-permute-done.9.refs_2_ = bf16[17,8,1024]{2,1,0:T(8,128)(2,1)S(1)} collective-permute-done((bf16[17,8,1024]{2,1,0:T(8,128)(2,1)S(1)}, bf16[17,8,1024]{2,1,0:T(8,128)(2,1)S(1)}, u32[]{:S(2)}, u32[]{:S(2)}) %collective-permute-start.9) | collective-permute-done | bytes 278560 | tf_op jit(solution)/shard_map/ppermute | solution.py:55
  121.1 2.1 %collective-permute-done.10.refs_3_ = bf16[17,8,1024]{2,1,0:T(8,128)(2,1)S(1)} collective-permute-done((bf16[17,8,1024]{2,1,0:T(8,128)(2,1)S(1)}, bf16[17,8,1024]{2,1,0:T(8,128)(2,1)S(1)}, u32[]{:S(2)}, u32[]{:S(2)}) %collective-permute-start.10) | collective-permute-done | bytes 278560 | tf_op jit(solution)/shard_map/ppermute | solution.py:55
  123.2 0.8 shard_map.66
  124.1 20.2 %all_to_all.22.returned_ref = bf16[528,8,128]{2,1,0:T(8,128)(2,1)S(1)} all-to-all(bf16[528,8,128]{2,1,0:T(8,128)(2,1)S(1)} %shard_map.66), channel_id=1, replica_groups={{2,10,0,14,6,5,3,8,7,11,15,1,12,13,9,4},{18,19,27,26,24,17,21,20,23,31,..., dimensions={0} | all-to-all | bytes 2162688 | tf_op jit(solution)/shard_map/all_to_all | solution.py:41
  144.3 1.9 %shard_map.67 = (f32[2,256]{1,0:T(2,128)}, bf16[32,8,1024]{2,1,0:T(8,128)(2,1)}) custom-call(s32[64]{0:T(128)S(1)} %get-tuple-element.28.slots_ref, f32[8,128]{1,0:T(8,128)S(1)} %get-tuple-element.41.squares_ref, bf16[528,8,128]{2,1,0:T(8,128)(2,1)S(1)} %all_to_all.22.returned_ref, f32[2,256]{1,0:T(2,128)S(1)} %get-tuple-element.51.earlier_ref), custom_call_target="tpu_custom_call" | custom-call | tf_op jit(solution)/shard_map/pallas_call | solution.py:435
  (9 shorter events, 0.1 us)
Async XLA Ops:
  0.6 15.4 %copy-start = (bf16[1,1024,1024]{2,1,0:T(8,128)(2,1)S(1)}, bf16[1,1024,1024]{2,1,0:T(8,128)(2,1)}, u32[]{:S(2)}) copy-start(bf16[1,1024,1024]{2,1,0:T(8,128)(2,1)} %param.5) | copy-start | bytes 6291460
  0.6 28.7 %collective-permute-start = (bf16[1024,1024]{1,0:T(8,128)(2,1)}, bf16[1024,1024]{1,0:T(8,128)(2,1)}, u32[]{:S(2)}, u32[]{:S(2)}) collective-permute-start(bf16[1024,1024]{1,0:T(8,128)(2,1)} %bitcast.12), channel_id=1, source_target_pairs={{0,96},{1,97},{2,98},{3,99},{4,100},{5,101},{6,102},{7,103},{8,104... | collective-permute-start | bytes 6291464 | tf_op jit(solution)/shard_map/ppermute | solution.py:55
  6.8 1.0 copy-start.1
  7.8 20.3 %all-to-all-start = ((bf16[528,8,128]{2,1,0:T(8,128)(2,1)}), bf16[528,8,128]{2,1,0:T(8,128)(2,1)S(1)}, u32[]{:S(2)}, u32[]{:S(2)}) async-start(bf16[528,8,128]{2,1,0:T(8,128)(2,1)} %copy-done.1), calls=%async_computation | async-start | bytes 2162688 | tf_op jit(solution)/shard_map/all_to_all | solution.py:41
  16.0 17.3 %collective-permute-start.3 = (bf16[1024,1024]{1,0:T(8,128)(2,1)S(1)}, bf16[1024,1024]{1,0:T(8,128)(2,1)}, u32[]{:S(2)}, u32[]{:S(2)}) collective-permute-start(bf16[1024,1024]{1,0:T(8,128)(2,1)S(1)} %bitcast.13), channel_id=1, source_target_pairs={{0,16},{1,17},{2,18},{3,19},{4,20},{5,21},{6,22},{7,23},{8,24},{9,... | collective-permute-start | bytes 6291464 | tf_op jit(solution)/shard_map/ppermute | solution.py:63
  29.4 8.1 %collective-permute-start.4 = (bf16[1024,1024]{1,0:T(8,128)(2,1)}, bf16[1024,1024]{1,0:T(8,128)(2,1)S(1)}, u32[]{:S(2)}, u32[]{:S(2)}) collective-permute-start(bf16[1024,1024]{1,0:T(8,128)(2,1)} %collective-permute-done.refs_6_), channel_id=1, source_target_pairs={{0,16},{1,17},{2,18},{3,19},{4,20},{5,21},{6,22},{7,23},{8,24},{9,... | collective-permute-start | bytes 6291464 | tf_op jit(solution)/shard_map/ppermute | solution.py:63
  30.0 8.2 %collective-permute-start.1 = (bf16[16,8,1024]{2,1,0:T(8,128)(2,1)S(1)}, bf16[16,8,1024]{2,1,0:T(8,128)(2,1)S(1)}, u32[]{:S(2)}, u32[]{:S(2)}) collective-permute-start(bf16[16,8,1024]{2,1,0:T(8,128)(2,1)S(1)} %get-tuple-element.34), channel_id=1, source_target_pairs={{0,32},{1,33},{2,34},{3,35},{4,36},{5,37},{6,38},{7,39},{8,40},{9,... | collective-permute-start | bytes 786440 | tf_op jit(solution)/shard_map/ppermute | solution.py:55
  31.7 7.5 %collective-permute-start.2 = (bf16[16,8,1024]{2,1,0:T(8,128)(2,1)S(1)}, bf16[16,8,1024]{2,1,0:T(8,128)(2,1)S(1)}, u32[]{:S(2)}, u32[]{:S(2)}) collective-permute-start(bf16[16,8,1024]{2,1,0:T(8,128)(2,1)S(1)} %get-tuple-element.35), channel_id=1, source_target_pairs={{0,96},{1,97},{2,98},{3,99},{4,100},{5,101},{6,102},{7,103},{8,104... | collective-permute-start | bytes 786440 | tf_op jit(solution)/shard_map/ppermute | solution.py:55
  37.4 1.7 %copy-start.2 = (bf16[1024,1024]{1,0:T(8,128)(2,1)}, bf16[1024,1024]{1,0:T(8,128)(2,1)S(1)}, u32[]{:S(2)}) copy-start(bf16[1024,1024]{1,0:T(8,128)(2,1)S(1)} %collective-permute-done.4.refs_7_) | copy-start | bytes 6291460
  44.8 10.2 %collective-permute-start.5 = (bf16[17,8,1024]{2,1,0:T(8,128)(2,1)S(1)}, bf16[17,8,1024]{2,1,0:T(8,128)(2,1)S(1)}, u32[]{:S(2)}, u32[]{:S(2)}) collective-permute-start(bf16[17,8,1024]{2,1,0:T(8,128)(2,1)S(1)} %get-tuple-element.39), channel_id=1, source_target_pairs={{0,96},{1,97},{2,98},{3,99},{4,100},{5,101},{6,102},{7,103},{8,104... | collective-permute-start | bytes 835592 | tf_op jit(solution)/shard_map/ppermute | solution.py:55
  48.6 7.8 %collective-permute-start.6 = (bf16[17,8,1024]{2,1,0:T(8,128)(2,1)S(1)}, bf16[17,8,1024]{2,1,0:T(8,128)(2,1)S(1)}, u32[]{:S(2)}, u32[]{:S(2)}) collective-permute-start(bf16[17,8,1024]{2,1,0:T(8,128)(2,1)S(1)} %get-tuple-element.40), channel_id=1, source_target_pairs={{0,32},{1,33},{2,34},{3,35},{4,36},{5,37},{6,38},{7,39},{8,40},{9,... | collective-permute-start | bytes 835592 | tf_op jit(solution)/shard_map/ppermute | solution.py:55
  97.1 10.7 %collective-permute-start.7 = (bf16[16,8,1024]{2,1,0:T(8,128)(2,1)S(1)}, bf16[16,8,1024]{2,1,0:T(8,128)(2,1)S(1)}, u32[]{:S(2)}, u32[]{:S(2)}) collective-permute-start(bf16[16,8,1024]{2,1,0:T(8,128)(2,1)S(1)} %get-tuple-element.45), channel_id=1, source_target_pairs={{0,32},{1,33},{2,34},{3,35},{4,36},{5,37},{6,38},{7,39},{8,40},{9,... | collective-permute-start | bytes 786440 | tf_op jit(solution)/shard_map/ppermute | solution.py:55
  99.4 8.3 %collective-permute-start.8 = (bf16[16,8,1024]{2,1,0:T(8,128)(2,1)S(1)}, bf16[16,8,1024]{2,1,0:T(8,128)(2,1)S(1)}, u32[]{:S(2)}, u32[]{:S(2)}) collective-permute-start(bf16[16,8,1024]{2,1,0:T(8,128)(2,1)S(1)} %get-tuple-element.46), channel_id=1, source_target_pairs={{0,96},{1,97},{2,98},{3,99},{4,100},{5,101},{6,102},{7,103},{8,104... | collective-permute-start | bytes 786440 | tf_op jit(solution)/shard_map/ppermute | solution.py:55
  113.3 7.8 %collective-permute-start.9 = (bf16[17,8,1024]{2,1,0:T(8,128)(2,1)S(1)}, bf16[17,8,1024]{2,1,0:T(8,128)(2,1)S(1)}, u32[]{:S(2)}, u32[]{:S(2)}) collective-permute-start(bf16[17,8,1024]{2,1,0:T(8,128)(2,1)S(1)} %get-tuple-element.49), channel_id=1, source_target_pairs={{0,96},{1,97},{2,98},{3,99},{4,100},{5,101},{6,102},{7,103},{8,104... | collective-permute-start | bytes 835592 | tf_op jit(solution)/shard_map/ppermute | solution.py:55
  115.5 7.8 %collective-permute-start.10 = (bf16[17,8,1024]{2,1,0:T(8,128)(2,1)S(1)}, bf16[17,8,1024]{2,1,0:T(8,128)(2,1)S(1)}, u32[]{:S(2)}, u32[]{:S(2)}) collective-permute-start(bf16[17,8,1024]{2,1,0:T(8,128)(2,1)S(1)} %get-tuple-element.50), channel_id=1, source_target_pairs={{0,32},{1,33},{2,34},{3,35},{4,36},{5,37},{6,38},{7,39},{8,40},{9,... | collective-permute-start | bytes 835592 | tf_op jit(solution)/shard_map/ppermute | solution.py:55
